TPU v7x, 512 devices: a whole 4x4x16 slice. The times are simulated.
512 devices in a mesh: var: 64 (over z, x_hi, core), samp: 8 (over y, x_lo).
Axes of the slice: x: 4 (x_hi: 2, x_lo: 2; x = x_hi * 2 + x_lo), y: 4, z: 16, core: 2. Of those that a mesh axis runs over, the one named last changes fastest.
Arguments:
- observed: bfloat16 [4096, 65536], P('samp', 'var'), may hold values from -40 to 40
- pattern: int32 [512, 3], P('var'), may hold values from 0 to 511, as said below
- omega_init: bfloat16 [512, 3, 128, 128], P('var'), may hold values from -4 to 4
Outputs:
- precision: float32 [512, 3, 128, 128], P(('var', 'samp'))
Inputs may be any that keep to these rules, and one draw needn't show every extreme that they name: pattern[R, 0] = R. The other two blocks of row block R belong to two different var devices among the four whose index differs from the owner of R by 1 or 2 (counted modulo the number of var devices). On every var device each of those four devices supplies the second block of exactly two of its row blocks.
All inputs are finite; a program needn't handle non-finite values.
Results may differ from a plain program's by a relative error of at most 0.0044.
Values may be sent and summed in bfloat16 or wider, within the bound.
No kernel may reach another device: no remote copies, remote signals or barrier semaphores. Data moves between devices by JAX's collectives and lax.ppermute only.
A program may use at most 64 MiB of HBM per device.

v0:
```python
import jax
import jax.numpy as jnp
from jax import lax
from jax.sharding import PartitionSpec as P

ITERS = 2


STEP_SCALE = 0.5
THRESHOLD = 0.25
EPSILON = 1e-06


def from_behind(block, axis, distance):
    devices = range(lax.axis_size(axis))
    route = [((i - distance) % len(devices), i) for i in devices]
    return lax.ppermute(block, axis, route)


def proximal(iterate, grad, mean_sq, diag_mask):
    step_size = STEP_SCALE / jnp.sqrt(mean_sq + EPSILON)
    stepped = iterate - step_size * grad
    shrunk = stepped - jnp.clip(stepped, -THRESHOLD, THRESHOLD)
    barrier = 0.5 * (stepped + jnp.sqrt(stepped * stepped + 4.0 * step_size))
    return jnp.where(diag_mask, barrier, shrunk)


def block_terms(packed, selected, inverse):
    weighted = jnp.einsum("rkab,nrkb->rna", packed, selected, preferred_element_type=jnp.float32)
    weighted = weighted.astype(jnp.bfloat16)
    return (
        jnp.einsum("rna,nrkb->rkab", weighted, selected, preferred_element_type=jnp.float32)
        * inverse
    )


def body(observed, pattern, omega_init):
    var_count = lax.axis_size("var")
    samp_count = lax.axis_size("samp")
    var_index = lax.axis_index("var")
    samp_index = lax.axis_index("samp")
    row_blocks = omega_init.shape[0]
    slot_count = omega_init.shape[1]
    block_size = omega_init.shape[2]
    sample_rows = observed.shape[0]
    inverse = 1.0 / (sample_rows * samp_count)
    below_one = from_behind(observed, "var", 1)
    above_one = from_behind(observed, "var", -1)
    below_two = from_behind(observed, "var", 2)
    above_two = from_behind(observed, "var", -2)
    strips = jnp.concatenate((below_two, below_one, observed, above_one, above_two), axis=1)
    blocks = strips.reshape(sample_rows, 5 * row_blocks, block_size)
    owners = pattern // row_blocks
    within = pattern % row_blocks
    offsets = (owners - var_index + var_count + 2) % var_count
    slot_index = (offsets * row_blocks + within).reshape(-1)
    selected = jnp.take(blocks, slot_index, axis=1).reshape(
        sample_rows, row_blocks, slot_count, block_size
    )
    slot_ids = lax.broadcasted_iota(jnp.int32, (slot_count, block_size, block_size), 0)
    row_ids = lax.broadcasted_iota(jnp.int32, (slot_count, block_size, block_size), 1)
    col_ids = lax.broadcasted_iota(jnp.int32, (slot_count, block_size, block_size), 2)
    diag_mask = (slot_ids == 0) & (row_ids == col_ids)
    entries = row_blocks * slot_count * block_size * block_size * var_count
    share_rows = row_blocks // samp_count
    iterate = omega_init.astype(jnp.float32)
    for iteration in range(ITERS):
        packed = iterate.astype(jnp.bfloat16)
        partial_grad = block_terms(packed, selected, inverse)
        grad = lax.psum(partial_grad, "samp")
        squares = lax.psum(jnp.sum(grad * grad), "var")
        iterate = proximal(iterate, grad, squares / entries, diag_mask)
    return lax.dynamic_slice_in_dim(iterate, samp_index * share_rows, share_rows, 0)


def solution(mesh):
    return jax.shard_map(
        body,
        mesh=mesh,
        in_specs=(P("samp", "var"), P("var", None), P("var", None, None, None)),
        out_specs=P(("var", "samp"), None, None, None),
        check_vma=False,
    )
```

profile of v0, /device:TPU:1, one launch (start us, length us, event | category | flops | bytes accessed | tf_op | source)
XLA Modules:
  0.0 600.7 jit_solution(1851241672571276455)
XLA Ops:
  6.5 0.0 copy-start.4
  6.5 0.0 all-reduce.3.cloned.1.call-start
  6.5 1.5 copy.16
  8.1 5.5 collective-permute-start
  13.5 4.3 collective-permute-start.1
  17.9 2.8 collective-permute-start.2
  20.7 8.2 %collective-permute-start.3 = (bf16[512,1024]{0,1:T(8,128)(2,1)S(1)}, bf16[512,1024]{0,1:T(8,128)(2,1)S(1)}, u32[]{:S(2)}, u32[]{:S(2)}) collective-permute-start(bf16[512,1024]{0,1:T(8,128)(2,1)S(1)} %copy.16), channel_id=1, source_target_pairs={{16,0},{24,8},{32,16},{40,24},{48,32},{56,40},{64,48},{72,56},{80,... | collective-permute-start | bytes 3145736 | tf_op jit(solution)/shard_map/ppermute | solution.py:17
  28.9 0.0 copy-done.4
  29.0 0.1 copy.21
  29.0 0.1 reshape.44
  29.1 0.1 copy.15
  29.2 37.4 %collective-permute-done = bf16[512,1024]{0,1:T(8,128)(2,1)} collective-permute-done((bf16[512,1024]{0,1:T(8,128)(2,1)S(1)}, bf16[512,1024]{0,1:T(8,128)(2,1)}, u32[]{:S(2)}, u32[]{:S(2)}) %collective-permute-start) | collective-permute-done | bytes 1048608 | tf_op jit(solution)/shard_map/ppermute | solution.py:17
  66.6 2.3 constant_dynamic-update-slice_fusion.4
  68.9 12.5 %collective-permute-done.1 = bf16[512,1024]{0,1:T(8,128)(2,1)} collective-permute-done((bf16[512,1024]{0,1:T(8,128)(2,1)S(1)}, bf16[512,1024]{0,1:T(8,128)(2,1)}, u32[]{:S(2)}, u32[]{:S(2)}) %collective-permute-start.1) | collective-permute-done | bytes 1048608 | tf_op jit(solution)/shard_map/ppermute | solution.py:17
  81.4 2.3 constant_dynamic-update-slice_fusion.3
  83.8 1.1 constant_dynamic-update-slice_fusion.2
  84.8 0.0 collective-permute-done.2
  84.8 1.1 constant_dynamic-update-slice_fusion.1
  85.9 0.0 collective-permute-done.3
  85.9 1.0 constant_dynamic-update-slice_fusion
  86.9 7.9 %copy.22 = bf16[512,40,128]{2,0,1:T(8,128)(2,1)} copy(bf16[512,40,128]{0,2,1:T(8,128)(2,1)} %bitcast) | data formatting | bytes 10485760 | tf_op jit(solution)/shard_map/reshape | solution.py:52
  94.8 3.6 gather_fusion
  98.5 2.8 copy.23
  101.3 6.2 %multiply_bitcast_fusion.1 = f32[8,3,128,128]{2,3,1,0:T(8,128)} fusion(bf16[512,8,3,128]{0,3,2,1:T(8,128)(2,1)} %copy.23, pred[8,3]{1,0:T(8,128)(4,1)S(1)} %copy.15, bf16[8,3,128,128]{3,2,1,0:T(8,128)(2,1)} %param.5), kind=kOutput, calls=%fused_computation.14 | convolution fusion | flops 809369600 | bytes 5505048 | tf_op jit(solution)/shard_map/rna,nrkb->rkab/dot_general | solution.py:32
  107.5 0.0 copy-start.3
  107.5 0.0 all-reduce.3.cloned.1.call-update
  107.5 0.0 all-reduce.5.cloned.1.call-start
  107.6 0.1 fusion.16
  107.7 106.0 %all-reduce.3.cloned.1.call-done = f32[8,3,128,128]{2,3,1,0:T(8,128)} async-done(((f32[8,3,128,128]{2,3,1,0:T(8,128)}), f32[8,3,128,128]{2,3,1,0:T(8,128)}) %all-reduce.3.cloned.1.call-update) | async-done | bytes 1572880 | tf_op jit(solution)/shard_map/psum | solution.py:70
  213.7 0.0 copy-start
  213.7 2.5 multiply_reduce_fusion.1
  216.3 0.0 copy-done.3
  216.3 0.4 copy.14
  216.6 0.0 copy-start.2
  216.7 132.6 %psum.29 = f32[]{:T(128)} all-reduce(f32[]{:T(128)} %multiply_reduce_fusion.1), channel_id=1, replica_groups=mesh['var'=64,'samp'=8] {'var'}, use_global_device_ids=true, to_apply=%region_2.3 | all-reduce | flops 1 | bytes 8 | tf_op jit(solution)/shard_map/psum | solution.py:71
  350.0 0.0 copy-done
  350.0 6.9 %multiply_bitcast_fusion = f32[8,3,128,128]{2,3,1,0:T(8,128)} fusion(bf16[512,8,3,128]{0,3,2,1:T(8,128)(2,1)} %copy.23, pred[8,3]{1,0:T(8,128)(4,1)S(1)} %copy.15, f32[8,3,128,128]{2,3,1,0:T(8,128)S(1)} %copy-done, bf16[8,3,128,128]{2,3,1,0:T(8,128)(2,1)S(1)} %copy.14, f32[]{:T(128)S(6)} %mul.58, f32[]{:T(128)S(6)} %div.29, pred[3,128,128]{1,2,0:T(8,128)(4,1)S(1)} %fusion.16), kind=kOutput, calls=%fused_computation.12 | convolution fusion | flops 813694976 | bytes 7127072 | tf_op jit(solution)/shard_map/rna,nrkb->rkab/dot_general | solution.py:32
  356.8 0.0 copy-done.2
  356.8 0.0 all-reduce.5.cloned.1.call-update
  356.9 98.1 %all-reduce.5.cloned.1.call-done = f32[8,3,128,128]{2,3,1,0:T(8,128)} async-done(((f32[8,3,128,128]{2,3,1,0:T(8,128)}), f32[8,3,128,128]{2,3,1,0:T(8,128)}) %all-reduce.5.cloned.1.call-update) | async-done | bytes 1572880 | tf_op jit(solution)/shard_map/psum | solution.py:70
  455.0 0.0 copy-start.1
  455.0 2.5 multiply_reduce_fusion
  457.5 132.6 %psum.31 = f32[]{:T(128)} all-reduce(f32[]{:T(128)} %multiply_reduce_fusion), channel_id=1, replica_groups=mesh['var'=64,'samp'=8] {'var'}, use_global_device_ids=true, to_apply=%region_5.6 | all-reduce | flops 1 | bytes 8 | tf_op jit(solution)/shard_map/psum | solution.py:71
  590.8 0.0 copy-done.1
  590.8 2.1 multiply_subtract_fusion
  593.0 0.1 fusion.15
  593.1 0.8 copy.27
  (4 shorter events, 0.0 us)
Async XLA Ops:
  6.5 22.4 %copy-start.4 = (s32[8,3]{0,1:T(4,128)S(1)}, s32[8,3]{0,1:T(4,128)}, u32[]{:S(2)}) copy-start(s32[8,3]{0,1:T(4,128)} %param.4) | copy-start | bytes 292
  6.5 207.2 %all-reduce.3.cloned.1.call-start = ((), (), s32[]{:S(2)}) async-start(), calls=%async_computation | async-start | bytes 3145728 | tf_op jit(solution)/shard_map/psum | solution.py:70
  8.1 58.6 %collective-permute-start = (bf16[512,1024]{0,1:T(8,128)(2,1)S(1)}, bf16[512,1024]{0,1:T(8,128)(2,1)}, u32[]{:S(2)}, u32[]{:S(2)}) collective-permute-start(bf16[512,1024]{0,1:T(8,128)(2,1)S(1)} %copy.16), channel_id=1, source_target_pairs={{496,0},{504,8},{0,16},{8,24},{16,32},{24,40},{32,48},{40,56},{48,... | collective-permute-start | bytes 3145736 | tf_op jit(solution)/shard_map/ppermute | solution.py:17
  13.5 67.9 %collective-permute-start.1 = (bf16[512,1024]{0,1:T(8,128)(2,1)S(1)}, bf16[512,1024]{0,1:T(8,128)(2,1)}, u32[]{:S(2)}, u32[]{:S(2)}) collective-permute-start(bf16[512,1024]{0,1:T(8,128)(2,1)S(1)} %copy.16), channel_id=1, source_target_pairs={{504,0},{0,8},{8,16},{16,24},{24,32},{32,40},{40,48},{48,56},{56,6... | collective-permute-start | bytes 3145736 | tf_op jit(solution)/shard_map/ppermute | solution.py:17
  17.9 66.9 %collective-permute-start.2 = (bf16[512,1024]{0,1:T(8,128)(2,1)S(1)}, bf16[512,1024]{0,1:T(8,128)(2,1)S(1)}, u32[]{:S(2)}, u32[]{:S(2)}) collective-permute-start(bf16[512,1024]{0,1:T(8,128)(2,1)S(1)} %copy.16), channel_id=1, source_target_pairs={{8,0},{16,8},{24,16},{32,24},{40,32},{48,40},{56,48},{64,56},{72,6... | collective-permute-start | bytes 3145736 | tf_op jit(solution)/shard_map/ppermute | solution.py:17
  20.7 65.2 %collective-permute-start.3 = (bf16[512,1024]{0,1:T(8,128)(2,1)S(1)}, bf16[512,1024]{0,1:T(8,128)(2,1)S(1)}, u32[]{:S(2)}, u32[]{:S(2)}) collective-permute-start(bf16[512,1024]{0,1:T(8,128)(2,1)S(1)} %copy.16), channel_id=1, source_target_pairs={{16,0},{24,8},{32,16},{40,24},{48,32},{56,40},{64,48},{72,56},{80,... | collective-permute-start | bytes 3145736 | tf_op jit(solution)/shard_map/ppermute | solution.py:17
  107.5 108.8 %copy-start.3 = (bf16[8,3,128,128]{3,2,1,0:T(8,128)(2,1)S(1)}, bf16[8,3,128,128]{3,2,1,0:T(8,128)(2,1)}, u32[]{:S(2)}) copy-start(bf16[8,3,128,128]{3,2,1,0:T(8,128)(2,1)} %param.5) | copy-start | bytes 2359300
  107.5 347.5 %all-reduce.5.cloned.1.call-start = ((), (), s32[]{:S(2)}) async-start(), calls=%async_computation.1 | async-start | bytes 3145728 | tf_op jit(solution)/shard_map/psum | solution.py:70
  213.7 136.2 %copy-start = (f32[8,3,128,128]{2,3,1,0:T(8,128)S(1)}, f32[8,3,128,128]{2,3,1,0:T(8,128)}, u32[]{:S(2)}) copy-start(f32[8,3,128,128]{2,3,1,0:T(8,128)} %all-reduce.3.cloned.1.call-done) | copy-start | bytes 4718596
  216.6 140.2 %copy-start.2 = (bf16[8,3,128,128]{2,3,1,0:T(8,128)(2,1)}, bf16[8,3,128,128]{2,3,1,0:T(8,128)(2,1)S(1)}, u32[]{:S(2)}) copy-start(bf16[8,3,128,128]{2,3,1,0:T(8,128)(2,1)S(1)} %copy.14) | copy-start | bytes 2359300
  455.0 135.8 %copy-start.1 = (f32[8,3,128,128]{2,3,1,0:T(8,128)S(1)}, f32[8,3,128,128]{2,3,1,0:T(8,128)}, u32[]{:S(2)}) copy-start(f32[8,3,128,128]{2,3,1,0:T(8,128)} %all-reduce.5.cloned.1.call-done) | copy-start | bytes 4718596
Sparse Core Ops, SparseCore 0:
  107.6 106.0 all-reduce.2
  357.0 97.9 all-reduce.4
where the time goes:
time: 602 us; the launch traced here: 601 us
  blocking collectives  265 us (44%)
  waiting for transfers between devices  254 us (42%)
  local copies, waits for them, and re-layouts  25.1 us (4%)
  starting transfers between devices  20.9 us (3%)
  between operations  14.9 us (2%)
  matrix products  13.1 us (2%)
  other arithmetic  7.45 us (1%)
    psum x2, blocking collectives, body(): squares = lax.psum(jnp.sum(grad * grad), 'var')  265 us
    psum x2, waiting for transfers between devices, body(): grad = lax.psum(partial_grad, 'samp')  204 us
    ppermute x4, waiting for transfers between devices, from_behind(): return lax.ppermute(block, axis, route)  49.9 us
    ppermute x4, starting transfers between devices, from_behind(): return lax.ppermute(block, axis, route)  20.8 us
    dot_general x2, matrix products, block_terms(): jnp.einsum('rna,nrkb->rkab', weighted, selected, preferred_element_type=j...  13.1 us
  transfers between devices with their start and end apart: 6, of which 4 were waited for; matrix products, arithmetic and copies ran while one was open for 1% of the time, Pallas kernels for 0%

commit v1 on v0

v1 whole, which is shorter than its diff:
```python
import jax
import jax.numpy as jnp
from jax import lax
from jax.experimental import pallas as pl
from jax.experimental.pallas import tpu as pltpu
from jax.sharding import Mesh, PartitionSpec as P

STEP_SCALE = 0.5
THRESHOLD = 0.25
EPSILON = 1e-06

AXES = ("z", "xh", "core", "y", "xl")
SIZES = (16, 2, 2, 4, 2)
VAR_AXES = ("z", "xh", "core")
SAMP_AXES = ("y", "xl")
CHUNKS = 2
ROWB = 8
K = 3
BLK = 128
SAMPLES = 4096
ENTRIES = 25165824
SAMP = 8
PAIRS = ((0, 0), (0, 1), (0, 2), (1, 1), (1, 2), (2, 2))
NPAIR = len(PAIRS)

VMEM = pl.BlockSpec(memory_space=pltpu.VMEM)
SMEM = pl.BlockSpec(memory_space=pltpu.SMEM)
ANY = pl.BlockSpec(memory_space=pl.ANY)
F32 = jnp.float32
BF16 = jnp.bfloat16


def params():
    return pltpu.CompilerParams(vmem_limit_bytes=48 * 1024 * 1024)


def gram_kernel(source, column, *refs):
    inputs = refs[: 2 + 3 * CHUNKS]
    out, held, sems = refs[2 + 3 * CHUNKS :]
    samples = held.shape[1]
    part = samples // CHUNKS
    copies = [
        pltpu.make_async_copy(inputs[0], held.at[0], sems.at[0]),
        pltpu.make_async_copy(inputs[1], held.at[1], sems.at[1]),
    ]
    for i in range(3 * CHUNKS):
        slot, chunk = 2 + i // CHUNKS, i % CHUNKS
        rows = pl.ds(chunk * part, part)
        copies.append(pltpu.make_async_copy(inputs[2 + i], held.at[slot, rows], sems.at[2 + i]))
    for copy in copies:
        copy.start()
    for copy in copies:
        copy.wait()

    def one(r, carry):
        cols = [
            held[source[r, k], :, pl.ds(pl.multiple_of(column[r, k] * BLK, BLK), BLK)]
            for k in range(K)
        ]
        for p, (i, j) in enumerate(PAIRS):
            gram = lax.dot_general(
                cols[i], cols[j], (((0,), (0,)), ((), ())), preferred_element_type=F32
            )
            out[r, p] = (gram * (1.0 / SAMPLES)).astype(BF16)
        return carry

    lax.fori_loop(0, ROWB, one, 0)


def gram(source, column, arrays):
    samples, columns = arrays[0].shape
    return pl.pallas_call(
        gram_kernel,
        out_shape=jax.ShapeDtypeStruct((ROWB, NPAIR, BLK, BLK), BF16),
        in_specs=[SMEM, SMEM] + [ANY] * len(arrays),
        out_specs=VMEM,
        scratch_shapes=[
            pltpu.VMEM((5, samples, columns), BF16),
            pltpu.SemaphoreType.DMA((len(arrays),)),
        ],
        compiler_params=params(),
        name="gram",
    )(source, column, *arrays)


def times_gram(packed, high, low):
    total = jnp.zeros((BLK, K * BLK), F32)
    for j in range(K):
        rows = slice(j * BLK, (j + 1) * BLK)
        total += jnp.dot(packed[j], high[rows, :], preferred_element_type=F32)
        total += jnp.dot(packed[j], low[rows, :], preferred_element_type=F32)
    return [total[:, k * BLK : (k + 1) * BLK] for k in range(K)]


def put_squares(grads, out):
    squares = sum(jnp.sum(g * g, axis=0, keepdims=True) for g in grads)
    out[...] = jnp.broadcast_to(squares, out.shape)


def first_kernel(parts, omega, high, low, grad, squares):
    for p, (i, j) in enumerate(PAIRS):
        block = sum(parts[s, p].astype(F32) for s in range(SAMP))
        hi = block.astype(BF16)
        lo = (block - hi.astype(F32)).astype(BF16)
        at = (pl.ds(i * BLK, BLK), pl.ds(j * BLK, BLK))
        high[at] = hi
        low[at] = lo
        if i != j:
            flipped = block.T
            hi = flipped.astype(BF16)
            lo = (flipped - hi.astype(F32)).astype(BF16)
            at = (pl.ds(j * BLK, BLK), pl.ds(i * BLK, BLK))
            high[at] = hi
            low[at] = lo
    grads = times_gram(omega, high, low)
    for k in range(K):
        grad[k] = grads[k]
    put_squares(grads, squares)


def step_of(squares):
    mean_sq = jnp.sum(squares[...]) * (1.0 / ENTRIES)
    mean_sq = jnp.full((8, BLK), mean_sq, F32)
    return (STEP_SCALE / jnp.sqrt(mean_sq + EPSILON))[0:1, :]


def proximal(iterate, grad, step, k):
    stepped = iterate - step * grad
    shrunk = stepped - jnp.clip(stepped, -THRESHOLD, THRESHOLD)
    if k:
        return shrunk
    row = lax.broadcasted_iota(jnp.int32, (BLK, BLK), 0)
    col = lax.broadcasted_iota(jnp.int32, (BLK, BLK), 1)
    barrier = 0.5 * (stepped + jnp.sqrt(stepped * stepped + 4.0 * step))
    return jnp.where(row == col, barrier, shrunk)


def second_kernel(squares, omega, grad, high, low, iterate, grad2, squares2):
    step = step_of(squares)
    packed = []
    for k in range(K):
        value = proximal(omega[k].astype(F32), grad[k], step, k)
        iterate[k] = value
        packed.append(value.astype(BF16))
    grads = times_gram(packed, high, low)
    for k in range(K):
        grad2[k] = grads[k]
    put_squares(grads, squares2)


def last_kernel(squares, iterate, grad, out):
    step = step_of(squares)
    for k in range(K):
        out[k] = proximal(iterate[k], grad[k], step, k)


def relay_kernel(rows, out):
    out[...] = jnp.broadcast_to(jnp.sum(rows[...], axis=0, keepdims=True), out.shape)


def call(kernel, shapes, *args):
    shapes = [jax.ShapeDtypeStruct(s, d) for s, d in shapes]
    return pl.pallas_call(
        kernel,
        out_shape=shapes,
        in_specs=[VMEM] * len(args),
        out_specs=[VMEM] * len(shapes),
        compiler_params=params(),
        name=kernel.__name__,
    )(*args)


def everywhere(rows):
    rows = lax.all_to_all(rows, ("xh", "y", "xl"), 0, 0, tiled=True)
    (rows,) = call(relay_kernel, [((32, BLK), F32)], rows)
    return lax.all_to_all(rows, ("z", "core"), 0, 0, tiled=True)


def swap(block, axis):
    return lax.ppermute(block, axis, [(0, 1), (1, 0)])


def along_z(block):
    depth, wide = SIZES[0], SIZES[1]
    route = []
    for z in range(depth):
        route.append((z * wide, (z + 1) % depth * wide))
        route.append((z * wide + 1, (z - 1) % depth * wide + 1))
    return lax.ppermute(block, ("z", "xh"), route)


def body(observed, pattern, omega_init):
    z, xh, core = (lax.axis_index(a) for a in VAR_AXES)
    samp = lax.axis_index("y") * 2 + lax.axis_index("xl")
    var = (z * 2 + xh) * 2 + core
    var_count = SIZES[0] * 4
    offset = (pattern // ROWB - var + var_count + 2) % var_count - 2
    near = jnp.where((offset == 1) == (core == 0), 1, 3)
    far = jnp.where((offset == 2) == (xh == 0), 2, 4)
    source = jnp.where(offset == 0, 0, jnp.where(abs(offset) == 1, near, far)).astype(jnp.int32)
    column = (pattern % ROWB).astype(jnp.int32)

    part = observed.shape[0] // CHUNKS
    partner = swap(observed, "core")
    across = [swap(observed[i * part : (i + 1) * part], "xh") for i in range(CHUNKS)]
    beyond = [along_z(a) for a in across]
    beside = [swap(jnp.where(core == xh, a, b), "core") for a, b in zip(across, beyond)]
    grams = gram(source, column, [observed, partner, *across, *beside, *beyond])
    parts = lax.all_to_all(grams, SAMP_AXES, 0, 0, tiled=True)

    omega = lax.dynamic_index_in_dim(omega_init, samp, 0, keepdims=False)
    side = K * BLK
    blocks = (K, BLK, BLK)
    high, low, grad, squares = call(
        first_kernel,
        [((side, side), BF16), ((side, side), BF16), (blocks, F32), ((16, BLK), F32)],
        parts,
        omega,
    )
    iterate, grad, squares = call(
        second_kernel,
        [(blocks, F32), (blocks, F32), ((16, BLK), F32)],
        everywhere(squares),
        omega,
        grad,
        high,
        low,
    )
    (precision,) = call(last_kernel, [(blocks, F32)], everywhere(squares), iterate, grad)
    return precision[None]


def solution(mesh):
    fine = Mesh(mesh.devices.reshape(SIZES), AXES)
    return jax.shard_map(
        body,
        mesh=fine,
        in_specs=(P(SAMP_AXES, VAR_AXES), P(VAR_AXES, None), P(VAR_AXES, None, None, None)),
        out_specs=P(AXES, None, None, None),
        check_vma=False,
    )
```

time: 602 us -> 154 us (0.26)
  waiting for transfers between devices: 254 us -> 41.5 us
  blocking collectives: 265 us -> 59.9 us
  local copies, waits for them, and re-layouts: 25.1 us -> 1.51 us
  starting transfers between devices: 20.9 us -> 38.4 us
  between operations: 14.9 us -> 0.17 us
  matrix products: 13.1 us -> 0 us
  Pallas kernels: 0 us -> 8.98 us
    psum x2 -> x0, blocking collectives: 265 us -> none  [body(): squares = lax.psum(jnp.sum(grad * grad), 'var')]
    psum x2 -> x0, waiting for transfers between devices: 204 us -> none  [body(): grad = lax.psum(partial_grad, 'samp')]
    all_to_all x0 -> x4, blocking collectives: none -> 59.9 us  [the longest x2 39.6 us: everywhere(): return lax.all_to_all(rows, ('z', 'core'), 0, 0, tiled=True)]
    ppermute x4 -> x7, waiting for transfers between devices: 49.9 us -> 20.7 us  [the longest x5 12.3 us: swap(): return lax.ppermute(block, axis, [(0, 1), (1, 0)])]
    all_to_all x0 -> x1, waiting for transfers between devices: none -> 20.8 us  [body(): parts = lax.all_to_all(grams, SAMP_AXES, 0, 0, tiled=True)]
    dot_general x2 -> x0, matrix products: 13.1 us -> none  [block_terms(): jnp.einsum('rna,nrkb->rkab', weighted, selected, preferred_element_type=j...]
    ppermute x4 -> x7, starting transfers between devices: 20.8 us -> 33.2 us  [the longest x5 19.4 us: swap(): return lax.ppermute(block, axis, [(0, 1), (1, 0)])]
    pallas_call x0 -> x6, Pallas kernels: none -> 8.98 us  [the longest x1 7.08 us: gram(): pl.pallas_call(gram_kernel, out_shape=jax.ShapeDtypeStruct((ROWB, NPAIR,...]
  transfers between devices with their start and end apart: 6 -> 8, of which waited for: 4 -> 6; matrix products, arithmetic and copies ran while one was open for 1% -> 2% of each run, Pallas kernels for 0% -> 0%
where the time goes in v1:
time: 154 us; the launch traced here: 153 us
  blocking collectives  59.9 us (39%)
  waiting for transfers between devices  41.5 us (27%)
  starting transfers between devices  38.4 us (25%)
  Pallas kernels  8.98 us (6%)
  other arithmetic  2.77 us (2%)
    all_to_all x2, blocking collectives, everywhere(): return lax.all_to_all(rows, ('z', 'core'), 0, 0, tiled=True)  39.6 us
    all_to_all x1, waiting for transfers between devices, body(): parts = lax.all_to_all(grams, SAMP_AXES, 0, 0, tiled=True)  20.8 us
    all_to_all x2, blocking collectives, everywhere(): rows = lax.all_to_all(rows, ('xh', 'y', 'xl'), 0, 0, tiled=True)  20.3 us
    ppermute x5, starting transfers between devices, swap(): return lax.ppermute(block, axis, [(0, 1), (1, 0)])  19.4 us
    ppermute x2, starting transfers between devices, along_z(): return lax.ppermute(block, ('z', 'xh'), route)  13.8 us
    ppermute x5, waiting for transfers between devices, swap(): return lax.ppermute(block, axis, [(0, 1), (1, 0)])  12.3 us
    ppermute x2, waiting for transfers between devices, along_z(): return lax.ppermute(block, ('z', 'xh'), route)  8.49 us
    pallas_call x1, Pallas kernels, gram(): pl.pallas_call(gram_kernel, out_shape=jax.ShapeDtypeStruct((ROWB, NPAIR,...  7.08 us
  transfers between devices with their start and end apart: 8, of which 6 were waited for; matrix products, arithmetic and copies ran while one was open for 2% of the time, Pallas kernels for 0%

profile of v1, /device:TPU:1, one launch (start us, length us, event | category | flops | bytes accessed | tf_op | source)
XLA Modules:
  0.0 153.2 jit_solution(4884012457546635922)
XLA Ops:
  0.0 0.0 copy-start
  0.0 0.0 copy-start.1
  0.0 1.4 fusion.6
  1.4 5.5 %collective-permute-start.1 = (bf16[256,1024]{1,0:T(8,128)(2,1)S(1)}, bf16[256,1024]{1,0:T(8,128)(2,1)S(1)}, u32[]{:S(2)}, u32[]{:S(2)}) collective-permute-start(bf16[256,1024]{1,0:T(8,128)(2,1)S(1)} %get-tuple-element.20), channel_id=1, source_target_pairs={{0,16},{16,0},{1,17},{17,1},{2,18},{18,2},{3,19},{19,3},{4,20},{20... | collective-permute-start | bytes 1572872 | tf_op jit(solution)/shard_map/ppermute | solution.py:180
  6.9 1.9 %collective-permute-start.2 = (bf16[256,1024]{1,0:T(8,128)(2,1)S(1)}, bf16[256,1024]{1,0:T(8,128)(2,1)S(1)}, u32[]{:S(2)}, u32[]{:S(2)}) collective-permute-start(bf16[256,1024]{1,0:T(8,128)(2,1)S(1)} %get-tuple-element.19), channel_id=1, source_target_pairs={{0,16},{16,0},{1,17},{17,1},{2,18},{18,2},{3,19},{19,3},{4,20},{20... | collective-permute-start | bytes 1572872 | tf_op jit(solution)/shard_map/ppermute | solution.py:180
  8.8 6.2 %collective-permute-done.1.refs_2_ = bf16[256,1024]{1,0:T(8,128)(2,1)S(1)} collective-permute-done((bf16[256,1024]{1,0:T(8,128)(2,1)S(1)}, bf16[256,1024]{1,0:T(8,128)(2,1)S(1)}, u32[]{:S(2)}, u32[]{:S(2)}) %collective-permute-start.1) | collective-permute-done | bytes 524320 | tf_op jit(solution)/shard_map/ppermute | solution.py:180
  15.1 6.9 %collective-permute-start.3 = (bf16[256,1024]{1,0:T(8,128)(2,1)S(1)}, bf16[256,1024]{1,0:T(8,128)(2,1)S(1)}, u32[]{:S(2)}, u32[]{:S(2)}) collective-permute-start(bf16[256,1024]{1,0:T(8,128)(2,1)S(1)} %collective-permute-done.1.refs_2_), channel_id=1, source_target_pairs={{0,32},{16,496},{32,64},{48,16},{64,96},{80,48},{96,128},{112,80},... | collective-permute-start | bytes 1572872 | tf_op jit(solution)/shard_map/ppermute | solution.py:189
  22.0 4.3 %collective-permute-done.2.refs_3_ = bf16[256,1024]{1,0:T(8,128)(2,1)S(1)} collective-permute-done((bf16[256,1024]{1,0:T(8,128)(2,1)S(1)}, bf16[256,1024]{1,0:T(8,128)(2,1)S(1)}, u32[]{:S(2)}, u32[]{:S(2)}) %collective-permute-start.2) | collective-permute-done | bytes 524320 | tf_op jit(solution)/shard_map/ppermute | solution.py:180
  26.3 6.9 %collective-permute-start.5 = (bf16[256,1024]{1,0:T(8,128)(2,1)S(1)}, bf16[256,1024]{1,0:T(8,128)(2,1)}, u32[]{:S(2)}, u32[]{:S(2)}) collective-permute-start(bf16[256,1024]{1,0:T(8,128)(2,1)S(1)} %collective-permute-done.2.refs_3_), channel_id=1, source_target_pairs={{0,32},{16,496},{32,64},{48,16},{64,96},{80,48},{96,128},{112,80},... | collective-permute-start | bytes 1572872 | tf_op jit(solution)/shard_map/ppermute | solution.py:189
  33.2 0.0 copy-done.1
  33.2 3.7 %collective-permute-start = (bf16[512,1024]{1,0:T(8,128)(2,1)S(1)}, bf16[512,1024]{1,0:T(8,128)(2,1)}, u32[]{:S(2)}, u32[]{:S(2)}) collective-permute-start(bf16[512,1024]{1,0:T(8,128)(2,1)S(1)} %copy-done.1), channel_id=1, source_target_pairs={{0,8},{8,0},{1,9},{9,1},{2,10},{10,2},{3,11},{11,3},{4,12},{12,4},... | collective-permute-start | bytes 3145736 | tf_op jit(solution)/shard_map/ppermute | solution.py:180
  37.0 0.0 copy-start.2
  37.0 2.1 %collective-permute-done.3.refs_6_ = bf16[256,1024]{1,0:T(8,128)(2,1)S(1)} collective-permute-done((bf16[256,1024]{1,0:T(8,128)(2,1)S(1)}, bf16[256,1024]{1,0:T(8,128)(2,1)S(1)}, u32[]{:S(2)}, u32[]{:S(2)}) %collective-permute-start.3) | collective-permute-done | bytes 524320 | tf_op jit(solution)/shard_map/ppermute | solution.py:189
  39.1 0.8 broadcast_select_fusion.1
  39.9 5.2 %collective-permute-start.4 = (bf16[256,1024]{1,0:T(8,128)(2,1)}, bf16[256,1024]{1,0:T(8,128)(2,1)}, u32[]{:S(2)}, u32[]{:S(2)}) collective-permute-start(bf16[256,1024]{1,0:T(8,128)(2,1)} %broadcast_select_fusion.1), channel_id=1, source_target_pairs={{0,8},{8,0},{1,9},{9,1},{2,10},{10,2},{3,11},{11,3},{4,12},{12,4},... | collective-permute-start | bytes 1572872 | tf_op jit(solution)/shard_map/ppermute | solution.py:180
  45.2 6.4 %collective-permute-done.5.refs_7_ = bf16[256,1024]{1,0:T(8,128)(2,1)} collective-permute-done((bf16[256,1024]{1,0:T(8,128)(2,1)S(1)}, bf16[256,1024]{1,0:T(8,128)(2,1)}, u32[]{:S(2)}, u32[]{:S(2)}) %collective-permute-start.5) | collective-permute-done | bytes 524320 | tf_op jit(solution)/shard_map/ppermute | solution.py:189
  51.6 1.9 %broadcast_select_fusion = bf16[256,1024]{1,0:T(8,128)(2,1)} fusion(bf16[256,1024]{1,0:T(8,128)(2,1)S(1)} %collective-permute-done.2.refs_3_, bf16[256,1024]{1,0:T(8,128)(2,1)} %collective-permute-done.5.refs_7_, pred[]{:T(512)S(6)} %eq.47), kind=kLoop, calls=%fused_computation | loop fusion | flops 262144 | bytes 1572865 | tf_op jit(solution)/shard_map/jit(_where)/select_n | solution.py:207
  53.5 3.0 %collective-permute-start.6 = (bf16[256,1024]{1,0:T(8,128)(2,1)}, bf16[256,1024]{1,0:T(8,128)(2,1)}, u32[]{:S(2)}, u32[]{:S(2)}) collective-permute-start(bf16[256,1024]{1,0:T(8,128)(2,1)} %broadcast_select_fusion), channel_id=1, source_target_pairs={{0,8},{8,0},{1,9},{9,1},{2,10},{10,2},{3,11},{11,3},{4,12},{12,4},... | collective-permute-start | bytes 1572872 | tf_op jit(solution)/shard_map/ppermute | solution.py:180
  56.5 0.0 copy-done.2
  56.5 0.1 copy.8
  56.7 0.0 collective-permute-done.refs_1_
  56.7 0.0 collective-permute-done.4.refs_4_
  56.7 1.7 %collective-permute-done.6.refs_5_ = bf16[256,1024]{1,0:T(8,128)(2,1)} collective-permute-done((bf16[256,1024]{1,0:T(8,128)(2,1)}, bf16[256,1024]{1,0:T(8,128)(2,1)}, u32[]{:S(2)}, u32[]{:S(2)}) %collective-permute-start.6) | collective-permute-done | bytes 524320 | tf_op jit(solution)/shard_map/ppermute | solution.py:180
  58.4 7.1 %gram.1 = bf16[8,6,128,128]{3,2,1,0:T(8,128)(2,1)} custom-call(s32[8,3]{1,0:T(8,128)S(1)} %get-tuple-element.22.source, s32[8,3]{1,0:T(8,128)S(1)} %get-tuple-element.21.column, bf16[512,1024]{1,0:T(8,128)(2,1)S(1)} %copy-done.1, bf16[512,1024]{1,0:T(8,128)(2,1)} %collective-permute-done.refs_1_, bf16[256,1024]{1,0:T(8,128)(2,1)S(1)} %collective-permute-done.1.refs_2_, ...), custom_call_target="tpu_custom_call" | custom-call | tf_op jit(solution)/shard_map/gram/pallas_call | solution.py:72
  65.5 5.1 %all-to-all-start = ((bf16[8,6,128,128]{3,2,1,0:T(8,128)(2,1)}), bf16[8,6,128,128]{3,2,1,0:T(8,128)(2,1)S(1)}, u32[]{:S(2)}, u32[]{:S(2)}) async-start(bf16[8,6,128,128]{3,2,1,0:T(8,128)(2,1)} %gram.1), calls=%async_computation | async-start | bytes 3145728 | tf_op jit(solution)/shard_map/all_to_all | solution.py:209
  70.6 0.0 copy-done
  70.6 20.8 %all-to-all-done.parts = bf16[8,6,128,128]{3,2,1,0:T(8,128)(2,1)S(1)} async-done(((bf16[8,6,128,128]{3,2,1,0:T(8,128)(2,1)}), bf16[8,6,128,128]{3,2,1,0:T(8,128)(2,1)S(1)}, u32[]{:S(2)}, u32[]{:S(2)}) %all-to-all-start) | async-done | bytes 1572896 | tf_op jit(solution)/shard_map/all_to_all | solution.py:209
  91.4 0.6 first_kernel.1
  92.0 11.2 %all_to_all.49 = f32[16,1,128]{2,1,0:T(1,128)S(1)} all-to-all(f32[16,1,128]{2,1,0:T(1,128)S(1)} %bitcast.26), channel_id=1, replica_groups=mesh['z'=16,'xh'=2,'core'=2,'y'=4,'xl'=2] {'xh','y','xl'}, dimensions={0} | all-to-all | bytes 16384 | tf_op jit(solution)/shard_map/all_to_all | solution.py:174
  103.2 22.8 %all_to_all.50 = f32[32,1,128]{2,1,0:T(1,128)S(1)} all-to-all(f32[32,1,128]{2,1,0:T(1,128)S(1)} %bitcast.21), channel_id=1, replica_groups=mesh['z'=16,'xh'=2,'core'=2,'y'=4,'xl'=2] {'z','core'}, dimensions={0} | all-to-all | bytes 32768 | tf_op jit(solution)/shard_map/all_to_all | solution.py:176
  126.0 0.5 second_kernel.1
  126.4 9.1 %all_to_all.51 = f32[16,1,128]{2,1,0:T(1,128)S(1)} all-to-all(f32[16,1,128]{2,1,0:T(1,128)S(1)} %bitcast.25), channel_id=1, replica_groups=mesh['z'=16,'xh'=2,'core'=2,'y'=4,'xl'=2] {'xh','y','xl'}, dimensions={0} | all-to-all | bytes 16384 | tf_op jit(solution)/shard_map/all_to_all | solution.py:174
  135.5 16.8 %all_to_all.52 = f32[32,1,128]{2,1,0:T(1,128)S(1)} all-to-all(f32[32,1,128]{2,1,0:T(1,128)S(1)} %bitcast.22), channel_id=1, replica_groups=mesh['z'=16,'xh'=2,'core'=2,'y'=4,'xl'=2] {'z','core'}, dimensions={0} | all-to-all | bytes 32768 | tf_op jit(solution)/shard_map/all_to_all | solution.py:176
  152.4 0.9 last_kernel.1
  (4 shorter events, 0.1 us)
Async XLA Ops:
  0.0 70.6 %copy-start = (bf16[8,3,128,128]{3,2,1,0:T(8,128)(2,1)S(1)}, bf16[8,3,128,128]{3,2,1,0:T(8,128)(2,1)}, u32[]{:S(2)}) copy-start(bf16[8,3,128,128]{3,2,1,0:T(8,128)(2,1)} %param.5) | copy-start | bytes 2359300
  0.0 33.2 %copy-start.1 = (bf16[512,1024]{1,0:T(8,128)(2,1)S(1)}, bf16[512,1024]{1,0:T(8,128)(2,1)}, u32[]{:S(2)}) copy-start(bf16[512,1024]{1,0:T(8,128)(2,1)} %refs_0_.1) | copy-start | bytes 3145732
  1.4 13.6 %collective-permute-start.1 = (bf16[256,1024]{1,0:T(8,128)(2,1)S(1)}, bf16[256,1024]{1,0:T(8,128)(2,1)S(1)}, u32[]{:S(2)}, u32[]{:S(2)}) collective-permute-start(bf16[256,1024]{1,0:T(8,128)(2,1)S(1)} %get-tuple-element.20), channel_id=1, source_target_pairs={{0,16},{16,0},{1,17},{17,1},{2,18},{18,2},{3,19},{19,3},{4,20},{20... | collective-permute-start | bytes 1572872 | tf_op jit(solution)/shard_map/ppermute | solution.py:180
  6.9 19.4 %collective-permute-start.2 = (bf16[256,1024]{1,0:T(8,128)(2,1)S(1)}, bf16[256,1024]{1,0:T(8,128)(2,1)S(1)}, u32[]{:S(2)}, u32[]{:S(2)}) collective-permute-start(bf16[256,1024]{1,0:T(8,128)(2,1)S(1)} %get-tuple-element.19), channel_id=1, source_target_pairs={{0,16},{16,0},{1,17},{17,1},{2,18},{18,2},{3,19},{19,3},{4,20},{20... | collective-permute-start | bytes 1572872 | tf_op jit(solution)/shard_map/ppermute | solution.py:180
  15.1 24.0 %collective-permute-start.3 = (bf16[256,1024]{1,0:T(8,128)(2,1)S(1)}, bf16[256,1024]{1,0:T(8,128)(2,1)S(1)}, u32[]{:S(2)}, u32[]{:S(2)}) collective-permute-start(bf16[256,1024]{1,0:T(8,128)(2,1)S(1)} %collective-permute-done.1.refs_2_), channel_id=1, source_target_pairs={{0,32},{16,496},{32,64},{48,16},{64,96},{80,48},{96,128},{112,80},... | collective-permute-start | bytes 1572872 | tf_op jit(solution)/shard_map/ppermute | solution.py:189
  26.3 25.3 %collective-permute-start.5 = (bf16[256,1024]{1,0:T(8,128)(2,1)S(1)}, bf16[256,1024]{1,0:T(8,128)(2,1)}, u32[]{:S(2)}, u32[]{:S(2)}) collective-permute-start(bf16[256,1024]{1,0:T(8,128)(2,1)S(1)} %collective-permute-done.2.refs_3_), channel_id=1, source_target_pairs={{0,32},{16,496},{32,64},{48,16},{64,96},{80,48},{96,128},{112,80},... | collective-permute-start | bytes 1572872 | tf_op jit(solution)/shard_map/ppermute | solution.py:189
  33.2 23.4 %collective-permute-start = (bf16[512,1024]{1,0:T(8,128)(2,1)S(1)}, bf16[512,1024]{1,0:T(8,128)(2,1)}, u32[]{:S(2)}, u32[]{:S(2)}) collective-permute-start(bf16[512,1024]{1,0:T(8,128)(2,1)S(1)} %copy-done.1), channel_id=1, source_target_pairs={{0,8},{8,0},{1,9},{9,1},{2,10},{10,2},{3,11},{11,3},{4,12},{12,4},... | collective-permute-start | bytes 3145736 | tf_op jit(solution)/shard_map/ppermute | solution.py:180
  37.0 19.6 %copy-start.2 = (s32[8,3]{0,1:T(4,128)S(1)}, s32[8,3]{0,1:T(4,128)}, u32[]{:S(2)}) copy-start(s32[8,3]{0,1:T(4,128)} %param.4) | copy-start | bytes 292
  39.9 16.7 %collective-permute-start.4 = (bf16[256,1024]{1,0:T(8,128)(2,1)}, bf16[256,1024]{1,0:T(8,128)(2,1)}, u32[]{:S(2)}, u32[]{:S(2)}) collective-permute-start(bf16[256,1024]{1,0:T(8,128)(2,1)} %broadcast_select_fusion.1), channel_id=1, source_target_pairs={{0,8},{8,0},{1,9},{9,1},{2,10},{10,2},{3,11},{11,3},{4,12},{12,4},... | collective-permute-start | bytes 1572872 | tf_op jit(solution)/shard_map/ppermute | solution.py:180
  53.5 4.9 %collective-permute-start.6 = (bf16[256,1024]{1,0:T(8,128)(2,1)}, bf16[256,1024]{1,0:T(8,128)(2,1)}, u32[]{:S(2)}, u32[]{:S(2)}) collective-permute-start(bf16[256,1024]{1,0:T(8,128)(2,1)} %broadcast_select_fusion), channel_id=1, source_target_pairs={{0,8},{8,0},{1,9},{9,1},{2,10},{10,2},{3,11},{11,3},{4,12},{12,4},... | collective-permute-start | bytes 1572872 | tf_op jit(solution)/shard_map/ppermute | solution.py:180
  65.5 25.9 %all-to-all-start = ((bf16[8,6,128,128]{3,2,1,0:T(8,128)(2,1)}), bf16[8,6,128,128]{3,2,1,0:T(8,128)(2,1)S(1)}, u32[]{:S(2)}, u32[]{:S(2)}) async-start(bf16[8,6,128,128]{3,2,1,0:T(8,128)(2,1)} %gram.1), calls=%async_computation | async-start | bytes 3145728 | tf_op jit(solution)/shard_map/all_to_all | solution.py:209

commit v2 on v1

--- a/solution.py
+++ b/solution.py
@@ -13,15 +13,18 @@
 SIZES = (16, 2, 2, 4, 2)
 VAR_AXES = ("z", "xh", "core")
 SAMP_AXES = ("y", "xl")
-CHUNKS = 2
+SIZES_OF_CHUNKS = (176, 176, 160)
+CHUNKS = len(SIZES_OF_CHUNKS)
 ROWB = 8
 K = 3
 BLK = 128
 SAMPLES = 4096
 ENTRIES = 25165824
 SAMP = 8
-PAIRS = ((0, 0), (0, 1), (0, 2), (1, 1), (1, 2), (2, 2))
-NPAIR = len(PAIRS)
+CROSS = ((0, 1), (0, 2), (1, 2))
+MIXED = 4 * BLK
+DIAGS = 5 * BLK
+GRAM_ROWS = 5 * BLK + 16
 
 VMEM = pl.BlockSpec(memory_space=pltpu.VMEM)
 SMEM = pl.BlockSpec(memory_space=pltpu.SMEM)
@@ -31,56 +34,85 @@
 
 
 def params():
-    return pltpu.CompilerParams(vmem_limit_bytes=48 * 1024 * 1024)
-
-
-def gram_kernel(source, column, *refs):
-    inputs = refs[: 2 + 3 * CHUNKS]
-    out, held, sems = refs[2 + 3 * CHUNKS :]
-    samples = held.shape[1]
-    part = samples // CHUNKS
-    copies = [
-        pltpu.make_async_copy(inputs[0], held.at[0], sems.at[0]),
-        pltpu.make_async_copy(inputs[1], held.at[1], sems.at[1]),
-    ]
+    return pltpu.CompilerParams(vmem_limit_bytes=16 * 1024 * 1024)
+
+
+def fetch(inputs, held, sems):
+    copies = [pltpu.make_async_copy(inputs[i], held.at[i], sems.at[i]) for i in range(2)]
     for i in range(3 * CHUNKS):
         slot, chunk = 2 + i // CHUNKS, i % CHUNKS
-        rows = pl.ds(chunk * part, part)
+        rows = pl.ds(sum(SIZES_OF_CHUNKS[:chunk]), SIZES_OF_CHUNKS[chunk])
         copies.append(pltpu.make_async_copy(inputs[2 + i], held.at[slot, rows], sems.at[2 + i]))
     for copy in copies:
         copy.start()
     for copy in copies:
         copy.wait()
 
+
+def columns_of(held, source, column, r):
+    return [
+        held[source[r, k], :, pl.ds(pl.multiple_of(column[r, k] * BLK, BLK), BLK)] for k in range(K)
+    ]
+
+
+def dot(left, right, left_dim, right_dim):
+    return lax.dot_general(
+        left, right, (((left_dim,), (right_dim,)), ((), ())), preferred_element_type=F32
+    )
+
+
+def diagonal_mask():
+    row = lax.broadcasted_iota(jnp.int32, (BLK, BLK), 0)
+    col = lax.broadcasted_iota(jnp.int32, (BLK, BLK), 1)
+    return row, col
+
+
+def gram_kernel(source, column, *refs):
+    *inputs, out, held, sems = refs
+    fetch(inputs, held, sems)
+    row, col = diagonal_mask()
+    line = lax.broadcasted_iota(jnp.int32, (16, BLK), 0)
+
     def one(r, carry):
-        cols = [
-            held[source[r, k], :, pl.ds(pl.multiple_of(column[r, k] * BLK, BLK), BLK)]
-            for k in range(K)
+        cols = columns_of(held, source, column, r)
+        scaled = [
+            dot(cols[i], jnp.concatenate(cols[i:], axis=1), 0, 0) * (1.0 / SAMPLES) for i in range(K)
         ]
-        for p, (i, j) in enumerate(PAIRS):
-            gram = lax.dot_general(
-                cols[i], cols[j], (((0,), (0,)), ((), ())), preferred_element_type=F32
-            )
-            out[r, p] = (gram * (1.0 / SAMPLES)).astype(BF16)
+        for p, (i, j) in enumerate(CROSS):
+            at = (j - i) * BLK
+            out[r, pl.ds(p * BLK, BLK), :] = scaled[i][:, at : at + BLK].astype(BF16)
+        own = [block[:, :BLK] for block in scaled]
+        out[r, pl.ds(3 * BLK, BLK), :] = own[2].astype(BF16)
+        out[r, pl.ds(MIXED, BLK), :] = jnp.where(row <= col, own[0], own[1]).astype(BF16)
+        lines = jnp.zeros((16, BLK), F32)
+        for k in range(K):
+            diag = jnp.sum(jnp.where(row == col, own[k], 0.0), axis=0, keepdims=True)
+            high = diag.astype(BF16).astype(F32)
+            lines = jnp.where(line == 2 * k, high, lines)
+            lines = jnp.where(line == 2 * k + 1, diag - high, lines)
+        out[r, pl.ds(DIAGS, 16), :] = lines.astype(BF16)
         return carry
 
-    lax.fori_loop(0, ROWB, one, 0)
-
-
-def gram(source, column, arrays):
+    lax.fori_loop(0, ROWB, one, 0, unroll=True)
+
+
+def on_strips(kernel, shape, specs, *args):
+    arrays = args[len(specs) :]
     samples, columns = arrays[0].shape
+    flops = 2 * ROWB * 6 * BLK * BLK * samples
     return pl.pallas_call(
-        gram_kernel,
-        out_shape=jax.ShapeDtypeStruct((ROWB, NPAIR, BLK, BLK), BF16),
-        in_specs=[SMEM, SMEM] + [ANY] * len(arrays),
+        kernel,
+        out_shape=jax.ShapeDtypeStruct(shape, BF16),
+        in_specs=specs + [ANY] * len(arrays),
         out_specs=VMEM,
         scratch_shapes=[
             pltpu.VMEM((5, samples, columns), BF16),
             pltpu.SemaphoreType.DMA((len(arrays),)),
         ],
         compiler_params=params(),
-        name="gram",
-    )(source, column, *arrays)
+        cost_estimate=pl.CostEstimate(flops=flops, bytes_accessed=12 * samples * columns, transcendentals=0),
+        name=kernel.__name__,
+    )(*args)
 
 
 def times_gram(packed, high, low):
@@ -98,20 +130,31 @@
 
 
 def first_kernel(parts, omega, high, low, grad, squares):
-    for p, (i, j) in enumerate(PAIRS):
-        block = sum(parts[s, p].astype(F32) for s in range(SAMP))
-        hi = block.astype(BF16)
-        lo = (block - hi.astype(F32)).astype(BF16)
+    def summed(start, count):
+        return sum(parts[s, pl.ds(start, count), :].astype(F32) for s in range(SAMP))
+
+    def put(i, j, block):
         at = (pl.ds(i * BLK, BLK), pl.ds(j * BLK, BLK))
-        high[at] = hi
-        low[at] = lo
-        if i != j:
-            flipped = block.T
-            hi = flipped.astype(BF16)
-            lo = (flipped - hi.astype(F32)).astype(BF16)
-            at = (pl.ds(j * BLK, BLK), pl.ds(i * BLK, BLK))
-            high[at] = hi
-            low[at] = lo
+        top = block.astype(BF16)
+        high[at] = top
+        low[at] = (block - top.astype(F32)).astype(BF16)
+
+    row, col = diagonal_mask()
+    lines = summed(DIAGS, 16)
+    mixed = summed(MIXED, BLK)
+    flipped = mixed.T
+    own = (
+        jnp.where(row < col, mixed, flipped),
+        jnp.where(row > col, mixed, flipped),
+        summed(3 * BLK, BLK),
+    )
+    for k in range(K):
+        diag = lines[2 * k : 2 * k + 1, :] + lines[2 * k + 1 : 2 * k + 2, :]
+        put(k, k, jnp.where(row == col, diag, own[k]))
+    for p, (i, j) in enumerate(CROSS):
+        block = summed(p * BLK, BLK)
+        put(i, j, block)
+        put(j, i, block.T)
     grads = times_gram(omega, high, low)
     for k in range(K):
         grad[k] = grads[k]
@@ -129,8 +172,7 @@
     shrunk = stepped - jnp.clip(stepped, -THRESHOLD, THRESHOLD)
     if k:
         return shrunk
-    row = lax.broadcasted_iota(jnp.int32, (BLK, BLK), 0)
-    col = lax.broadcasted_iota(jnp.int32, (BLK, BLK), 1)
+    row, col = diagonal_mask()
     barrier = 0.5 * (stepped + jnp.sqrt(stepped * stepped + 4.0 * step))
     return jnp.where(row == col, barrier, shrunk)
 
@@ -200,14 +242,14 @@
     source = jnp.where(offset == 0, 0, jnp.where(abs(offset) == 1, near, far)).astype(jnp.int32)
     column = (pattern % ROWB).astype(jnp.int32)
 
-    part = observed.shape[0] // CHUNKS
     partner = swap(observed, "core")
-    across = [swap(observed[i * part : (i + 1) * part], "xh") for i in range(CHUNKS)]
+    edges = [sum(SIZES_OF_CHUNKS[:i]) for i in range(CHUNKS + 1)]
+    across = [swap(observed[a:b], "xh") for a, b in zip(edges, edges[1:])]
     beyond = [along_z(a) for a in across]
     beside = [swap(jnp.where(core == xh, a, b), "core") for a, b in zip(across, beyond)]
-    grams = gram(source, column, [observed, partner, *across, *beside, *beyond])
+    strips = [observed, partner, *across, *beside, *beyond]
+    grams = on_strips(gram_kernel, (ROWB, GRAM_ROWS, BLK), [SMEM, SMEM], source, column, *strips)
     parts = lax.all_to_all(grams, SAMP_AXES, 0, 0, tiled=True)
-
     omega = lax.dynamic_index_in_dim(omega_init, samp, 0, keepdims=False)
     side = K * BLK
     blocks = (K, BLK, BLK)

time: 154 us -> 146 us (0.948)
  waiting for transfers between devices: 41.5 us -> 24.6 us
  starting transfers between devices: 38.4 us -> 50.8 us
  blocking collectives: 59.9 us -> 57 us
  local copies, waits for them, and re-layouts: 1.51 us -> 3.84 us
  Pallas kernels: 8.98 us -> 6.91 us
    ppermute x5 -> x7, starting transfers between devices: 19.4 us -> 36 us  [swap(): return lax.ppermute(block, axis, [(0, 1), (1, 0)])]
    ppermute x5 -> x7, waiting for transfers between devices: 12.3 us -> 4.32 us  [swap(): return lax.ppermute(block, axis, [(0, 1), (1, 0)])]
    ppermute x2 -> x3, waiting for transfers between devices: 8.49 us -> 1.96 us  [along_z(): return lax.ppermute(block, ('z', 'xh'), route)]
    ppermute x2 -> x3, starting transfers between devices: 13.8 us -> 10.6 us  [along_z(): return lax.ppermute(block, ('z', 'xh'), route)]
    all_to_all x1, waiting for transfers between devices: 20.8 us -> 18.3 us  [body(): parts = lax.all_to_all(grams, SAMP_AXES, 0, 0, tiled=True)]
    pallas_call x1, Pallas kernels: 7.08 us -> 4.99 us  [on_strips(): pl.pallas_call(kernel, out_shape=jax.ShapeDtypeStruct(shape, BF16), in_sp...]
    unnamed x7 -> x11, local copies, waits for them, and re-layouts: 0.1 us -> 1.8 us
  transfers between devices with their start and end apart: 8 -> 11, of which waited for: 6 -> 4; matrix products, arithmetic and copies ran while one was open for 2% -> 2% of each run, Pallas kernels for 0% -> 0%
where the time goes in v2:
time: 146 us
  blocking collectives  57 us (39%)
  starting transfers between devices  50.8 us (35%)
  waiting for transfers between devices  24.6 us (17%)
  Pallas kernels  6.91 us (5%)
  local copies, waits for them, and re-layouts  3.84 us (3%)
  other arithmetic  2.38 us (2%)
    all_to_all x2, blocking collectives, everywhere(): return lax.all_to_all(rows, ('z', 'core'), 0, 0, tiled=True)  38.2 us
    ppermute x7, starting transfers between devices, swap(): return lax.ppermute(block, axis, [(0, 1), (1, 0)])  36 us
    all_to_all x2, blocking collectives, everywhere(): rows = lax.all_to_all(rows, ('xh', 'y', 'xl'), 0, 0, tiled=True)  18.9 us
    all_to_all x1, waiting for transfers between devices, body(): parts = lax.all_to_all(grams, SAMP_AXES, 0, 0, tiled=True)  18.3 us
    ppermute x3, starting transfers between devices, along_z(): return lax.ppermute(block, ('z', 'xh'), route)  10.6 us
    pallas_call x1, Pallas kernels, on_strips(): pl.pallas_call(kernel, out_shape=jax.ShapeDtypeStruct(shape, BF16), in_sp...  4.99 us
    ppermute x7, waiting for transfers between devices, swap(): return lax.ppermute(block, axis, [(0, 1), (1, 0)])  4.32 us
    all_to_all x1, starting transfers between devices, body(): parts = lax.all_to_all(grams, SAMP_AXES, 0, 0, tiled=True)  4.23 us
  transfers between devices with their start and end apart: 11, of which 4 were waited for; matrix products, arithmetic and copies ran while one was open for 2% of the time, Pallas kernels for 0%

profile of v2, /device:TPU:1, one launch (start us, length us, event | category | flops | bytes accessed | tf_op | source)
XLA Modules:
  0.0 145.8 jit_solution(559811050302324359)
XLA Ops:
  0.0 0.0 copy-start
  0.0 0.0 copy-start.1
  0.0 1.3 fusion.6
  1.3 5.5 %collective-permute-start.1 = (bf16[176,1024]{1,0:T(8,128)(2,1)S(1)}, bf16[176,1024]{1,0:T(8,128)(2,1)S(1)}, u32[]{:S(2)}, u32[]{:S(2)}) collective-permute-start(bf16[176,1024]{1,0:T(8,128)(2,1)S(1)} %get-tuple-element.20), channel_id=1, source_target_pairs={{0,16},{16,0},{1,17},{17,1},{2,18},{18,2},{3,19},{19,3},{4,20},{20... | collective-permute-start | bytes 1081352 | tf_op jit(solution)/shard_map/ppermute | solution.py:222
  6.8 1.9 %collective-permute-start.2 = (bf16[176,1024]{1,0:T(8,128)(2,1)S(1)}, bf16[176,1024]{1,0:T(8,128)(2,1)S(1)}, u32[]{:S(2)}, u32[]{:S(2)}) collective-permute-start(bf16[176,1024]{1,0:T(8,128)(2,1)S(1)} %get-tuple-element.19), channel_id=1, source_target_pairs={{0,16},{16,0},{1,17},{17,1},{2,18},{18,2},{3,19},{19,3},{4,20},{20... | collective-permute-start | bytes 1081352 | tf_op jit(solution)/shard_map/ppermute | solution.py:222
  8.7 2.9 %collective-permute-done.1.refs_2_ = bf16[176,1024]{1,0:T(8,128)(2,1)S(1)} collective-permute-done((bf16[176,1024]{1,0:T(8,128)(2,1)S(1)}, bf16[176,1024]{1,0:T(8,128)(2,1)S(1)}, u32[]{:S(2)}, u32[]{:S(2)}) %collective-permute-start.1) | collective-permute-done | bytes 360480 | tf_op jit(solution)/shard_map/ppermute | solution.py:222
  11.6 6.8 %collective-permute-start.4 = (bf16[176,1024]{1,0:T(8,128)(2,1)S(1)}, bf16[176,1024]{1,0:T(8,128)(2,1)S(1)}, u32[]{:S(2)}, u32[]{:S(2)}) collective-permute-start(bf16[176,1024]{1,0:T(8,128)(2,1)S(1)} %collective-permute-done.1.refs_2_), channel_id=1, source_target_pairs={{0,32},{16,496},{32,64},{48,16},{64,96},{80,48},{96,128},{112,80},... | collective-permute-start | bytes 1081352 | tf_op jit(solution)/shard_map/ppermute | solution.py:231
  18.3 0.0 copy-done.1
  18.3 0.8 slice.11
  19.1 12.2 %collective-permute-start.3 = (bf16[160,1024]{1,0:T(8,128)(2,1)}, bf16[160,1024]{1,0:T(8,128)(2,1)}, u32[]{:S(2)}, u32[]{:S(2)}) collective-permute-start(bf16[160,1024]{1,0:T(8,128)(2,1)} %slice.11), channel_id=1, source_target_pairs={{0,16},{16,0},{1,17},{17,1},{2,18},{18,2},{3,19},{19,3},{4,20},{20... | collective-permute-start | bytes 983048 | tf_op jit(solution)/shard_map/ppermute | solution.py:222
  31.3 0.0 collective-permute-done.2.refs_3_
  31.3 1.9 %collective-permute-start.6 = (bf16[176,1024]{1,0:T(8,128)(2,1)S(1)}, bf16[176,1024]{1,0:T(8,128)(2,1)S(1)}, u32[]{:S(2)}, u32[]{:S(2)}) collective-permute-start(bf16[176,1024]{1,0:T(8,128)(2,1)S(1)} %collective-permute-done.2.refs_3_), channel_id=1, source_target_pairs={{0,32},{16,496},{32,64},{48,16},{64,96},{80,48},{96,128},{112,80},... | collective-permute-start | bytes 1081352 | tf_op jit(solution)/shard_map/ppermute | solution.py:231
  33.3 5.2 %collective-permute-start = (bf16[512,1024]{1,0:T(8,128)(2,1)S(1)}, bf16[512,1024]{1,0:T(8,128)(2,1)}, u32[]{:S(2)}, u32[]{:S(2)}) collective-permute-start(bf16[512,1024]{1,0:T(8,128)(2,1)S(1)} %copy-done.1), channel_id=1, source_target_pairs={{0,8},{8,0},{1,9},{9,1},{2,10},{10,2},{3,11},{11,3},{4,12},{12,4},... | collective-permute-start | bytes 3145736 | tf_op jit(solution)/shard_map/ppermute | solution.py:222
  38.4 0.0 copy-start.4
  38.5 0.0 collective-permute-done.3.refs_4_
  38.5 1.9 %collective-permute-start.8 = (bf16[160,1024]{1,0:T(8,128)(2,1)}, bf16[160,1024]{1,0:T(8,128)(2,1)S(1)}, u32[]{:S(2)}, u32[]{:S(2)}) collective-permute-start(bf16[160,1024]{1,0:T(8,128)(2,1)} %collective-permute-done.3.refs_4_), channel_id=1, source_target_pairs={{0,32},{16,496},{32,64},{48,16},{64,96},{80,48},{96,128},{112,80},... | collective-permute-start | bytes 983048 | tf_op jit(solution)/shard_map/ppermute | solution.py:231
  40.4 0.0 collective-permute-done.4.refs_8_
  40.4 0.8 broadcast_select_fusion.1
  41.2 3.7 %collective-permute-start.5 = (bf16[176,1024]{1,0:T(8,128)(2,1)}, bf16[176,1024]{1,0:T(8,128)(2,1)}, u32[]{:S(2)}, u32[]{:S(2)}) collective-permute-start(bf16[176,1024]{1,0:T(8,128)(2,1)} %broadcast_select_fusion.1), channel_id=1, source_target_pairs={{0,8},{8,0},{1,9},{9,1},{2,10},{10,2},{3,11},{11,3},{4,12},{12,4},... | collective-permute-start | bytes 1081352 | tf_op jit(solution)/shard_map/ppermute | solution.py:222
  44.9 0.0 collective-permute-done.6.refs_9_
  44.9 0.8 broadcast_select_fusion
  45.7 2.3 %collective-permute-start.7 = (bf16[176,1024]{1,0:T(8,128)(2,1)}, bf16[176,1024]{1,0:T(8,128)(2,1)}, u32[]{:S(2)}, u32[]{:S(2)}) collective-permute-start(bf16[176,1024]{1,0:T(8,128)(2,1)} %broadcast_select_fusion), channel_id=1, source_target_pairs={{0,8},{8,0},{1,9},{9,1},{2,10},{10,2},{3,11},{11,3},{4,12},{12,4},... | collective-permute-start | bytes 1081352 | tf_op jit(solution)/shard_map/ppermute | solution.py:222
  48.0 2.0 %collective-permute-done.8.refs_10_ = bf16[160,1024]{1,0:T(8,128)(2,1)S(1)} collective-permute-done((bf16[160,1024]{1,0:T(8,128)(2,1)}, bf16[160,1024]{1,0:T(8,128)(2,1)S(1)}, u32[]{:S(2)}, u32[]{:S(2)}) %collective-permute-start.8) | collective-permute-done | bytes 327712 | tf_op jit(solution)/shard_map/ppermute | solution.py:231
  49.9 0.8 broadcast_select_fusion.2
  50.7 0.0 copy-start.2
  50.7 0.7 copy-done.2
  51.5 5.2 %collective-permute-start.9 = (bf16[160,1024]{1,0:T(8,128)(2,1)}, bf16[160,1024]{1,0:T(8,128)(2,1)}, u32[]{:S(2)}, u32[]{:S(2)}) collective-permute-start(bf16[160,1024]{1,0:T(8,128)(2,1)} %broadcast_select_fusion.2), channel_id=1, source_target_pairs={{0,8},{8,0},{1,9},{9,1},{2,10},{10,2},{3,11},{11,3},{4,12},{12,4},... | collective-permute-start | bytes 983048 | tf_op jit(solution)/shard_map/ppermute | solution.py:222
  56.7 0.0 copy-done.4
  56.7 0.1 copy.8
  56.8 1.4 collective-permute-done.9.refs_7_
  58.3 0.0 collective-permute-done.refs_1_
  58.3 0.0 collective-permute-done.5.refs_5_
  58.3 0.0 collective-permute-done.7.refs_6_
  58.3 0.0 copy-start.3
  58.3 1.0 copy-done.3
  59.3 5.0 %gram_kernel.1 = bf16[8,656,128]{2,1,0:T(8,128)(2,1)} custom-call(s32[8,3]{1,0:T(8,128)S(1)} %get-tuple-element.22.source, s32[8,3]{1,0:T(8,128)S(1)} %get-tuple-element.21.column, bf16[512,1024]{1,0:T(8,128)(2,1)S(1)} %copy-done.1, bf16[512,1024]{1,0:T(8,128)(2,1)} %collective-permute-done.refs_1_, bf16[176,1024]{1,0:T(8,128)(2,1)S(1)} %collective-permute-done.1.refs_2_, ...), custom_call_target="tpu_custom_call" | custom-call | flops 805306368 | bytes 6291456 | tf_op jit(solution)/shard_map/gram_kernel/pallas_call | solution.py:103
  64.3 4.2 %all-to-all-start = ((bf16[8,656,128]{2,1,0:T(8,128)(2,1)}), bf16[8,656,128]{2,1,0:T(8,128)(2,1)S(1)}, u32[]{:S(2)}, u32[]{:S(2)}) async-start(bf16[8,656,128]{2,1,0:T(8,128)(2,1)} %gram_kernel.1), calls=%async_computation | async-start | bytes 2686976 | tf_op jit(solution)/shard_map/all_to_all | solution.py:252
  68.5 0.0 copy-done
  68.5 18.3 %all-to-all-done.parts = bf16[8,656,128]{2,1,0:T(8,128)(2,1)S(1)} async-done(((bf16[8,656,128]{2,1,0:T(8,128)(2,1)}), bf16[8,656,128]{2,1,0:T(8,128)(2,1)S(1)}, u32[]{:S(2)}, u32[]{:S(2)}) %all-to-all-start) | async-done | bytes 1343520 | tf_op jit(solution)/shard_map/all_to_all | solution.py:252
  86.8 0.6 first_kernel.1
  87.4 9.8 %all_to_all.49 = f32[16,1,128]{2,1,0:T(1,128)S(1)} all-to-all(f32[16,1,128]{2,1,0:T(1,128)S(1)} %bitcast.26), channel_id=1, replica_groups=mesh['z'=16,'xh'=2,'core'=2,'y'=4,'xl'=2] {'xh','y','xl'}, dimensions={0} | all-to-all | bytes 16384 | tf_op jit(solution)/shard_map/all_to_all | solution.py:216
  97.2 21.3 %all_to_all.50 = f32[32,1,128]{2,1,0:T(1,128)S(1)} all-to-all(f32[32,1,128]{2,1,0:T(1,128)S(1)} %bitcast.21), channel_id=1, replica_groups=mesh['z'=16,'xh'=2,'core'=2,'y'=4,'xl'=2] {'z','core'}, dimensions={0} | all-to-all | bytes 32768 | tf_op jit(solution)/shard_map/all_to_all | solution.py:218
  118.5 0.5 second_kernel.1
  118.9 9.1 %all_to_all.51 = f32[16,1,128]{2,1,0:T(1,128)S(1)} all-to-all(f32[16,1,128]{2,1,0:T(1,128)S(1)} %bitcast.25), channel_id=1, replica_groups=mesh['z'=16,'xh'=2,'core'=2,'y'=4,'xl'=2] {'xh','y','xl'}, dimensions={0} | all-to-all | bytes 16384 | tf_op jit(solution)/shard_map/all_to_all | solution.py:216
  128.1 16.8 %all_to_all.52 = f32[32,1,128]{2,1,0:T(1,128)S(1)} all-to-all(f32[32,1,128]{2,1,0:T(1,128)S(1)} %bitcast.22), channel_id=1, replica_groups=mesh['z'=16,'xh'=2,'core'=2,'y'=4,'xl'=2] {'z','core'}, dimensions={0} | all-to-all | bytes 32768 | tf_op jit(solution)/shard_map/all_to_all | solution.py:218
  144.9 0.9 last_kernel.1
  (4 shorter events, 0.1 us)
Async XLA Ops:
  0.0 68.5 %copy-start = (bf16[8,3,128,128]{3,2,1,0:T(8,128)(2,1)S(1)}, bf16[8,3,128,128]{3,2,1,0:T(8,128)(2,1)}, u32[]{:S(2)}) copy-start(bf16[8,3,128,128]{3,2,1,0:T(8,128)(2,1)} %param.5) | copy-start | bytes 2359300
  0.0 18.3 %copy-start.1 = (bf16[512,1024]{1,0:T(8,128)(2,1)S(1)}, bf16[512,1024]{1,0:T(8,128)(2,1)}, u32[]{:S(2)}) copy-start(bf16[512,1024]{1,0:T(8,128)(2,1)} %refs_0_.1) | copy-start | bytes 3145732
  1.3 10.3 %collective-permute-start.1 = (bf16[176,1024]{1,0:T(8,128)(2,1)S(1)}, bf16[176,1024]{1,0:T(8,128)(2,1)S(1)}, u32[]{:S(2)}, u32[]{:S(2)}) collective-permute-start(bf16[176,1024]{1,0:T(8,128)(2,1)S(1)} %get-tuple-element.20), channel_id=1, source_target_pairs={{0,16},{16,0},{1,17},{17,1},{2,18},{18,2},{3,19},{19,3},{4,20},{20... | collective-permute-start | bytes 1081352 | tf_op jit(solution)/shard_map/ppermute | solution.py:222
  6.8 24.6 %collective-permute-start.2 = (bf16[176,1024]{1,0:T(8,128)(2,1)S(1)}, bf16[176,1024]{1,0:T(8,128)(2,1)S(1)}, u32[]{:S(2)}, u32[]{:S(2)}) collective-permute-start(bf16[176,1024]{1,0:T(8,128)(2,1)S(1)} %get-tuple-element.19), channel_id=1, source_target_pairs={{0,16},{16,0},{1,17},{17,1},{2,18},{18,2},{3,19},{19,3},{4,20},{20... | collective-permute-start | bytes 1081352 | tf_op jit(solution)/shard_map/ppermute | solution.py:222
  11.6 28.8 %collective-permute-start.4 = (bf16[176,1024]{1,0:T(8,128)(2,1)S(1)}, bf16[176,1024]{1,0:T(8,128)(2,1)S(1)}, u32[]{:S(2)}, u32[]{:S(2)}) collective-permute-start(bf16[176,1024]{1,0:T(8,128)(2,1)S(1)} %collective-permute-done.1.refs_2_), channel_id=1, source_target_pairs={{0,32},{16,496},{32,64},{48,16},{64,96},{80,48},{96,128},{112,80},... | collective-permute-start | bytes 1081352 | tf_op jit(solution)/shard_map/ppermute | solution.py:231
  19.1 19.4 %collective-permute-start.3 = (bf16[160,1024]{1,0:T(8,128)(2,1)}, bf16[160,1024]{1,0:T(8,128)(2,1)}, u32[]{:S(2)}, u32[]{:S(2)}) collective-permute-start(bf16[160,1024]{1,0:T(8,128)(2,1)} %slice.11), channel_id=1, source_target_pairs={{0,16},{16,0},{1,17},{17,1},{2,18},{18,2},{3,19},{19,3},{4,20},{20... | collective-permute-start | bytes 983048 | tf_op jit(solution)/shard_map/ppermute | solution.py:222
  31.3 13.6 %collective-permute-start.6 = (bf16[176,1024]{1,0:T(8,128)(2,1)S(1)}, bf16[176,1024]{1,0:T(8,128)(2,1)S(1)}, u32[]{:S(2)}, u32[]{:S(2)}) collective-permute-start(bf16[176,1024]{1,0:T(8,128)(2,1)S(1)} %collective-permute-done.2.refs_3_), channel_id=1, source_target_pairs={{0,32},{16,496},{32,64},{48,16},{64,96},{80,48},{96,128},{112,80},... | collective-permute-start | bytes 1081352 | tf_op jit(solution)/shard_map/ppermute | solution.py:231
  33.3 25.0 %collective-permute-start = (bf16[512,1024]{1,0:T(8,128)(2,1)S(1)}, bf16[512,1024]{1,0:T(8,128)(2,1)}, u32[]{:S(2)}, u32[]{:S(2)}) collective-permute-start(bf16[512,1024]{1,0:T(8,128)(2,1)S(1)} %copy-done.1), channel_id=1, source_target_pairs={{0,8},{8,0},{1,9},{9,1},{2,10},{10,2},{3,11},{11,3},{4,12},{12,4},... | collective-permute-start | bytes 3145736 | tf_op jit(solution)/shard_map/ppermute | solution.py:222
  38.4 18.3 %copy-start.4 = (s32[8,3]{0,1:T(4,128)S(1)}, s32[8,3]{0,1:T(4,128)}, u32[]{:S(2)}) copy-start(s32[8,3]{0,1:T(4,128)} %param.4) | copy-start | bytes 292
  38.5 11.5 %collective-permute-start.8 = (bf16[160,1024]{1,0:T(8,128)(2,1)}, bf16[160,1024]{1,0:T(8,128)(2,1)S(1)}, u32[]{:S(2)}, u32[]{:S(2)}) collective-permute-start(bf16[160,1024]{1,0:T(8,128)(2,1)} %collective-permute-done.3.refs_4_), channel_id=1, source_target_pairs={{0,32},{16,496},{32,64},{48,16},{64,96},{80,48},{96,128},{112,80},... | collective-permute-start | bytes 983048 | tf_op jit(solution)/shard_map/ppermute | solution.py:231
  41.2 17.1 %collective-permute-start.5 = (bf16[176,1024]{1,0:T(8,128)(2,1)}, bf16[176,1024]{1,0:T(8,128)(2,1)}, u32[]{:S(2)}, u32[]{:S(2)}) collective-permute-start(bf16[176,1024]{1,0:T(8,128)(2,1)} %broadcast_select_fusion.1), channel_id=1, source_target_pairs={{0,8},{8,0},{1,9},{9,1},{2,10},{10,2},{3,11},{11,3},{4,12},{12,4},... | collective-permute-start | bytes 1081352 | tf_op jit(solution)/shard_map/ppermute | solution.py:222
  45.7 12.6 %collective-permute-start.7 = (bf16[176,1024]{1,0:T(8,128)(2,1)}, bf16[176,1024]{1,0:T(8,128)(2,1)}, u32[]{:S(2)}, u32[]{:S(2)}) collective-permute-start(bf16[176,1024]{1,0:T(8,128)(2,1)} %broadcast_select_fusion), channel_id=1, source_target_pairs={{0,8},{8,0},{1,9},{9,1},{2,10},{10,2},{3,11},{11,3},{4,12},{12,4},... | collective-permute-start | bytes 1081352 | tf_op jit(solution)/shard_map/ppermute | solution.py:222
  50.7 0.7 copy-start.2
  51.5 6.8 %collective-permute-start.9 = (bf16[160,1024]{1,0:T(8,128)(2,1)}, bf16[160,1024]{1,0:T(8,128)(2,1)}, u32[]{:S(2)}, u32[]{:S(2)}) collective-permute-start(bf16[160,1024]{1,0:T(8,128)(2,1)} %broadcast_select_fusion.2), channel_id=1, source_target_pairs={{0,8},{8,0},{1,9},{9,1},{2,10},{10,2},{3,11},{11,3},{4,12},{12,4},... | collective-permute-start | bytes 983048 | tf_op jit(solution)/shard_map/ppermute | solution.py:222
  58.3 1.0 copy-start.3
  64.3 22.6 %all-to-all-start = ((bf16[8,656,128]{2,1,0:T(8,128)(2,1)}), bf16[8,656,128]{2,1,0:T(8,128)(2,1)S(1)}, u32[]{:S(2)}, u32[]{:S(2)}) async-start(bf16[8,656,128]{2,1,0:T(8,128)(2,1)} %gram_kernel.1), calls=%async_computation | async-start | bytes 2686976 | tf_op jit(solution)/shard_map/all_to_all | solution.py:252

commit v3 on v2

--- a/solution.py
+++ b/solution.py
@@ -13,7 +13,7 @@
 SIZES = (16, 2, 2, 4, 2)
 VAR_AXES = ("z", "xh", "core")
 SAMP_AXES = ("y", "xl")
-SIZES_OF_CHUNKS = (176, 176, 160)
+SIZES_OF_CHUNKS = (128, 128, 128, 128)
 CHUNKS = len(SIZES_OF_CHUNKS)
 ROWB = 8
 K = 3
@@ -22,9 +22,11 @@
 ENTRIES = 25165824
 SAMP = 8
 CROSS = ((0, 1), (0, 2), (1, 2))
-MIXED = 4 * BLK
-DIAGS = 5 * BLK
-GRAM_ROWS = 5 * BLK + 16
+HALF = BLK // 2
+MIXED = 3 * BLK
+FOLDED = 4 * BLK
+DIAGS = FOLDED + HALF
+GRAM_ROWS = DIAGS + 16
 
 VMEM = pl.BlockSpec(memory_space=pltpu.VMEM)
 SMEM = pl.BlockSpec(memory_space=pltpu.SMEM)
@@ -82,7 +84,9 @@
             at = (j - i) * BLK
             out[r, pl.ds(p * BLK, BLK), :] = scaled[i][:, at : at + BLK].astype(BF16)
         own = [block[:, :BLK] for block in scaled]
-        out[r, pl.ds(3 * BLK, BLK), :] = own[2].astype(BF16)
+        top, bottom = own[2][:HALF], pltpu.roll(own[2][HALF:], HALF, 1)
+        folded = jnp.where(row[:HALF] <= col[:HALF], top, bottom)
+        out[r, pl.ds(FOLDED, HALF), :] = folded.astype(BF16)
         out[r, pl.ds(MIXED, BLK), :] = jnp.where(row <= col, own[0], own[1]).astype(BF16)
         lines = jnp.zeros((16, BLK), F32)
         for k in range(K):
@@ -143,10 +147,13 @@
     lines = summed(DIAGS, 16)
     mixed = summed(MIXED, BLK)
     flipped = mixed.T
+    folded = summed(FOLDED, HALF)
+    unfolded = jnp.concatenate([folded, pltpu.roll(folded, HALF, 1)], axis=0)
+    kept = ((row < HALF) & (row < col)) | ((col >= HALF) & (row > col))
     own = (
         jnp.where(row < col, mixed, flipped),
         jnp.where(row > col, mixed, flipped),
-        summed(3 * BLK, BLK),
+        jnp.where(kept, unfolded, unfolded.T),
     )
     for k in range(K):
         diag = lines[2 * k : 2 * k + 1, :] + lines[2 * k + 1 : 2 * k + 2, :]

time: 146 us -> 151 us (1.034)
  waiting for transfers between devices: 24.6 us -> 18.3 us
  blocking collectives: 57 us -> 60.8 us
  other arithmetic: 2.38 us -> 4.91 us
  starting transfers between devices: 50.8 us -> 53.1 us
  local copies, waits for them, and re-layouts: 3.84 us -> 5.6 us
    all_to_all x2, blocking collectives: 18.9 us -> 23.4 us  [everywhere(): rows = lax.all_to_all(rows, ('xh', 'y', 'xl'), 0, 0, tiled=True)]
    ppermute x7 -> x9, waiting for transfers between devices: 4.32 us -> 1.34 us  [swap(): return lax.ppermute(block, axis, [(0, 1), (1, 0)])]
    select_n x3 -> x4, other arithmetic: 2.36 us -> 4.89 us  [body(): jnp.where(core == xh, a, b)]
    ppermute x3 -> x4, waiting for transfers between devices: 1.96 us -> 0.01 us  [along_z(): return lax.ppermute(block, ('z', 'xh'), route)]
    ppermute x3 -> x4, starting transfers between devices: 10.6 us -> 12.5 us  [along_z(): return lax.ppermute(block, ('z', 'xh'), route)]
    unnamed x11 -> x15, local copies, waits for them, and re-layouts: 1.8 us -> 3.4 us
    ppermute x7 -> x9, starting transfers between devices: 36 us -> 35.7 us  [swap(): return lax.ppermute(block, axis, [(0, 1), (1, 0)])]
  transfers between devices with their start and end apart: 11 -> 14, of which waited for: 4 -> 2; matrix products, arithmetic and copies ran while one was open for 2% -> 3% of each run, Pallas kernels for 0% -> 0%
where the time goes in v3:
time: 151 us; the launch traced here: 150 us
  blocking collectives  60.8 us (40%)
  starting transfers between devices  53.1 us (35%)
  waiting for transfers between devices  18.3 us (12%)
  Pallas kernels  7.05 us (5%)
  local copies, waits for them, and re-layouts  5.6 us (4%)
  other arithmetic  4.91 us (3%)
    all_to_all x2, blocking collectives, everywhere(): return lax.all_to_all(rows, ('z', 'core'), 0, 0, tiled=True)  37.4 us
    ppermute x9, starting transfers between devices, swap(): return lax.ppermute(block, axis, [(0, 1), (1, 0)])  35.7 us
    all_to_all x2, blocking collectives, everywhere(): rows = lax.all_to_all(rows, ('xh', 'y', 'xl'), 0, 0, tiled=True)  23.4 us
    all_to_all x1, waiting for transfers between devices, body(): parts = lax.all_to_all(grams, SAMP_AXES, 0, 0, tiled=True)  16.9 us
    ppermute x4, starting transfers between devices, along_z(): return lax.ppermute(block, ('z', 'xh'), route)  12.5 us
    pallas_call x1, Pallas kernels, on_strips(): pl.pallas_call(kernel, out_shape=jax.ShapeDtypeStruct(shape, BF16), in_sp...  5.15 us
    all_to_all x1, starting transfers between devices, body(): parts = lax.all_to_all(grams, SAMP_AXES, 0, 0, tiled=True)  4.92 us
    select_n x4, other arithmetic, body(): jnp.where(core == xh, a, b)  4.89 us
  transfers between devices with their start and end apart: 14, of which 2 were waited for; matrix products, arithmetic and copies ran while one was open for 3% of the time, Pallas kernels for 0%

profile of v3, /device:TPU:1, one launch (start us, length us, event | category | flops | bytes accessed | tf_op | source)
XLA Modules:
  0.0 150.0 jit_solution(7786162204221285749)
XLA Ops:
  0.0 0.0 copy-start
  0.0 0.0 copy-start.1
  0.0 2.2 %fusion.6 = (bf16[128,1024]{1,0:T(8,128)(2,1)S(1)}, bf16[128,1024]{1,0:T(8,128)(2,1)S(1)}, bf16[128,1024]{1,0:T(8,128)(2,1)}, bf16[128,1024]{1,0:T(8,128)(2,1)}) fusion(bf16[512,1024]{1,0:T(8,128)(2,1)} %refs_0_.1), kind=kLoop, calls=%fused_computation.22 | loop fusion | bytes 2097152 | tf_op jit(solution)/shard_map/slice | solution.py:254
  2.2 5.5 %collective-permute-start.3 = (bf16[128,1024]{1,0:T(8,128)(2,1)S(1)}, bf16[128,1024]{1,0:T(8,128)(2,1)S(1)}, u32[]{:S(2)}, u32[]{:S(2)}) collective-permute-start(bf16[128,1024]{1,0:T(8,128)(2,1)S(1)} %get-tuple-element.20), channel_id=1, source_target_pairs={{0,16},{16,0},{1,17},{17,1},{2,18},{18,2},{3,19},{19,3},{4,20},{20... | collective-permute-start | bytes 786440 | tf_op jit(solution)/shard_map/ppermute | solution.py:229
  7.7 1.9 %collective-permute-start.4 = (bf16[128,1024]{1,0:T(8,128)(2,1)S(1)}, bf16[128,1024]{1,0:T(8,128)(2,1)S(1)}, u32[]{:S(2)}, u32[]{:S(2)}) collective-permute-start(bf16[128,1024]{1,0:T(8,128)(2,1)S(1)} %get-tuple-element.19), channel_id=1, source_target_pairs={{0,16},{16,0},{1,17},{17,1},{2,18},{18,2},{3,19},{19,3},{4,20},{20... | collective-permute-start | bytes 786440 | tf_op jit(solution)/shard_map/ppermute | solution.py:229
  9.6 4.9 %collective-permute-start.1 = (bf16[128,1024]{1,0:T(8,128)(2,1)}, bf16[128,1024]{1,0:T(8,128)(2,1)}, u32[]{:S(2)}, u32[]{:S(2)}) collective-permute-start(bf16[128,1024]{1,0:T(8,128)(2,1)} %get-tuple-element.22), channel_id=1, source_target_pairs={{0,16},{16,0},{1,17},{17,1},{2,18},{18,2},{3,19},{19,3},{4,20},{20... | collective-permute-start | bytes 786440 | tf_op jit(solution)/shard_map/ppermute | solution.py:229
  14.5 1.9 %collective-permute-start.2 = (bf16[128,1024]{1,0:T(8,128)(2,1)}, bf16[128,1024]{1,0:T(8,128)(2,1)}, u32[]{:S(2)}, u32[]{:S(2)}) collective-permute-start(bf16[128,1024]{1,0:T(8,128)(2,1)} %get-tuple-element.21), channel_id=1, source_target_pairs={{0,16},{16,0},{1,17},{17,1},{2,18},{18,2},{3,19},{19,3},{4,20},{20... | collective-permute-start | bytes 786440 | tf_op jit(solution)/shard_map/ppermute | solution.py:229
  16.4 0.0 collective-permute-done.3.refs_4_
  16.4 3.8 %collective-permute-start.9 = (bf16[128,1024]{1,0:T(8,128)(2,1)S(1)}, bf16[128,1024]{1,0:T(8,128)(2,1)}, u32[]{:S(2)}, u32[]{:S(2)}) collective-permute-start(bf16[128,1024]{1,0:T(8,128)(2,1)S(1)} %collective-permute-done.3.refs_4_), channel_id=1, source_target_pairs={{0,32},{16,496},{32,64},{48,16},{64,96},{80,48},{96,128},{112,80},... | collective-permute-start | bytes 786440 | tf_op jit(solution)/shard_map/ppermute | solution.py:238
  20.2 0.0 collective-permute-done.4.refs_5_
  20.2 3.5 %collective-permute-start.11 = (bf16[128,1024]{1,0:T(8,128)(2,1)S(1)}, bf16[128,1024]{1,0:T(8,128)(2,1)}, u32[]{:S(2)}, u32[]{:S(2)}) collective-permute-start(bf16[128,1024]{1,0:T(8,128)(2,1)S(1)} %collective-permute-done.4.refs_5_), channel_id=1, source_target_pairs={{0,32},{16,496},{32,64},{48,16},{64,96},{80,48},{96,128},{112,80},... | collective-permute-start | bytes 786440 | tf_op jit(solution)/shard_map/ppermute | solution.py:238
  23.8 0.0 copy-done.1
  23.8 7.4 %collective-permute-start = (bf16[512,1024]{1,0:T(8,128)(2,1)S(1)}, bf16[512,1024]{1,0:T(8,128)(2,1)S(1)}, u32[]{:S(2)}, u32[]{:S(2)}) collective-permute-start(bf16[512,1024]{1,0:T(8,128)(2,1)S(1)} %copy-done.1), channel_id=1, source_target_pairs={{0,8},{8,0},{1,9},{9,1},{2,10},{10,2},{3,11},{11,3},{4,12},{12,4},... | collective-permute-start | bytes 3145736 | tf_op jit(solution)/shard_map/ppermute | solution.py:229
  31.2 0.0 collective-permute-done.1.refs_2_
  31.2 1.9 %collective-permute-start.5 = (bf16[128,1024]{1,0:T(8,128)(2,1)}, bf16[128,1024]{1,0:T(8,128)(2,1)S(1)}, u32[]{:S(2)}, u32[]{:S(2)}) collective-permute-start(bf16[128,1024]{1,0:T(8,128)(2,1)} %collective-permute-done.1.refs_2_), channel_id=1, source_target_pairs={{0,32},{16,496},{32,64},{48,16},{64,96},{80,48},{96,128},{112,80},... | collective-permute-start | bytes 786440 | tf_op jit(solution)/shard_map/ppermute | solution.py:238
  33.1 0.0 collective-permute-done.2.refs_3_
  33.1 3.2 %collective-permute-start.7 = (bf16[128,1024]{1,0:T(8,128)(2,1)}, bf16[128,1024]{1,0:T(8,128)(2,1)S(1)}, u32[]{:S(2)}, u32[]{:S(2)}) collective-permute-start(bf16[128,1024]{1,0:T(8,128)(2,1)} %collective-permute-done.2.refs_3_), channel_id=1, source_target_pairs={{0,32},{16,496},{32,64},{48,16},{64,96},{80,48},{96,128},{112,80},... | collective-permute-start | bytes 786440 | tf_op jit(solution)/shard_map/ppermute | solution.py:238
  36.4 0.0 collective-permute-done.9.refs_12_
  36.4 1.7 %broadcast_select_fusion.1 = bf16[128,1024]{1,0:T(8,128)(2,1)} fusion(bf16[128,1024]{1,0:T(8,128)(2,1)S(1)} %collective-permute-done.3.refs_4_, bf16[128,1024]{1,0:T(8,128)(2,1)} %collective-permute-done.9.refs_12_, pred[]{:T(512)S(6)} %eq.49), kind=kLoop, calls=%fused_computation.1 | loop fusion | flops 131072 | bytes 786433 | tf_op jit(solution)/shard_map/jit(_where)/select_n | solution.py:256
  38.1 0.0 copy-start.6
  38.1 2.0 %collective-permute-start.10 = (bf16[128,1024]{1,0:T(8,128)(2,1)}, bf16[128,1024]{1,0:T(8,128)(2,1)}, u32[]{:S(2)}, u32[]{:S(2)}) collective-permute-start(bf16[128,1024]{1,0:T(8,128)(2,1)} %broadcast_select_fusion.1), channel_id=1, source_target_pairs={{0,8},{8,0},{1,9},{9,1},{2,10},{10,2},{3,11},{11,3},{4,12},{12,4},... | collective-permute-start | bytes 786440 | tf_op jit(solution)/shard_map/ppermute | solution.py:229
  40.1 0.0 collective-permute-done.11.refs_13_
  40.1 1.7 %broadcast_select_fusion = bf16[128,1024]{1,0:T(8,128)(2,1)} fusion(bf16[128,1024]{1,0:T(8,128)(2,1)S(1)} %collective-permute-done.4.refs_5_, bf16[128,1024]{1,0:T(8,128)(2,1)} %collective-permute-done.11.refs_13_, pred[]{:T(512)S(6)} %eq.49), kind=kLoop, calls=%fused_computation | loop fusion | flops 131072 | bytes 786433 | tf_op jit(solution)/shard_map/jit(_where)/select_n | solution.py:256
  41.8 3.6 %collective-permute-start.12 = (bf16[128,1024]{1,0:T(8,128)(2,1)}, bf16[128,1024]{1,0:T(8,128)(2,1)}, u32[]{:S(2)}, u32[]{:S(2)}) collective-permute-start(bf16[128,1024]{1,0:T(8,128)(2,1)} %broadcast_select_fusion), channel_id=1, source_target_pairs={{0,8},{8,0},{1,9},{9,1},{2,10},{10,2},{3,11},{11,3},{4,12},{12,4},... | collective-permute-start | bytes 786440 | tf_op jit(solution)/shard_map/ppermute | solution.py:229
  45.4 0.0 collective-permute-done.5.refs_10_
  45.4 0.8 broadcast_select_fusion.3
  46.2 0.0 copy-start.2
  46.2 0.7 copy-done.2
  46.9 5.7 %collective-permute-start.6 = (bf16[128,1024]{1,0:T(8,128)(2,1)}, bf16[128,1024]{1,0:T(8,128)(2,1)}, u32[]{:S(2)}, u32[]{:S(2)}) collective-permute-start(bf16[128,1024]{1,0:T(8,128)(2,1)} %broadcast_select_fusion.3), channel_id=1, source_target_pairs={{0,8},{8,0},{1,9},{9,1},{2,10},{10,2},{3,11},{11,3},{4,12},{12,4},... | collective-permute-start | bytes 786440 | tf_op jit(solution)/shard_map/ppermute | solution.py:229
  52.6 0.0 collective-permute-done.7.refs_11_
  52.6 0.8 broadcast_select_fusion.2
  53.4 0.0 copy-start.4
  53.4 0.7 copy-done.4
  54.1 2.9 %collective-permute-start.8 = (bf16[128,1024]{1,0:T(8,128)(2,1)}, bf16[128,1024]{1,0:T(8,128)(2,1)}, u32[]{:S(2)}, u32[]{:S(2)}) collective-permute-start(bf16[128,1024]{1,0:T(8,128)(2,1)} %broadcast_select_fusion.2), channel_id=1, source_target_pairs={{0,8},{8,0},{1,9},{9,1},{2,10},{10,2},{3,11},{11,3},{4,12},{12,4},... | collective-permute-start | bytes 786440 | tf_op jit(solution)/shard_map/ppermute | solution.py:229
  56.9 0.0 copy-done.6
  57.0 0.1 copy.8
  57.1 0.0 collective-permute-done.10.refs_8_
  57.1 0.0 collective-permute-done.12.refs_9_
  57.1 0.0 collective-permute-done.6.refs_6_
  57.1 1.3 collective-permute-done.8.refs_7_
  58.4 0.0 collective-permute-done.refs_1_
  58.4 0.0 copy-start.3
  58.4 0.9 copy-done.3
  59.4 0.0 copy-start.5
  59.4 0.9 copy-done.5
  60.3 5.1 %gram_kernel.1 = bf16[8,592,128]{2,1,0:T(8,128)(2,1)} custom-call(s32[8,3]{1,0:T(8,128)S(1)} %get-tuple-element.24.source, s32[8,3]{1,0:T(8,128)S(1)} %get-tuple-element.23.column, bf16[512,1024]{1,0:T(8,128)(2,1)S(1)} %copy-done.1, bf16[512,1024]{1,0:T(8,128)(2,1)S(1)} %collective-permute-done.refs_1_, bf16[128,1024]{1,0:T(8,128)(2,1)} %collective-permute-done.1.refs_2_, ...), custom_call_target="tpu_custom_call" | custom-call | flops 805306368 | bytes 6291456 | tf_op jit(solution)/shard_map/gram_kernel/pallas_call | solution.py:107
  65.5 4.9 %all-to-all-start = ((bf16[8,592,128]{2,1,0:T(8,128)(2,1)}), bf16[8,592,128]{2,1,0:T(8,128)(2,1)S(1)}, u32[]{:S(2)}, u32[]{:S(2)}) async-start(bf16[8,592,128]{2,1,0:T(8,128)(2,1)} %gram_kernel.1), calls=%async_computation | async-start | bytes 2424832 | tf_op jit(solution)/shard_map/all_to_all | solution.py:259
  70.4 0.0 copy-done
  70.4 16.9 %all-to-all-done.parts = bf16[8,592,128]{2,1,0:T(8,128)(2,1)S(1)} async-done(((bf16[8,592,128]{2,1,0:T(8,128)(2,1)}), bf16[8,592,128]{2,1,0:T(8,128)(2,1)S(1)}, u32[]{:S(2)}, u32[]{:S(2)}) %all-to-all-start) | async-done | bytes 1212448 | tf_op jit(solution)/shard_map/all_to_all | solution.py:259
  87.3 0.6 first_kernel.1
  87.9 14.3 %all_to_all.49 = f32[16,1,128]{2,1,0:T(1,128)S(1)} all-to-all(f32[16,1,128]{2,1,0:T(1,128)S(1)} %bitcast.26), channel_id=1, replica_groups=mesh['z'=16,'xh'=2,'core'=2,'y'=4,'xl'=2] {'xh','y','xl'}, dimensions={0} | all-to-all | bytes 16384 | tf_op jit(solution)/shard_map/all_to_all | solution.py:223
  102.2 20.6 %all_to_all.50 = f32[32,1,128]{2,1,0:T(1,128)S(1)} all-to-all(f32[32,1,128]{2,1,0:T(1,128)S(1)} %bitcast.21), channel_id=1, replica_groups=mesh['z'=16,'xh'=2,'core'=2,'y'=4,'xl'=2] {'z','core'}, dimensions={0} | all-to-all | bytes 32768 | tf_op jit(solution)/shard_map/all_to_all | solution.py:225
  122.8 0.5 second_kernel.1
  123.2 9.1 %all_to_all.51 = f32[16,1,128]{2,1,0:T(1,128)S(1)} all-to-all(f32[16,1,128]{2,1,0:T(1,128)S(1)} %bitcast.25), channel_id=1, replica_groups=mesh['z'=16,'xh'=2,'core'=2,'y'=4,'xl'=2] {'xh','y','xl'}, dimensions={0} | all-to-all | bytes 16384 | tf_op jit(solution)/shard_map/all_to_all | solution.py:223
  132.3 16.8 %all_to_all.52 = f32[32,1,128]{2,1,0:T(1,128)S(1)} all-to-all(f32[32,1,128]{2,1,0:T(1,128)S(1)} %bitcast.22), channel_id=1, replica_groups=mesh['z'=16,'xh'=2,'core'=2,'y'=4,'xl'=2] {'z','core'}, dimensions={0} | all-to-all | bytes 32768 | tf_op jit(solution)/shard_map/all_to_all | solution.py:225
  149.2 0.9 last_kernel.1
  (4 shorter events, 0.1 us)
Async XLA Ops:
  0.0 70.4 %copy-start = (bf16[8,3,128,128]{3,2,1,0:T(8,128)(2,1)S(1)}, bf16[8,3,128,128]{3,2,1,0:T(8,128)(2,1)}, u32[]{:S(2)}) copy-start(bf16[8,3,128,128]{3,2,1,0:T(8,128)(2,1)} %param.5) | copy-start | bytes 2359300
  0.0 23.8 %copy-start.1 = (bf16[512,1024]{1,0:T(8,128)(2,1)S(1)}, bf16[512,1024]{1,0:T(8,128)(2,1)}, u32[]{:S(2)}) copy-start(bf16[512,1024]{1,0:T(8,128)(2,1)} %refs_0_.1) | copy-start | bytes 3145732
  2.2 14.2 %collective-permute-start.3 = (bf16[128,1024]{1,0:T(8,128)(2,1)S(1)}, bf16[128,1024]{1,0:T(8,128)(2,1)S(1)}, u32[]{:S(2)}, u32[]{:S(2)}) collective-permute-start(bf16[128,1024]{1,0:T(8,128)(2,1)S(1)} %get-tuple-element.20), channel_id=1, source_target_pairs={{0,16},{16,0},{1,17},{17,1},{2,18},{18,2},{3,19},{19,3},{4,20},{20... | collective-permute-start | bytes 786440 | tf_op jit(solution)/shard_map/ppermute | solution.py:229
  7.7 12.5 %collective-permute-start.4 = (bf16[128,1024]{1,0:T(8,128)(2,1)S(1)}, bf16[128,1024]{1,0:T(8,128)(2,1)S(1)}, u32[]{:S(2)}, u32[]{:S(2)}) collective-permute-start(bf16[128,1024]{1,0:T(8,128)(2,1)S(1)} %get-tuple-element.19), channel_id=1, source_target_pairs={{0,16},{16,0},{1,17},{17,1},{2,18},{18,2},{3,19},{19,3},{4,20},{20... | collective-permute-start | bytes 786440 | tf_op jit(solution)/shard_map/ppermute | solution.py:229
  9.6 21.6 %collective-permute-start.1 = (bf16[128,1024]{1,0:T(8,128)(2,1)}, bf16[128,1024]{1,0:T(8,128)(2,1)}, u32[]{:S(2)}, u32[]{:S(2)}) collective-permute-start(bf16[128,1024]{1,0:T(8,128)(2,1)} %get-tuple-element.22), channel_id=1, source_target_pairs={{0,16},{16,0},{1,17},{17,1},{2,18},{18,2},{3,19},{19,3},{4,20},{20... | collective-permute-start | bytes 786440 | tf_op jit(solution)/shard_map/ppermute | solution.py:229
  14.5 18.6 %collective-permute-start.2 = (bf16[128,1024]{1,0:T(8,128)(2,1)}, bf16[128,1024]{1,0:T(8,128)(2,1)}, u32[]{:S(2)}, u32[]{:S(2)}) collective-permute-start(bf16[128,1024]{1,0:T(8,128)(2,1)} %get-tuple-element.21), channel_id=1, source_target_pairs={{0,16},{16,0},{1,17},{17,1},{2,18},{18,2},{3,19},{19,3},{4,20},{20... | collective-permute-start | bytes 786440 | tf_op jit(solution)/shard_map/ppermute | solution.py:229
  16.4 20.0 %collective-permute-start.9 = (bf16[128,1024]{1,0:T(8,128)(2,1)S(1)}, bf16[128,1024]{1,0:T(8,128)(2,1)}, u32[]{:S(2)}, u32[]{:S(2)}) collective-permute-start(bf16[128,1024]{1,0:T(8,128)(2,1)S(1)} %collective-permute-done.3.refs_4_), channel_id=1, source_target_pairs={{0,32},{16,496},{32,64},{48,16},{64,96},{80,48},{96,128},{112,80},... | collective-permute-start | bytes 786440 | tf_op jit(solution)/shard_map/ppermute | solution.py:238
  20.2 19.9 %collective-permute-start.11 = (bf16[128,1024]{1,0:T(8,128)(2,1)S(1)}, bf16[128,1024]{1,0:T(8,128)(2,1)}, u32[]{:S(2)}, u32[]{:S(2)}) collective-permute-start(bf16[128,1024]{1,0:T(8,128)(2,1)S(1)} %collective-permute-done.4.refs_5_), channel_id=1, source_target_pairs={{0,32},{16,496},{32,64},{48,16},{64,96},{80,48},{96,128},{112,80},... | collective-permute-start | bytes 786440 | tf_op jit(solution)/shard_map/ppermute | solution.py:238
  23.8 34.6 %collective-permute-start = (bf16[512,1024]{1,0:T(8,128)(2,1)S(1)}, bf16[512,1024]{1,0:T(8,128)(2,1)S(1)}, u32[]{:S(2)}, u32[]{:S(2)}) collective-permute-start(bf16[512,1024]{1,0:T(8,128)(2,1)S(1)} %copy-done.1), channel_id=1, source_target_pairs={{0,8},{8,0},{1,9},{9,1},{2,10},{10,2},{3,11},{11,3},{4,12},{12,4},... | collective-permute-start | bytes 3145736 | tf_op jit(solution)/shard_map/ppermute | solution.py:229
  31.2 14.2 %collective-permute-start.5 = (bf16[128,1024]{1,0:T(8,128)(2,1)}, bf16[128,1024]{1,0:T(8,128)(2,1)S(1)}, u32[]{:S(2)}, u32[]{:S(2)}) collective-permute-start(bf16[128,1024]{1,0:T(8,128)(2,1)} %collective-permute-done.1.refs_2_), channel_id=1, source_target_pairs={{0,32},{16,496},{32,64},{48,16},{64,96},{80,48},{96,128},{112,80},... | collective-permute-start | bytes 786440 | tf_op jit(solution)/shard_map/ppermute | solution.py:238
  33.1 19.5 %collective-permute-start.7 = (bf16[128,1024]{1,0:T(8,128)(2,1)}, bf16[128,1024]{1,0:T(8,128)(2,1)S(1)}, u32[]{:S(2)}, u32[]{:S(2)}) collective-permute-start(bf16[128,1024]{1,0:T(8,128)(2,1)} %collective-permute-done.2.refs_3_), channel_id=1, source_target_pairs={{0,32},{16,496},{32,64},{48,16},{64,96},{80,48},{96,128},{112,80},... | collective-permute-start | bytes 786440 | tf_op jit(solution)/shard_map/ppermute | solution.py:238
  38.1 18.9 %copy-start.6 = (s32[8,3]{0,1:T(4,128)S(1)}, s32[8,3]{0,1:T(4,128)}, u32[]{:S(2)}) copy-start(s32[8,3]{0,1:T(4,128)} %param.4) | copy-start | bytes 292
  38.1 19.0 %collective-permute-start.10 = (bf16[128,1024]{1,0:T(8,128)(2,1)}, bf16[128,1024]{1,0:T(8,128)(2,1)}, u32[]{:S(2)}, u32[]{:S(2)}) collective-permute-start(bf16[128,1024]{1,0:T(8,128)(2,1)} %broadcast_select_fusion.1), channel_id=1, source_target_pairs={{0,8},{8,0},{1,9},{9,1},{2,10},{10,2},{3,11},{11,3},{4,12},{12,4},... | collective-permute-start | bytes 786440 | tf_op jit(solution)/shard_map/ppermute | solution.py:229
  41.8 15.2 %collective-permute-start.12 = (bf16[128,1024]{1,0:T(8,128)(2,1)}, bf16[128,1024]{1,0:T(8,128)(2,1)}, u32[]{:S(2)}, u32[]{:S(2)}) collective-permute-start(bf16[128,1024]{1,0:T(8,128)(2,1)} %broadcast_select_fusion), channel_id=1, source_target_pairs={{0,8},{8,0},{1,9},{9,1},{2,10},{10,2},{3,11},{11,3},{4,12},{12,4},... | collective-permute-start | bytes 786440 | tf_op jit(solution)/shard_map/ppermute | solution.py:229
  46.2 0.7 copy-start.2
  46.9 10.2 %collective-permute-start.6 = (bf16[128,1024]{1,0:T(8,128)(2,1)}, bf16[128,1024]{1,0:T(8,128)(2,1)}, u32[]{:S(2)}, u32[]{:S(2)}) collective-permute-start(bf16[128,1024]{1,0:T(8,128)(2,1)} %broadcast_select_fusion.3), channel_id=1, source_target_pairs={{0,8},{8,0},{1,9},{9,1},{2,10},{10,2},{3,11},{11,3},{4,12},{12,4},... | collective-permute-start | bytes 786440 | tf_op jit(solution)/shard_map/ppermute | solution.py:229
  53.4 0.7 copy-start.4
  54.1 4.3 %collective-permute-start.8 = (bf16[128,1024]{1,0:T(8,128)(2,1)}, bf16[128,1024]{1,0:T(8,128)(2,1)}, u32[]{:S(2)}, u32[]{:S(2)}) collective-permute-start(bf16[128,1024]{1,0:T(8,128)(2,1)} %broadcast_select_fusion.2), channel_id=1, source_target_pairs={{0,8},{8,0},{1,9},{9,1},{2,10},{10,2},{3,11},{11,3},{4,12},{12,4},... | collective-permute-start | bytes 786440 | tf_op jit(solution)/shard_map/ppermute | solution.py:229
  58.4 1.0 copy-start.3
  59.4 0.9 copy-start.5
  65.5 21.9 %all-to-all-start = ((bf16[8,592,128]{2,1,0:T(8,128)(2,1)}), bf16[8,592,128]{2,1,0:T(8,128)(2,1)S(1)}, u32[]{:S(2)}, u32[]{:S(2)}) async-start(bf16[8,592,128]{2,1,0:T(8,128)(2,1)} %gram_kernel.1), calls=%async_computation | async-start | bytes 2424832 | tf_op jit(solution)/shard_map/all_to_all | solution.py:259

commit v4 on v3

--- a/solution.py
+++ b/solution.py
@@ -13,7 +13,7 @@
 SIZES = (16, 2, 2, 4, 2)
 VAR_AXES = ("z", "xh", "core")
 SAMP_AXES = ("y", "xl")
-SIZES_OF_CHUNKS = (128, 128, 128, 128)
+SIZES_OF_CHUNKS = (176, 176, 160)
 CHUNKS = len(SIZES_OF_CHUNKS)
 ROWB = 8
 K = 3
@@ -39,22 +39,23 @@
     return pltpu.CompilerParams(vmem_limit_bytes=16 * 1024 * 1024)
 
 
-def fetch(inputs, held, sems):
-    copies = [pltpu.make_async_copy(inputs[i], held.at[i], sems.at[i]) for i in range(2)]
-    for i in range(3 * CHUNKS):
-        slot, chunk = 2 + i // CHUNKS, i % CHUNKS
-        rows = pl.ds(sum(SIZES_OF_CHUNKS[:chunk]), SIZES_OF_CHUNKS[chunk])
-        copies.append(pltpu.make_async_copy(inputs[2 + i], held.at[slot, rows], sems.at[2 + i]))
-    for copy in copies:
-        copy.start()
-    for copy in copies:
-        copy.wait()
-
-
-def columns_of(held, source, column, r):
-    return [
-        held[source[r, k], :, pl.ds(pl.multiple_of(column[r, k] * BLK, BLK), BLK)] for k in range(K)
-    ]
+def choose(inputs, held, source, column):
+    def one(n, carry):
+        r, k = n // (K - 1), n % (K - 1) + 1
+        at = pl.ds(pl.multiple_of(column[r, k] * BLK, BLK), BLK)
+        for slot in range(1, 5):
+
+            @pl.when(source[r, k] == slot)
+            def _():
+                start = 0
+                for strip in inputs[slot]:
+                    rows = strip.shape[0]
+                    held[n, pl.ds(start, rows), :] = strip[:, at]
+                    start += rows
+
+        return carry
+
+    lax.fori_loop(0, ROWB * (K - 1), one, 0)
 
 
 def dot(left, right, left_dim, right_dim):
@@ -70,13 +71,15 @@
 
 
 def gram_kernel(source, column, *refs):
-    *inputs, out, held, sems = refs
-    fetch(inputs, held, sems)
+    *strips, out, held = refs
+    inputs = [strips[:1], strips[1:2]]
+    inputs += [strips[2 + CHUNKS * i : 2 + CHUNKS * (i + 1)] for i in range(3)]
+    choose(inputs, held, source, column)
     row, col = diagonal_mask()
     line = lax.broadcasted_iota(jnp.int32, (16, BLK), 0)
 
-    def one(r, carry):
-        cols = columns_of(held, source, column, r)
+    for r in range(ROWB):
+        cols = [strips[0][:, r * BLK : (r + 1) * BLK], held[2 * r], held[2 * r + 1]]
         scaled = [
             dot(cols[i], jnp.concatenate(cols[i:], axis=1), 0, 0) * (1.0 / SAMPLES) for i in range(K)
         ]
@@ -95,9 +98,6 @@
             lines = jnp.where(line == 2 * k, high, lines)
             lines = jnp.where(line == 2 * k + 1, diag - high, lines)
         out[r, pl.ds(DIAGS, 16), :] = lines.astype(BF16)
-        return carry
-
-    lax.fori_loop(0, ROWB, one, 0, unroll=True)
 
 
 def on_strips(kernel, shape, specs, *args):
@@ -107,12 +107,9 @@
     return pl.pallas_call(
         kernel,
         out_shape=jax.ShapeDtypeStruct(shape, BF16),
-        in_specs=specs + [ANY] * len(arrays),
+        in_specs=specs + [VMEM] * len(arrays),
         out_specs=VMEM,
-        scratch_shapes=[
-            pltpu.VMEM((5, samples, columns), BF16),
-            pltpu.SemaphoreType.DMA((len(arrays),)),
-        ],
+        scratch_shapes=[pltpu.VMEM((ROWB * (K - 1), samples, BLK), BF16)],
         compiler_params=params(),
         cost_estimate=pl.CostEstimate(flops=flops, bytes_accessed=12 * samples * columns, transcendentals=0),
         name=kernel.__name__,

time: 151 us -> 145 us (0.960)
  waiting for transfers between devices: 18.3 us -> 23.2 us
  blocking collectives: 60.8 us -> 56.8 us
  other arithmetic: 4.91 us -> 2.38 us
  starting transfers between devices: 53.1 us -> 50.8 us
  local copies, waits for them, and re-layouts: 5.6 us -> 3.83 us
    all_to_all x2, blocking collectives: 23.4 us -> 18.9 us  [everywhere(): rows = lax.all_to_all(rows, ('xh', 'y', 'xl'), 0, 0, tiled=True)]
    ppermute x9 -> x7, waiting for transfers between devices: 1.34 us -> 4.32 us  [swap(): return lax.ppermute(block, axis, [(0, 1), (1, 0)])]
    select_n x4 -> x3, other arithmetic: 4.89 us -> 2.36 us  [body(): jnp.where(core == xh, a, b)]
    ppermute x4 -> x3, waiting for transfers between devices: 0.01 us -> 1.95 us  [along_z(): return lax.ppermute(block, ('z', 'xh'), route)]
    ppermute x4 -> x3, starting transfers between devices: 12.5 us -> 10.6 us  [along_z(): return lax.ppermute(block, ('z', 'xh'), route)]
    unnamed x15 -> x11, local copies, waits for them, and re-layouts: 3.4 us -> 1.8 us
    ppermute x9 -> x7, starting transfers between devices: 35.7 us -> 36 us  [swap(): return lax.ppermute(block, axis, [(0, 1), (1, 0)])]
  transfers between devices with their start and end apart: 14 -> 11, of which waited for: 2 -> 4; matrix products, arithmetic and copies ran while one was open for 3% -> 2% of each run, Pallas kernels for 0% -> 0%
where the time goes in v4:
time: 145 us; the launch traced here: 144 us
  blocking collectives  56.8 us (39%)
  starting transfers between devices  50.8 us (35%)
  waiting for transfers between devices  23.2 us (16%)
  Pallas kernels  7.24 us (5%)
  local copies, waits for them, and re-layouts  3.83 us (3%)
  other arithmetic  2.38 us (2%)
    all_to_all x2, blocking collectives, everywhere(): return lax.all_to_all(rows, ('z', 'core'), 0, 0, tiled=True)  37.9 us
    ppermute x7, starting transfers between devices, swap(): return lax.ppermute(block, axis, [(0, 1), (1, 0)])  36 us
    all_to_all x2, blocking collectives, everywhere(): rows = lax.all_to_all(rows, ('xh', 'y', 'xl'), 0, 0, tiled=True)  18.9 us
    all_to_all x1, waiting for transfers between devices, body(): parts = lax.all_to_all(grams, SAMP_AXES, 0, 0, tiled=True)  16.9 us
    ppermute x3, starting transfers between devices, along_z(): return lax.ppermute(block, ('z', 'xh'), route)  10.6 us
    pallas_call x1, Pallas kernels, on_strips(): pl.pallas_call(kernel, out_shape=jax.ShapeDtypeStruct(shape, BF16), in_sp...  5.34 us
    ppermute x7, waiting for transfers between devices, swap(): return lax.ppermute(block, axis, [(0, 1), (1, 0)])  4.32 us
    all_to_all x1, starting transfers between devices, body(): parts = lax.all_to_all(grams, SAMP_AXES, 0, 0, tiled=True)  4.22 us
  transfers between devices with their start and end apart: 11, of which 4 were waited for; matrix products, arithmetic and copies ran while one was open for 2% of the time, Pallas kernels for 0%

profile of v4, /device:TPU:1, one launch (start us, length us, event | category | flops | bytes accessed | tf_op | source)
XLA Modules:
  0.0 144.5 jit_solution(17497151643443788290)
XLA Ops:
  0.0 0.0 copy-start
  0.0 0.0 copy-start.1
  0.0 1.3 fusion.6
  1.3 5.5 %collective-permute-start.1 = (bf16[176,1024]{1,0:T(8,128)(2,1)S(1)}, bf16[176,1024]{1,0:T(8,128)(2,1)S(1)}, u32[]{:S(2)}, u32[]{:S(2)}) collective-permute-start(bf16[176,1024]{1,0:T(8,128)(2,1)S(1)} %get-tuple-element.20), channel_id=1, source_target_pairs={{0,16},{16,0},{1,17},{17,1},{2,18},{18,2},{3,19},{19,3},{4,20},{20... | collective-permute-start | bytes 1081352 | tf_op jit(solution)/shard_map/ppermute | solution.py:226
  6.8 1.9 %collective-permute-start.2 = (bf16[176,1024]{1,0:T(8,128)(2,1)S(1)}, bf16[176,1024]{1,0:T(8,128)(2,1)S(1)}, u32[]{:S(2)}, u32[]{:S(2)}) collective-permute-start(bf16[176,1024]{1,0:T(8,128)(2,1)S(1)} %get-tuple-element.19), channel_id=1, source_target_pairs={{0,16},{16,0},{1,17},{17,1},{2,18},{18,2},{3,19},{19,3},{4,20},{20... | collective-permute-start | bytes 1081352 | tf_op jit(solution)/shard_map/ppermute | solution.py:226
  8.7 2.9 %collective-permute-done.1.refs_2_ = bf16[176,1024]{1,0:T(8,128)(2,1)S(1)} collective-permute-done((bf16[176,1024]{1,0:T(8,128)(2,1)S(1)}, bf16[176,1024]{1,0:T(8,128)(2,1)S(1)}, u32[]{:S(2)}, u32[]{:S(2)}) %collective-permute-start.1) | collective-permute-done | bytes 360480 | tf_op jit(solution)/shard_map/ppermute | solution.py:226
  11.6 6.8 %collective-permute-start.4 = (bf16[176,1024]{1,0:T(8,128)(2,1)S(1)}, bf16[176,1024]{1,0:T(8,128)(2,1)S(1)}, u32[]{:S(2)}, u32[]{:S(2)}) collective-permute-start(bf16[176,1024]{1,0:T(8,128)(2,1)S(1)} %collective-permute-done.1.refs_2_), channel_id=1, source_target_pairs={{0,32},{16,496},{32,64},{48,16},{64,96},{80,48},{96,128},{112,80},... | collective-permute-start | bytes 1081352 | tf_op jit(solution)/shard_map/ppermute | solution.py:235
  18.3 0.0 copy-done.1
  18.3 0.8 slice.11
  19.1 12.2 %collective-permute-start.3 = (bf16[160,1024]{1,0:T(8,128)(2,1)}, bf16[160,1024]{1,0:T(8,128)(2,1)}, u32[]{:S(2)}, u32[]{:S(2)}) collective-permute-start(bf16[160,1024]{1,0:T(8,128)(2,1)} %slice.11), channel_id=1, source_target_pairs={{0,16},{16,0},{1,17},{17,1},{2,18},{18,2},{3,19},{19,3},{4,20},{20... | collective-permute-start | bytes 983048 | tf_op jit(solution)/shard_map/ppermute | solution.py:226
  31.3 0.0 collective-permute-done.2.refs_3_
  31.3 1.9 %collective-permute-start.6 = (bf16[176,1024]{1,0:T(8,128)(2,1)S(1)}, bf16[176,1024]{1,0:T(8,128)(2,1)S(1)}, u32[]{:S(2)}, u32[]{:S(2)}) collective-permute-start(bf16[176,1024]{1,0:T(8,128)(2,1)S(1)} %collective-permute-done.2.refs_3_), channel_id=1, source_target_pairs={{0,32},{16,496},{32,64},{48,16},{64,96},{80,48},{96,128},{112,80},... | collective-permute-start | bytes 1081352 | tf_op jit(solution)/shard_map/ppermute | solution.py:235
  33.3 5.2 %collective-permute-start = (bf16[512,1024]{1,0:T(8,128)(2,1)S(1)}, bf16[512,1024]{1,0:T(8,128)(2,1)}, u32[]{:S(2)}, u32[]{:S(2)}) collective-permute-start(bf16[512,1024]{1,0:T(8,128)(2,1)S(1)} %copy-done.1), channel_id=1, source_target_pairs={{0,8},{8,0},{1,9},{9,1},{2,10},{10,2},{3,11},{11,3},{4,12},{12,4},... | collective-permute-start | bytes 3145736 | tf_op jit(solution)/shard_map/ppermute | solution.py:226
  38.4 0.0 collective-permute-done.3.refs_4_
  38.4 1.9 %collective-permute-start.8 = (bf16[160,1024]{1,0:T(8,128)(2,1)}, bf16[160,1024]{1,0:T(8,128)(2,1)S(1)}, u32[]{:S(2)}, u32[]{:S(2)}) collective-permute-start(bf16[160,1024]{1,0:T(8,128)(2,1)} %collective-permute-done.3.refs_4_), channel_id=1, source_target_pairs={{0,32},{16,496},{32,64},{48,16},{64,96},{80,48},{96,128},{112,80},... | collective-permute-start | bytes 983048 | tf_op jit(solution)/shard_map/ppermute | solution.py:235
  40.4 0.0 collective-permute-done.4.refs_8_
  40.4 0.8 broadcast_select_fusion.1
  41.2 0.0 copy-start.4
  41.2 3.9 %collective-permute-start.5 = (bf16[176,1024]{1,0:T(8,128)(2,1)}, bf16[176,1024]{1,0:T(8,128)(2,1)}, u32[]{:S(2)}, u32[]{:S(2)}) collective-permute-start(bf16[176,1024]{1,0:T(8,128)(2,1)} %broadcast_select_fusion.1), channel_id=1, source_target_pairs={{0,8},{8,0},{1,9},{9,1},{2,10},{10,2},{3,11},{11,3},{4,12},{12,4},... | collective-permute-start | bytes 1081352 | tf_op jit(solution)/shard_map/ppermute | solution.py:226
  45.0 0.0 collective-permute-done.6.refs_9_
  45.0 0.8 broadcast_select_fusion
  45.8 2.2 %collective-permute-start.7 = (bf16[176,1024]{1,0:T(8,128)(2,1)}, bf16[176,1024]{1,0:T(8,128)(2,1)}, u32[]{:S(2)}, u32[]{:S(2)}) collective-permute-start(bf16[176,1024]{1,0:T(8,128)(2,1)} %broadcast_select_fusion), channel_id=1, source_target_pairs={{0,8},{8,0},{1,9},{9,1},{2,10},{10,2},{3,11},{11,3},{4,12},{12,4},... | collective-permute-start | bytes 1081352 | tf_op jit(solution)/shard_map/ppermute | solution.py:226
  48.0 1.9 %collective-permute-done.8.refs_10_ = bf16[160,1024]{1,0:T(8,128)(2,1)S(1)} collective-permute-done((bf16[160,1024]{1,0:T(8,128)(2,1)}, bf16[160,1024]{1,0:T(8,128)(2,1)S(1)}, u32[]{:S(2)}, u32[]{:S(2)}) %collective-permute-start.8) | collective-permute-done | bytes 327712 | tf_op jit(solution)/shard_map/ppermute | solution.py:235
  49.9 0.8 broadcast_select_fusion.2
  50.7 0.0 copy-start.2
  50.7 0.7 copy-done.2
  51.5 5.2 %collective-permute-start.9 = (bf16[160,1024]{1,0:T(8,128)(2,1)}, bf16[160,1024]{1,0:T(8,128)(2,1)}, u32[]{:S(2)}, u32[]{:S(2)}) collective-permute-start(bf16[160,1024]{1,0:T(8,128)(2,1)} %broadcast_select_fusion.2), channel_id=1, source_target_pairs={{0,8},{8,0},{1,9},{9,1},{2,10},{10,2},{3,11},{11,3},{4,12},{12,4},... | collective-permute-start | bytes 983048 | tf_op jit(solution)/shard_map/ppermute | solution.py:226
  56.7 0.0 copy-done.4
  56.7 0.1 copy.8
  56.8 1.4 collective-permute-done.9.refs_7_
  58.3 0.0 collective-permute-done.refs_1_
  58.3 0.0 collective-permute-done.5.refs_5_
  58.3 0.0 collective-permute-done.7.refs_6_
  58.3 0.0 copy-start.3
  58.3 1.0 copy-done.3
  59.3 5.3 %gram_kernel.1 = bf16[8,592,128]{2,1,0:T(8,128)(2,1)} custom-call(s32[8,3]{1,0:T(8,128)S(1)} %get-tuple-element.22.source, s32[8,3]{1,0:T(8,128)S(1)} %get-tuple-element.21.column, bf16[512,1024]{1,0:T(8,128)(2,1)S(1)} %copy-done.1, bf16[512,1024]{1,0:T(8,128)(2,1)} %collective-permute-done.refs_1_, bf16[176,1024]{1,0:T(8,128)(2,1)S(1)} %collective-permute-done.1.refs_2_, ...), custom_call_target="tpu_custom_call" | custom-call | flops 805306368 | bytes 6291456 | tf_op jit(solution)/shard_map/gram_kernel/pallas_call | solution.py:107
  64.6 4.2 %all-to-all-start = ((bf16[8,592,128]{2,1,0:T(8,128)(2,1)}), bf16[8,592,128]{2,1,0:T(8,128)(2,1)S(1)}, u32[]{:S(2)}, u32[]{:S(2)}) async-start(bf16[8,592,128]{2,1,0:T(8,128)(2,1)} %gram_kernel.1), calls=%async_computation | async-start | bytes 2424832 | tf_op jit(solution)/shard_map/all_to_all | solution.py:256
  68.8 0.0 copy-done
  68.8 16.9 %all-to-all-done.parts = bf16[8,592,128]{2,1,0:T(8,128)(2,1)S(1)} async-done(((bf16[8,592,128]{2,1,0:T(8,128)(2,1)}), bf16[8,592,128]{2,1,0:T(8,128)(2,1)S(1)}, u32[]{:S(2)}, u32[]{:S(2)}) %all-to-all-start) | async-done | bytes 1212448 | tf_op jit(solution)/shard_map/all_to_all | solution.py:256
  85.7 0.6 first_kernel.1
  86.3 9.7 %all_to_all.49 = f32[16,1,128]{2,1,0:T(1,128)S(1)} all-to-all(f32[16,1,128]{2,1,0:T(1,128)S(1)} %bitcast.26), channel_id=1, replica_groups=mesh['z'=16,'xh'=2,'core'=2,'y'=4,'xl'=2] {'xh','y','xl'}, dimensions={0} | all-to-all | bytes 16384 | tf_op jit(solution)/shard_map/all_to_all | solution.py:220
  96.1 21.1 %all_to_all.50 = f32[32,1,128]{2,1,0:T(1,128)S(1)} all-to-all(f32[32,1,128]{2,1,0:T(1,128)S(1)} %bitcast.21), channel_id=1, replica_groups=mesh['z'=16,'xh'=2,'core'=2,'y'=4,'xl'=2] {'z','core'}, dimensions={0} | all-to-all | bytes 32768 | tf_op jit(solution)/shard_map/all_to_all | solution.py:222
  117.2 0.5 second_kernel.1
  117.6 9.1 %all_to_all.51 = f32[16,1,128]{2,1,0:T(1,128)S(1)} all-to-all(f32[16,1,128]{2,1,0:T(1,128)S(1)} %bitcast.25), channel_id=1, replica_groups=mesh['z'=16,'xh'=2,'core'=2,'y'=4,'xl'=2] {'xh','y','xl'}, dimensions={0} | all-to-all | bytes 16384 | tf_op jit(solution)/shard_map/all_to_all | solution.py:220
  126.8 16.8 %all_to_all.52 = f32[32,1,128]{2,1,0:T(1,128)S(1)} all-to-all(f32[32,1,128]{2,1,0:T(1,128)S(1)} %bitcast.22), channel_id=1, replica_groups=mesh['z'=16,'xh'=2,'core'=2,'y'=4,'xl'=2] {'z','core'}, dimensions={0} | all-to-all | bytes 32768 | tf_op jit(solution)/shard_map/all_to_all | solution.py:222
  143.6 0.9 last_kernel.1
  (4 shorter events, 0.1 us)
Async XLA Ops:
  0.0 68.8 %copy-start = (bf16[8,3,128,128]{3,2,1,0:T(8,128)(2,1)S(1)}, bf16[8,3,128,128]{3,2,1,0:T(8,128)(2,1)}, u32[]{:S(2)}) copy-start(bf16[8,3,128,128]{3,2,1,0:T(8,128)(2,1)} %param.5) | copy-start | bytes 2359300
  0.0 18.3 %copy-start.1 = (bf16[512,1024]{1,0:T(8,128)(2,1)S(1)}, bf16[512,1024]{1,0:T(8,128)(2,1)}, u32[]{:S(2)}) copy-start(bf16[512,1024]{1,0:T(8,128)(2,1)} %refs_0_.1) | copy-start | bytes 3145732
  1.3 10.3 %collective-permute-start.1 = (bf16[176,1024]{1,0:T(8,128)(2,1)S(1)}, bf16[176,1024]{1,0:T(8,128)(2,1)S(1)}, u32[]{:S(2)}, u32[]{:S(2)}) collective-permute-start(bf16[176,1024]{1,0:T(8,128)(2,1)S(1)} %get-tuple-element.20), channel_id=1, source_target_pairs={{0,16},{16,0},{1,17},{17,1},{2,18},{18,2},{3,19},{19,3},{4,20},{20... | collective-permute-start | bytes 1081352 | tf_op jit(solution)/shard_map/ppermute | solution.py:226
  6.8 24.6 %collective-permute-start.2 = (bf16[176,1024]{1,0:T(8,128)(2,1)S(1)}, bf16[176,1024]{1,0:T(8,128)(2,1)S(1)}, u32[]{:S(2)}, u32[]{:S(2)}) collective-permute-start(bf16[176,1024]{1,0:T(8,128)(2,1)S(1)} %get-tuple-element.19), channel_id=1, source_target_pairs={{0,16},{16,0},{1,17},{17,1},{2,18},{18,2},{3,19},{19,3},{4,20},{20... | collective-permute-start | bytes 1081352 | tf_op jit(solution)/shard_map/ppermute | solution.py:226
  11.6 28.8 %collective-permute-start.4 = (bf16[176,1024]{1,0:T(8,128)(2,1)S(1)}, bf16[176,1024]{1,0:T(8,128)(2,1)S(1)}, u32[]{:S(2)}, u32[]{:S(2)}) collective-permute-start(bf16[176,1024]{1,0:T(8,128)(2,1)S(1)} %collective-permute-done.1.refs_2_), channel_id=1, source_target_pairs={{0,32},{16,496},{32,64},{48,16},{64,96},{80,48},{96,128},{112,80},... | collective-permute-start | bytes 1081352 | tf_op jit(solution)/shard_map/ppermute | solution.py:235
  19.1 19.3 %collective-permute-start.3 = (bf16[160,1024]{1,0:T(8,128)(2,1)}, bf16[160,1024]{1,0:T(8,128)(2,1)}, u32[]{:S(2)}, u32[]{:S(2)}) collective-permute-start(bf16[160,1024]{1,0:T(8,128)(2,1)} %slice.11), channel_id=1, source_target_pairs={{0,16},{16,0},{1,17},{17,1},{2,18},{18,2},{3,19},{19,3},{4,20},{20... | collective-permute-start | bytes 983048 | tf_op jit(solution)/shard_map/ppermute | solution.py:226
  31.3 13.7 %collective-permute-start.6 = (bf16[176,1024]{1,0:T(8,128)(2,1)S(1)}, bf16[176,1024]{1,0:T(8,128)(2,1)S(1)}, u32[]{:S(2)}, u32[]{:S(2)}) collective-permute-start(bf16[176,1024]{1,0:T(8,128)(2,1)S(1)} %collective-permute-done.2.refs_3_), channel_id=1, source_target_pairs={{0,32},{16,496},{32,64},{48,16},{64,96},{80,48},{96,128},{112,80},... | collective-permute-start | bytes 1081352 | tf_op jit(solution)/shard_map/ppermute | solution.py:235
  33.3 25.0 %collective-permute-start = (bf16[512,1024]{1,0:T(8,128)(2,1)S(1)}, bf16[512,1024]{1,0:T(8,128)(2,1)}, u32[]{:S(2)}, u32[]{:S(2)}) collective-permute-start(bf16[512,1024]{1,0:T(8,128)(2,1)S(1)} %copy-done.1), channel_id=1, source_target_pairs={{0,8},{8,0},{1,9},{9,1},{2,10},{10,2},{3,11},{11,3},{4,12},{12,4},... | collective-permute-start | bytes 3145736 | tf_op jit(solution)/shard_map/ppermute | solution.py:226
  38.4 11.5 %collective-permute-start.8 = (bf16[160,1024]{1,0:T(8,128)(2,1)}, bf16[160,1024]{1,0:T(8,128)(2,1)S(1)}, u32[]{:S(2)}, u32[]{:S(2)}) collective-permute-start(bf16[160,1024]{1,0:T(8,128)(2,1)} %collective-permute-done.3.refs_4_), channel_id=1, source_target_pairs={{0,32},{16,496},{32,64},{48,16},{64,96},{80,48},{96,128},{112,80},... | collective-permute-start | bytes 983048 | tf_op jit(solution)/shard_map/ppermute | solution.py:235
  41.2 15.5 %copy-start.4 = (s32[8,3]{0,1:T(4,128)S(1)}, s32[8,3]{0,1:T(4,128)}, u32[]{:S(2)}) copy-start(s32[8,3]{0,1:T(4,128)} %param.4) | copy-start | bytes 292
  41.2 17.1 %collective-permute-start.5 = (bf16[176,1024]{1,0:T(8,128)(2,1)}, bf16[176,1024]{1,0:T(8,128)(2,1)}, u32[]{:S(2)}, u32[]{:S(2)}) collective-permute-start(bf16[176,1024]{1,0:T(8,128)(2,1)} %broadcast_select_fusion.1), channel_id=1, source_target_pairs={{0,8},{8,0},{1,9},{9,1},{2,10},{10,2},{3,11},{11,3},{4,12},{12,4},... | collective-permute-start | bytes 1081352 | tf_op jit(solution)/shard_map/ppermute | solution.py:226
  45.8 12.5 %collective-permute-start.7 = (bf16[176,1024]{1,0:T(8,128)(2,1)}, bf16[176,1024]{1,0:T(8,128)(2,1)}, u32[]{:S(2)}, u32[]{:S(2)}) collective-permute-start(bf16[176,1024]{1,0:T(8,128)(2,1)} %broadcast_select_fusion), channel_id=1, source_target_pairs={{0,8},{8,0},{1,9},{9,1},{2,10},{10,2},{3,11},{11,3},{4,12},{12,4},... | collective-permute-start | bytes 1081352 | tf_op jit(solution)/shard_map/ppermute | solution.py:226
  50.7 0.7 copy-start.2
  51.5 6.8 %collective-permute-start.9 = (bf16[160,1024]{1,0:T(8,128)(2,1)}, bf16[160,1024]{1,0:T(8,128)(2,1)}, u32[]{:S(2)}, u32[]{:S(2)}) collective-permute-start(bf16[160,1024]{1,0:T(8,128)(2,1)} %broadcast_select_fusion.2), channel_id=1, source_target_pairs={{0,8},{8,0},{1,9},{9,1},{2,10},{10,2},{3,11},{11,3},{4,12},{12,4},... | collective-permute-start | bytes 983048 | tf_op jit(solution)/shard_map/ppermute | solution.py:226
  58.3 1.0 copy-start.3
  64.6 21.2 %all-to-all-start = ((bf16[8,592,128]{2,1,0:T(8,128)(2,1)}), bf16[8,592,128]{2,1,0:T(8,128)(2,1)S(1)}, u32[]{:S(2)}, u32[]{:S(2)}) async-start(bf16[8,592,128]{2,1,0:T(8,128)(2,1)} %gram_kernel.1), calls=%async_computation | async-start | bytes 2424832 | tf_op jit(solution)/shard_map/all_to_all | solution.py:256

commit v5 on v4

--- a/solution.py
+++ b/solution.py
@@ -39,6 +39,15 @@
     return pltpu.CompilerParams(vmem_limit_bytes=16 * 1024 * 1024)
 
 
+STRIPS = (
+    (0, 1),
+    (1, 2),
+    (2, 2 + CHUNKS),
+    (2 + CHUNKS, 3 + 2 * CHUNKS),
+    (3 + 2 * CHUNKS, 3 + 3 * CHUNKS),
+)
+
+
 def choose(inputs, held, source, column):
     def one(n, carry):
         r, k = n // (K - 1), n % (K - 1) + 1
@@ -49,8 +58,8 @@
             def _():
                 start = 0
                 for strip in inputs[slot]:
-                    rows = strip.shape[0]
-                    held[n, pl.ds(start, rows), :] = strip[:, at]
+                    rows = strip[0].shape[0]
+                    held[n, pl.ds(start, rows), :] = sum(part[:, at] for part in strip)
                     start += rows
 
         return carry
@@ -72,8 +81,8 @@
 
 def gram_kernel(source, column, *refs):
     *strips, out, held = refs
-    inputs = [strips[:1], strips[1:2]]
-    inputs += [strips[2 + CHUNKS * i : 2 + CHUNKS * (i + 1)] for i in range(3)]
+    inputs = [[(strip,) for strip in strips[a:b]] for a, b in STRIPS]
+    inputs[3][-2:] = [inputs[3][-2] + inputs[3][-1]]
     choose(inputs, held, source, column)
     row, col = diagonal_mask()
     line = lax.broadcasted_iota(jnp.int32, (16, BLK), 0)
@@ -226,6 +235,11 @@
     return lax.ppermute(block, axis, [(0, 1), (1, 0)])
 
 
+def swap_some(block, alike):
+    route = [(0, 1), (3, 2)] if alike else [(1, 0), (2, 3)]
+    return lax.ppermute(block, ("xh", "core"), route)
+
+
 def along_z(block):
     depth, wide = SIZES[0], SIZES[1]
     route = []
@@ -250,7 +264,8 @@
     edges = [sum(SIZES_OF_CHUNKS[:i]) for i in range(CHUNKS + 1)]
     across = [swap(observed[a:b], "xh") for a, b in zip(edges, edges[1:])]
     beyond = [along_z(a) for a in across]
-    beside = [swap(jnp.where(core == xh, a, b), "core") for a, b in zip(across, beyond)]
+    beside = [swap(jnp.where(core == xh, a, b), "core") for a, b in zip(across[:-1], beyond[:-1])]
+    beside += [swap_some(across[-1], True), swap_some(beyond[-1], False)]
     strips = [observed, partner, *across, *beside, *beyond]
     grams = on_strips(gram_kernel, (ROWB, GRAM_ROWS, BLK), [SMEM, SMEM], source, column, *strips)
     parts = lax.all_to_all(grams, SAMP_AXES, 0, 0, tiled=True)

time: 145 us -> 147 us (1.014)
  waiting for transfers between devices: 23.2 us -> 27.2 us
  local copies, waits for them, and re-layouts: 3.83 us -> 2.13 us
    ppermute x3, waiting for transfers between devices: 1.95 us -> 6.68 us  [along_z(): return lax.ppermute(block, ('z', 'xh'), route)]
    ppermute x0 -> x2, starting transfers between devices: none -> 4.71 us  [swap_some(): return lax.ppermute(block, ('xh', 'core'), route)]
    ppermute x7 -> x6, starting transfers between devices: 36 us -> 31.7 us  [swap(): return lax.ppermute(block, axis, [(0, 1), (1, 0)])]
    unnamed x11 -> x7, local copies, waits for them, and re-layouts: 1.8 us -> 0.09 us
    ppermute x7 -> x6, waiting for transfers between devices: 4.32 us -> 2.88 us  [swap(): return lax.ppermute(block, axis, [(0, 1), (1, 0)])]
  transfers between devices with their start and end apart: 11 -> 12, of which waited for: 4 -> 5; matrix products, arithmetic and copies ran while one was open for 2% -> 2% of each run, Pallas kernels for 0% -> 0%
where the time goes in v5:
time: 147 us; the launch traced here: 146 us
  blocking collectives  56.5 us (38%)
  starting transfers between devices  51.2 us (35%)
  waiting for transfers between devices  27.2 us (19%)
  Pallas kernels  7.54 us (5%)
  local copies, waits for them, and re-layouts  2.13 us (1%)
  other arithmetic  1.6 us (1%)
    all_to_all x2, blocking collectives, everywhere(): return lax.all_to_all(rows, ('z', 'core'), 0, 0, tiled=True)  37.6 us
    ppermute x6, starting transfers between devices, swap(): return lax.ppermute(block, axis, [(0, 1), (1, 0)])  31.7 us
    all_to_all x2, blocking collectives, everywhere(): rows = lax.all_to_all(rows, ('xh', 'y', 'xl'), 0, 0, tiled=True)  18.8 us
    all_to_all x1, waiting for transfers between devices, body(): parts = lax.all_to_all(grams, SAMP_AXES, 0, 0, tiled=True)  16.9 us
    ppermute x3, starting transfers between devices, along_z(): return lax.ppermute(block, ('z', 'xh'), route)  10.6 us
    ppermute x3, waiting for transfers between devices, along_z(): return lax.ppermute(block, ('z', 'xh'), route)  6.68 us
    pallas_call x1, Pallas kernels, on_strips(): pl.pallas_call(kernel, out_shape=jax.ShapeDtypeStruct(shape, BF16), in_sp...  5.63 us
    ppermute x2, starting transfers between devices, swap_some(): return lax.ppermute(block, ('xh', 'core'), route)  4.71 us
  transfers between devices with their start and end apart: 12, of which 5 were waited for; matrix products, arithmetic and copies ran while one was open for 2% of the time, Pallas kernels for 0%

profile of v5, /device:TPU:1, one launch (start us, length us, event | category | flops | bytes accessed | tf_op | source)
XLA Modules:
  0.0 146.4 jit_solution(16185959757111596351)
XLA Ops:
  0.0 0.0 copy-start
  0.0 0.0 copy-start.1
  0.0 1.3 fusion.6
  1.3 5.5 %collective-permute-start.1 = (bf16[176,1024]{1,0:T(8,128)(2,1)S(1)}, bf16[176,1024]{1,0:T(8,128)(2,1)S(1)}, u32[]{:S(2)}, u32[]{:S(2)}) collective-permute-start(bf16[176,1024]{1,0:T(8,128)(2,1)S(1)} %get-tuple-element.20), channel_id=1, source_target_pairs={{0,16},{16,0},{1,17},{17,1},{2,18},{18,2},{3,19},{19,3},{4,20},{20... | collective-permute-start | bytes 1081352 | tf_op jit(solution)/shard_map/ppermute | solution.py:235
  6.8 1.9 %collective-permute-start.2 = (bf16[176,1024]{1,0:T(8,128)(2,1)S(1)}, bf16[176,1024]{1,0:T(8,128)(2,1)S(1)}, u32[]{:S(2)}, u32[]{:S(2)}) collective-permute-start(bf16[176,1024]{1,0:T(8,128)(2,1)S(1)} %get-tuple-element.19), channel_id=1, source_target_pairs={{0,16},{16,0},{1,17},{17,1},{2,18},{18,2},{3,19},{19,3},{4,20},{20... | collective-permute-start | bytes 1081352 | tf_op jit(solution)/shard_map/ppermute | solution.py:235
  8.7 2.9 %collective-permute-done.1.refs_2_ = bf16[176,1024]{1,0:T(8,128)(2,1)S(1)} collective-permute-done((bf16[176,1024]{1,0:T(8,128)(2,1)S(1)}, bf16[176,1024]{1,0:T(8,128)(2,1)S(1)}, u32[]{:S(2)}, u32[]{:S(2)}) %collective-permute-start.1) | collective-permute-done | bytes 360480 | tf_op jit(solution)/shard_map/ppermute | solution.py:235
  11.6 6.8 %collective-permute-start.4 = (bf16[176,1024]{1,0:T(8,128)(2,1)S(1)}, bf16[176,1024]{1,0:T(8,128)(2,1)S(1)}, u32[]{:S(2)}, u32[]{:S(2)}) collective-permute-start(bf16[176,1024]{1,0:T(8,128)(2,1)S(1)} %collective-permute-done.1.refs_2_), channel_id=1, source_target_pairs={{0,32},{16,496},{32,64},{48,16},{64,96},{80,48},{96,128},{112,80},... | collective-permute-start | bytes 1081352 | tf_op jit(solution)/shard_map/ppermute | solution.py:249
  18.3 0.0 copy-done.1
  18.3 0.8 slice.11
  19.1 0.0 copy-start.2
  19.1 12.3 %collective-permute-start.3 = (bf16[160,1024]{1,0:T(8,128)(2,1)}, bf16[160,1024]{1,0:T(8,128)(2,1)}, u32[]{:S(2)}, u32[]{:S(2)}) collective-permute-start(bf16[160,1024]{1,0:T(8,128)(2,1)} %slice.11), channel_id=1, source_target_pairs={{0,16},{16,0},{1,17},{17,1},{2,18},{18,2},{3,19},{19,3},{4,20},{20... | collective-permute-start | bytes 983048 | tf_op jit(solution)/shard_map/ppermute | solution.py:235
  31.5 5.2 %collective-permute-start = (bf16[512,1024]{1,0:T(8,128)(2,1)S(1)}, bf16[512,1024]{1,0:T(8,128)(2,1)}, u32[]{:S(2)}, u32[]{:S(2)}) collective-permute-start(bf16[512,1024]{1,0:T(8,128)(2,1)S(1)} %copy-done.1), channel_id=1, source_target_pairs={{0,8},{8,0},{1,9},{9,1},{2,10},{10,2},{3,11},{11,3},{4,12},{12,4},... | collective-permute-start | bytes 3145736 | tf_op jit(solution)/shard_map/ppermute | solution.py:235
  36.6 0.0 collective-permute-done.2.refs_3_
  36.6 1.9 %collective-permute-start.6 = (bf16[176,1024]{1,0:T(8,128)(2,1)S(1)}, bf16[176,1024]{1,0:T(8,128)(2,1)S(1)}, u32[]{:S(2)}, u32[]{:S(2)}) collective-permute-start(bf16[176,1024]{1,0:T(8,128)(2,1)S(1)} %collective-permute-done.2.refs_3_), channel_id=1, source_target_pairs={{0,32},{16,496},{32,64},{48,16},{64,96},{80,48},{96,128},{112,80},... | collective-permute-start | bytes 1081352 | tf_op jit(solution)/shard_map/ppermute | solution.py:249
  38.6 0.0 collective-permute-done.3.refs_4_
  38.6 1.9 %collective-permute-start.9 = (bf16[160,1024]{1,0:T(8,128)(2,1)}, bf16[160,1024]{1,0:T(8,128)(2,1)}, u32[]{:S(2)}, u32[]{:S(2)}) collective-permute-start(bf16[160,1024]{1,0:T(8,128)(2,1)} %collective-permute-done.3.refs_4_), channel_id=1, source_target_pairs={{0,32},{16,496},{32,64},{48,16},{64,96},{80,48},{96,128},{112,80},... | collective-permute-start | bytes 983048 | tf_op jit(solution)/shard_map/ppermute | solution.py:249
  40.5 0.0 collective-permute-done.4.refs_9_
  40.5 0.8 broadcast_select_fusion.1
  41.3 3.7 %collective-permute-start.5 = (bf16[176,1024]{1,0:T(8,128)(2,1)}, bf16[176,1024]{1,0:T(8,128)(2,1)}, u32[]{:S(2)}, u32[]{:S(2)}) collective-permute-start(bf16[176,1024]{1,0:T(8,128)(2,1)} %broadcast_select_fusion.1), channel_id=1, source_target_pairs={{0,8},{8,0},{1,9},{9,1},{2,10},{10,2},{3,11},{11,3},{4,12},{12,4},... | collective-permute-start | bytes 1081352 | tf_op jit(solution)/shard_map/ppermute | solution.py:235
  45.0 4.7 %collective-permute-done.6.refs_10_ = bf16[176,1024]{1,0:T(8,128)(2,1)S(1)} collective-permute-done((bf16[176,1024]{1,0:T(8,128)(2,1)S(1)}, bf16[176,1024]{1,0:T(8,128)(2,1)S(1)}, u32[]{:S(2)}, u32[]{:S(2)}) %collective-permute-start.6) | collective-permute-done | bytes 360480 | tf_op jit(solution)/shard_map/ppermute | solution.py:249
  49.8 0.8 broadcast_select_fusion
  50.6 3.1 %collective-permute-start.7 = (bf16[176,1024]{1,0:T(8,128)(2,1)}, bf16[176,1024]{1,0:T(8,128)(2,1)}, u32[]{:S(2)}, u32[]{:S(2)}) collective-permute-start(bf16[176,1024]{1,0:T(8,128)(2,1)} %broadcast_select_fusion), channel_id=1, source_target_pairs={{0,8},{8,0},{1,9},{9,1},{2,10},{10,2},{3,11},{11,3},{4,12},{12,4},... | collective-permute-start | bytes 1081352 | tf_op jit(solution)/shard_map/ppermute | solution.py:235
  53.7 1.3 collective-permute-start.8
  55.0 1.9 %collective-permute-done.9.refs_11_ = bf16[160,1024]{1,0:T(8,128)(2,1)} collective-permute-done((bf16[160,1024]{1,0:T(8,128)(2,1)}, bf16[160,1024]{1,0:T(8,128)(2,1)}, u32[]{:S(2)}, u32[]{:S(2)}) %collective-permute-start.9) | collective-permute-done | bytes 327712 | tf_op jit(solution)/shard_map/ppermute | solution.py:249
  56.9 3.4 %collective-permute-start.10 = (bf16[160,1024]{1,0:T(8,128)(2,1)}, bf16[160,1024]{1,0:T(8,128)(2,1)}, u32[]{:S(2)}, u32[]{:S(2)}) collective-permute-start(bf16[160,1024]{1,0:T(8,128)(2,1)} %collective-permute-done.9.refs_11_), channel_id=1, source_target_pairs={{8,0},{16,24},{9,1},{17,25},{10,2},{18,26},{11,3},{19,27},{12,4},{... | collective-permute-start | bytes 983048 | tf_op jit(solution)/shard_map/ppermute | solution.py:240
  60.3 0.0 copy-done.2
  60.3 0.1 copy.8
  60.4 0.0 collective-permute-done.8.refs_7_
  60.4 0.7 collective-permute-done.10.refs_8_
  61.2 0.0 collective-permute-done.refs_1_
  61.2 0.0 collective-permute-done.5.refs_5_
  61.2 0.0 collective-permute-done.7.refs_6_
  61.2 5.6 %gram_kernel.1 = bf16[8,592,128]{2,1,0:T(8,128)(2,1)} custom-call(s32[8,3]{1,0:T(8,128)S(1)} %get-tuple-element.22.source, s32[8,3]{1,0:T(8,128)S(1)} %get-tuple-element.21.column, bf16[512,1024]{1,0:T(8,128)(2,1)S(1)} %copy-done.1, bf16[512,1024]{1,0:T(8,128)(2,1)} %collective-permute-done.refs_1_, bf16[176,1024]{1,0:T(8,128)(2,1)S(1)} %collective-permute-done.1.refs_2_, ...), custom_call_target="tpu_custom_call" | custom-call | flops 805306368 | bytes 6291456 | tf_op jit(solution)/shard_map/gram_kernel/pallas_call | solution.py:116
  66.8 4.2 %all-to-all-start = ((bf16[8,592,128]{2,1,0:T(8,128)(2,1)}), bf16[8,592,128]{2,1,0:T(8,128)(2,1)S(1)}, u32[]{:S(2)}, u32[]{:S(2)}) async-start(bf16[8,592,128]{2,1,0:T(8,128)(2,1)} %gram_kernel.1), calls=%async_computation | async-start | bytes 2424832 | tf_op jit(solution)/shard_map/all_to_all | solution.py:271
  71.0 0.0 copy-done
  71.1 16.9 %all-to-all-done.parts = bf16[8,592,128]{2,1,0:T(8,128)(2,1)S(1)} async-done(((bf16[8,592,128]{2,1,0:T(8,128)(2,1)}), bf16[8,592,128]{2,1,0:T(8,128)(2,1)S(1)}, u32[]{:S(2)}, u32[]{:S(2)}) %all-to-all-start) | async-done | bytes 1212448 | tf_op jit(solution)/shard_map/all_to_all | solution.py:271
  88.0 0.6 first_kernel.1
  88.6 9.7 %all_to_all.49 = f32[16,1,128]{2,1,0:T(1,128)S(1)} all-to-all(f32[16,1,128]{2,1,0:T(1,128)S(1)} %bitcast.26), channel_id=1, replica_groups=mesh['z'=16,'xh'=2,'core'=2,'y'=4,'xl'=2] {'xh','y','xl'}, dimensions={0} | all-to-all | bytes 16384 | tf_op jit(solution)/shard_map/all_to_all | solution.py:229
  98.3 20.8 %all_to_all.50 = f32[32,1,128]{2,1,0:T(1,128)S(1)} all-to-all(f32[32,1,128]{2,1,0:T(1,128)S(1)} %bitcast.21), channel_id=1, replica_groups=mesh['z'=16,'xh'=2,'core'=2,'y'=4,'xl'=2] {'z','core'}, dimensions={0} | all-to-all | bytes 32768 | tf_op jit(solution)/shard_map/all_to_all | solution.py:231
  119.1 0.5 second_kernel.1
  119.6 9.1 %all_to_all.51 = f32[16,1,128]{2,1,0:T(1,128)S(1)} all-to-all(f32[16,1,128]{2,1,0:T(1,128)S(1)} %bitcast.25), channel_id=1, replica_groups=mesh['z'=16,'xh'=2,'core'=2,'y'=4,'xl'=2] {'xh','y','xl'}, dimensions={0} | all-to-all | bytes 16384 | tf_op jit(solution)/shard_map/all_to_all | solution.py:229
  128.7 16.8 %all_to_all.52 = f32[32,1,128]{2,1,0:T(1,128)S(1)} all-to-all(f32[32,1,128]{2,1,0:T(1,128)S(1)} %bitcast.22), channel_id=1, replica_groups=mesh['z'=16,'xh'=2,'core'=2,'y'=4,'xl'=2] {'z','core'}, dimensions={0} | all-to-all | bytes 32768 | tf_op jit(solution)/shard_map/all_to_all | solution.py:231
  145.5 0.9 last_kernel.1
  (4 shorter events, 0.1 us)
Async XLA Ops:
  0.0 71.0 %copy-start = (bf16[8,3,128,128]{3,2,1,0:T(8,128)(2,1)S(1)}, bf16[8,3,128,128]{3,2,1,0:T(8,128)(2,1)}, u32[]{:S(2)}) copy-start(bf16[8,3,128,128]{3,2,1,0:T(8,128)(2,1)} %param.5) | copy-start | bytes 2359300
  0.0 18.3 %copy-start.1 = (bf16[512,1024]{1,0:T(8,128)(2,1)S(1)}, bf16[512,1024]{1,0:T(8,128)(2,1)}, u32[]{:S(2)}) copy-start(bf16[512,1024]{1,0:T(8,128)(2,1)} %refs_0_.1) | copy-start | bytes 3145732
  1.3 10.3 %collective-permute-start.1 = (bf16[176,1024]{1,0:T(8,128)(2,1)S(1)}, bf16[176,1024]{1,0:T(8,128)(2,1)S(1)}, u32[]{:S(2)}, u32[]{:S(2)}) collective-permute-start(bf16[176,1024]{1,0:T(8,128)(2,1)S(1)} %get-tuple-element.20), channel_id=1, source_target_pairs={{0,16},{16,0},{1,17},{17,1},{2,18},{18,2},{3,19},{19,3},{4,20},{20... | collective-permute-start | bytes 1081352 | tf_op jit(solution)/shard_map/ppermute | solution.py:235
  6.8 29.9 %collective-permute-start.2 = (bf16[176,1024]{1,0:T(8,128)(2,1)S(1)}, bf16[176,1024]{1,0:T(8,128)(2,1)S(1)}, u32[]{:S(2)}, u32[]{:S(2)}) collective-permute-start(bf16[176,1024]{1,0:T(8,128)(2,1)S(1)} %get-tuple-element.19), channel_id=1, source_target_pairs={{0,16},{16,0},{1,17},{17,1},{2,18},{18,2},{3,19},{19,3},{4,20},{20... | collective-permute-start | bytes 1081352 | tf_op jit(solution)/shard_map/ppermute | solution.py:235
  11.6 28.9 %collective-permute-start.4 = (bf16[176,1024]{1,0:T(8,128)(2,1)S(1)}, bf16[176,1024]{1,0:T(8,128)(2,1)S(1)}, u32[]{:S(2)}, u32[]{:S(2)}) collective-permute-start(bf16[176,1024]{1,0:T(8,128)(2,1)S(1)} %collective-permute-done.1.refs_2_), channel_id=1, source_target_pairs={{0,32},{16,496},{32,64},{48,16},{64,96},{80,48},{96,128},{112,80},... | collective-permute-start | bytes 1081352 | tf_op jit(solution)/shard_map/ppermute | solution.py:249
  19.1 41.2 %copy-start.2 = (s32[8,3]{0,1:T(4,128)S(1)}, s32[8,3]{0,1:T(4,128)}, u32[]{:S(2)}) copy-start(s32[8,3]{0,1:T(4,128)} %param.4) | copy-start | bytes 292
  19.1 19.5 %collective-permute-start.3 = (bf16[160,1024]{1,0:T(8,128)(2,1)}, bf16[160,1024]{1,0:T(8,128)(2,1)}, u32[]{:S(2)}, u32[]{:S(2)}) collective-permute-start(bf16[160,1024]{1,0:T(8,128)(2,1)} %slice.11), channel_id=1, source_target_pairs={{0,16},{16,0},{1,17},{17,1},{2,18},{18,2},{3,19},{19,3},{4,20},{20... | collective-permute-start | bytes 983048 | tf_op jit(solution)/shard_map/ppermute | solution.py:235
  31.5 29.7 %collective-permute-start = (bf16[512,1024]{1,0:T(8,128)(2,1)S(1)}, bf16[512,1024]{1,0:T(8,128)(2,1)}, u32[]{:S(2)}, u32[]{:S(2)}) collective-permute-start(bf16[512,1024]{1,0:T(8,128)(2,1)S(1)} %copy-done.1), channel_id=1, source_target_pairs={{0,8},{8,0},{1,9},{9,1},{2,10},{10,2},{3,11},{11,3},{4,12},{12,4},... | collective-permute-start | bytes 3145736 | tf_op jit(solution)/shard_map/ppermute | solution.py:235
  36.6 13.1 %collective-permute-start.6 = (bf16[176,1024]{1,0:T(8,128)(2,1)S(1)}, bf16[176,1024]{1,0:T(8,128)(2,1)S(1)}, u32[]{:S(2)}, u32[]{:S(2)}) collective-permute-start(bf16[176,1024]{1,0:T(8,128)(2,1)S(1)} %collective-permute-done.2.refs_3_), channel_id=1, source_target_pairs={{0,32},{16,496},{32,64},{48,16},{64,96},{80,48},{96,128},{112,80},... | collective-permute-start | bytes 1081352 | tf_op jit(solution)/shard_map/ppermute | solution.py:249
  38.6 18.3 %collective-permute-start.9 = (bf16[160,1024]{1,0:T(8,128)(2,1)}, bf16[160,1024]{1,0:T(8,128)(2,1)}, u32[]{:S(2)}, u32[]{:S(2)}) collective-permute-start(bf16[160,1024]{1,0:T(8,128)(2,1)} %collective-permute-done.3.refs_4_), channel_id=1, source_target_pairs={{0,32},{16,496},{32,64},{48,16},{64,96},{80,48},{96,128},{112,80},... | collective-permute-start | bytes 983048 | tf_op jit(solution)/shard_map/ppermute | solution.py:249
  41.3 19.9 %collective-permute-start.5 = (bf16[176,1024]{1,0:T(8,128)(2,1)}, bf16[176,1024]{1,0:T(8,128)(2,1)}, u32[]{:S(2)}, u32[]{:S(2)}) collective-permute-start(bf16[176,1024]{1,0:T(8,128)(2,1)} %broadcast_select_fusion.1), channel_id=1, source_target_pairs={{0,8},{8,0},{1,9},{9,1},{2,10},{10,2},{3,11},{11,3},{4,12},{12,4},... | collective-permute-start | bytes 1081352 | tf_op jit(solution)/shard_map/ppermute | solution.py:235
  50.6 10.6 %collective-permute-start.7 = (bf16[176,1024]{1,0:T(8,128)(2,1)}, bf16[176,1024]{1,0:T(8,128)(2,1)}, u32[]{:S(2)}, u32[]{:S(2)}) collective-permute-start(bf16[176,1024]{1,0:T(8,128)(2,1)} %broadcast_select_fusion), channel_id=1, source_target_pairs={{0,8},{8,0},{1,9},{9,1},{2,10},{10,2},{3,11},{11,3},{4,12},{12,4},... | collective-permute-start | bytes 1081352 | tf_op jit(solution)/shard_map/ppermute | solution.py:235
  53.7 6.8 %collective-permute-start.8 = (bf16[160,1024]{1,0:T(8,128)(2,1)}, bf16[160,1024]{1,0:T(8,128)(2,1)}, u32[]{:S(2)}, u32[]{:S(2)}) collective-permute-start(bf16[160,1024]{1,0:T(8,128)(2,1)} %collective-permute-done.3.refs_4_), channel_id=1, source_target_pairs={{0,8},{24,16},{1,9},{25,17},{2,10},{26,18},{3,11},{27,19},{4,12},{... | collective-permute-start | bytes 983048 | tf_op jit(solution)/shard_map/ppermute | solution.py:240
  56.9 4.3 %collective-permute-start.10 = (bf16[160,1024]{1,0:T(8,128)(2,1)}, bf16[160,1024]{1,0:T(8,128)(2,1)}, u32[]{:S(2)}, u32[]{:S(2)}) collective-permute-start(bf16[160,1024]{1,0:T(8,128)(2,1)} %collective-permute-done.9.refs_11_), channel_id=1, source_target_pairs={{8,0},{16,24},{9,1},{17,25},{10,2},{18,26},{11,3},{19,27},{12,4},{... | collective-permute-start | bytes 983048 | tf_op jit(solution)/shard_map/ppermute | solution.py:240
  66.8 21.2 %all-to-all-start = ((bf16[8,592,128]{2,1,0:T(8,128)(2,1)}), bf16[8,592,128]{2,1,0:T(8,128)(2,1)S(1)}, u32[]{:S(2)}, u32[]{:S(2)}) async-start(bf16[8,592,128]{2,1,0:T(8,128)(2,1)} %gram_kernel.1), calls=%async_computation | async-start | bytes 2424832 | tf_op jit(solution)/shard_map/all_to_all | solution.py:271

commit v6 on v5

--- a/solution.py
+++ b/solution.py
@@ -13,7 +13,7 @@
 SIZES = (16, 2, 2, 4, 2)
 VAR_AXES = ("z", "xh", "core")
 SAMP_AXES = ("y", "xl")
-SIZES_OF_CHUNKS = (176, 176, 160)
+SIZES_OF_CHUNKS = (192, 176, 144)
 CHUNKS = len(SIZES_OF_CHUNKS)
 ROWB = 8
 K = 3
@@ -41,10 +41,10 @@
 
 STRIPS = (
     (0, 1),
-    (1, 2),
-    (2, 2 + CHUNKS),
-    (2 + CHUNKS, 3 + 2 * CHUNKS),
-    (3 + 2 * CHUNKS, 3 + 3 * CHUNKS),
+    (1, 3),
+    (3, 3 + CHUNKS),
+    (3 + CHUNKS, 4 + 2 * CHUNKS),
+    (4 + 2 * CHUNKS, 4 + 3 * CHUNKS),
 )
 
 
@@ -260,13 +260,14 @@
     source = jnp.where(offset == 0, 0, jnp.where(abs(offset) == 1, near, far)).astype(jnp.int32)
     column = (pattern % ROWB).astype(jnp.int32)
 
-    partner = swap(observed, "core")
+    half = observed.shape[0] // 2
+    partner = [swap(observed[:half], "core"), swap(observed[half:], "core")]
     edges = [sum(SIZES_OF_CHUNKS[:i]) for i in range(CHUNKS + 1)]
     across = [swap(observed[a:b], "xh") for a, b in zip(edges, edges[1:])]
     beyond = [along_z(a) for a in across]
     beside = [swap(jnp.where(core == xh, a, b), "core") for a, b in zip(across[:-1], beyond[:-1])]
     beside += [swap_some(across[-1], True), swap_some(beyond[-1], False)]
-    strips = [observed, partner, *across, *beside, *beyond]
+    strips = [observed, *partner, *across, *beside, *beyond]
     grams = on_strips(gram_kernel, (ROWB, GRAM_ROWS, BLK), [SMEM, SMEM], source, column, *strips)
     parts = lax.all_to_all(grams, SAMP_AXES, 0, 0, tiled=True)
     omega = lax.dynamic_index_in_dim(omega_init, samp, 0, keepdims=False)

time: 147 us -> 146 us (level)
  waiting for transfers between devices: 27.2 us -> 22.9 us
  local copies, waits for them, and re-layouts: 2.13 us -> 4.05 us
  blocking collectives: 56.5 us -> 58.4 us
    ppermute x3, waiting for transfers between devices: 6.68 us -> 2.95 us  [along_z(): return lax.ppermute(block, ('z', 'xh'), route)]
    ppermute x6 -> x7, starting transfers between devices: 31.7 us -> 31.1 us  [swap(): return lax.ppermute(block, axis, [(0, 1), (1, 0)])]
  transfers between devices with their start and end apart: 12 -> 13, of which waited for: 5 -> 4; matrix products, arithmetic and copies ran while one was open for 2% -> 3% of each run, Pallas kernels for 0% -> 0%
where the time goes in v6:
time: 146 us
  blocking collectives  58.4 us (40%)
  starting transfers between devices  51 us (35%)
  waiting for transfers between devices  22.9 us (16%)
  Pallas kernels  7.46 us (5%)
  local copies, waits for them, and re-layouts  4.05 us (3%)
  other arithmetic  1.6 us (1%)
    all_to_all x2, blocking collectives, everywhere(): return lax.all_to_all(rows, ('z', 'core'), 0, 0, tiled=True)  38.6 us
    ppermute x7, starting transfers between devices, swap(): return lax.ppermute(block, axis, [(0, 1), (1, 0)])  31.1 us
    all_to_all x2, blocking collectives, everywhere(): rows = lax.all_to_all(rows, ('xh', 'y', 'xl'), 0, 0, tiled=True)  19.8 us
    all_to_all x1, waiting for transfers between devices, body(): parts = lax.all_to_all(grams, SAMP_AXES, 0, 0, tiled=True)  16.9 us
    ppermute x3, starting transfers between devices, along_z(): return lax.ppermute(block, ('z', 'xh'), route)  10.8 us
    pallas_call x1, Pallas kernels, on_strips(): pl.pallas_call(kernel, out_shape=jax.ShapeDtypeStruct(shape, BF16), in_sp...  5.56 us
    ppermute x2, starting transfers between devices, swap_some(): return lax.ppermute(block, ('xh', 'core'), route)  4.94 us
    all_to_all x1, starting transfers between devices, body(): parts = lax.all_to_all(grams, SAMP_AXES, 0, 0, tiled=True)  4.22 us
  transfers between devices with their start and end apart: 13, of which 4 were waited for; matrix products, arithmetic and copies ran while one was open for 3% of the time, Pallas kernels for 0%

profile of v6, /device:TPU:1, one launch (start us, length us, event | category | flops | bytes accessed | tf_op | source)
XLA Modules:
  0.0 145.7 jit_solution(10200654943458726532)
XLA Ops:
  0.0 0.0 copy-start
  0.0 0.0 copy-start.1
  0.0 1.2 slice.17
  1.2 5.5 %collective-permute-start.2 = (bf16[192,1024]{1,0:T(8,128)(2,1)S(1)}, bf16[192,1024]{1,0:T(8,128)(2,1)S(1)}, u32[]{:S(2)}, u32[]{:S(2)}) collective-permute-start(bf16[192,1024]{1,0:T(8,128)(2,1)S(1)} %slice.17), channel_id=1, source_target_pairs={{0,16},{16,0},{1,17},{17,1},{2,18},{18,2},{3,19},{19,3},{4,20},{20... | collective-permute-start | bytes 1179656 | tf_op jit(solution)/shard_map/ppermute | solution.py:235
  6.7 1.0 slice.18
  7.7 1.9 %collective-permute-start.3 = (bf16[176,1024]{1,0:T(8,128)(2,1)S(1)}, bf16[176,1024]{1,0:T(8,128)(2,1)S(1)}, u32[]{:S(2)}, u32[]{:S(2)}) collective-permute-start(bf16[176,1024]{1,0:T(8,128)(2,1)S(1)} %slice.18), channel_id=1, source_target_pairs={{0,16},{16,0},{1,17},{17,1},{2,18},{18,2},{3,19},{19,3},{4,20},{20... | collective-permute-start | bytes 1081352 | tf_op jit(solution)/shard_map/ppermute | solution.py:235
  9.6 2.4 %collective-permute-done.2.refs_3_ = bf16[192,1024]{1,0:T(8,128)(2,1)S(1)} collective-permute-done((bf16[192,1024]{1,0:T(8,128)(2,1)S(1)}, bf16[192,1024]{1,0:T(8,128)(2,1)S(1)}, u32[]{:S(2)}, u32[]{:S(2)}) %collective-permute-start.2) | collective-permute-done | bytes 393248 | tf_op jit(solution)/shard_map/ppermute | solution.py:235
  12.0 6.9 %collective-permute-start.5 = (bf16[192,1024]{1,0:T(8,128)(2,1)S(1)}, bf16[192,1024]{1,0:T(8,128)(2,1)S(1)}, u32[]{:S(2)}, u32[]{:S(2)}) collective-permute-start(bf16[192,1024]{1,0:T(8,128)(2,1)S(1)} %collective-permute-done.2.refs_3_), channel_id=1, source_target_pairs={{0,32},{16,496},{32,64},{48,16},{64,96},{80,48},{96,128},{112,80},... | collective-permute-start | bytes 1179656 | tf_op jit(solution)/shard_map/ppermute | solution.py:249
  18.9 0.0 copy-done.1
  18.9 0.7 slice.19
  19.7 12.2 %collective-permute-start.4 = (bf16[144,1024]{1,0:T(8,128)(2,1)}, bf16[144,1024]{1,0:T(8,128)(2,1)}, u32[]{:S(2)}, u32[]{:S(2)}) collective-permute-start(bf16[144,1024]{1,0:T(8,128)(2,1)} %slice.19), channel_id=1, source_target_pairs={{0,16},{16,0},{1,17},{17,1},{2,18},{18,2},{3,19},{19,3},{4,20},{20... | collective-permute-start | bytes 884744 | tf_op jit(solution)/shard_map/ppermute | solution.py:235
  31.9 0.0 collective-permute-done.3.refs_4_
  31.9 1.9 %collective-permute-start.7 = (bf16[176,1024]{1,0:T(8,128)(2,1)S(1)}, bf16[176,1024]{1,0:T(8,128)(2,1)S(1)}, u32[]{:S(2)}, u32[]{:S(2)}) collective-permute-start(bf16[176,1024]{1,0:T(8,128)(2,1)S(1)} %collective-permute-done.3.refs_4_), channel_id=1, source_target_pairs={{0,32},{16,496},{32,64},{48,16},{64,96},{80,48},{96,128},{112,80},... | collective-permute-start | bytes 1081352 | tf_op jit(solution)/shard_map/ppermute | solution.py:249
  33.8 1.1 fusion.6
  34.9 0.0 copy-start.2
  34.9 5.3 %collective-permute-start = (bf16[256,1024]{1,0:T(8,128)(2,1)}, bf16[256,1024]{1,0:T(8,128)(2,1)}, u32[]{:S(2)}, u32[]{:S(2)}) collective-permute-start(bf16[256,1024]{1,0:T(8,128)(2,1)} %get-tuple-element.20), channel_id=1, source_target_pairs={{0,8},{8,0},{1,9},{9,1},{2,10},{10,2},{3,11},{11,3},{4,12},{12,4},... | collective-permute-start | bytes 1572872 | tf_op jit(solution)/shard_map/ppermute | solution.py:235
  40.2 1.9 %collective-permute-start.1 = (bf16[256,1024]{1,0:T(8,128)(2,1)}, bf16[256,1024]{1,0:T(8,128)(2,1)}, u32[]{:S(2)}, u32[]{:S(2)}) collective-permute-start(bf16[256,1024]{1,0:T(8,128)(2,1)} %get-tuple-element.19), channel_id=1, source_target_pairs={{0,8},{8,0},{1,9},{9,1},{2,10},{10,2},{3,11},{11,3},{4,12},{12,4},... | collective-permute-start | bytes 1572872 | tf_op jit(solution)/shard_map/ppermute | solution.py:235
  42.1 0.0 collective-permute-done.4.refs_5_
  42.1 1.9 %collective-permute-start.10 = (bf16[144,1024]{1,0:T(8,128)(2,1)}, bf16[144,1024]{1,0:T(8,128)(2,1)}, u32[]{:S(2)}, u32[]{:S(2)}) collective-permute-start(bf16[144,1024]{1,0:T(8,128)(2,1)} %collective-permute-done.4.refs_5_), channel_id=1, source_target_pairs={{0,32},{16,496},{32,64},{48,16},{64,96},{80,48},{96,128},{112,80},... | collective-permute-start | bytes 884744 | tf_op jit(solution)/shard_map/ppermute | solution.py:249
  44.0 0.0 collective-permute-done.5.refs_10_
  44.1 0.8 broadcast_select_fusion
  44.8 2.4 %collective-permute-start.6 = (bf16[192,1024]{1,0:T(8,128)(2,1)}, bf16[192,1024]{1,0:T(8,128)(2,1)}, u32[]{:S(2)}, u32[]{:S(2)}) collective-permute-start(bf16[192,1024]{1,0:T(8,128)(2,1)} %broadcast_select_fusion), channel_id=1, source_target_pairs={{0,8},{8,0},{1,9},{9,1},{2,10},{10,2},{3,11},{11,3},{4,12},{12,4},... | collective-permute-start | bytes 1179656 | tf_op jit(solution)/shard_map/ppermute | solution.py:235
  47.2 0.0 collective-permute-done.7.refs_11_
  47.3 0.8 broadcast_select_fusion.1
  48.0 1.9 %collective-permute-start.8 = (bf16[176,1024]{1,0:T(8,128)(2,1)}, bf16[176,1024]{1,0:T(8,128)(2,1)}, u32[]{:S(2)}, u32[]{:S(2)}) collective-permute-start(bf16[176,1024]{1,0:T(8,128)(2,1)} %broadcast_select_fusion.1), channel_id=1, source_target_pairs={{0,8},{8,0},{1,9},{9,1},{2,10},{10,2},{3,11},{11,3},{4,12},{12,4},... | collective-permute-start | bytes 1081352 | tf_op jit(solution)/shard_map/ppermute | solution.py:235
  50.0 0.0 collective-permute-done.refs_1_
  50.0 1.3 collective-permute-start.9
  51.3 2.9 %collective-permute-done.10.refs_12_ = bf16[144,1024]{1,0:T(8,128)(2,1)} collective-permute-done((bf16[144,1024]{1,0:T(8,128)(2,1)}, bf16[144,1024]{1,0:T(8,128)(2,1)}, u32[]{:S(2)}, u32[]{:S(2)}) %collective-permute-start.10) | collective-permute-done | bytes 294944 | tf_op jit(solution)/shard_map/ppermute | solution.py:249
  54.2 3.6 %collective-permute-start.11 = (bf16[144,1024]{1,0:T(8,128)(2,1)}, bf16[144,1024]{1,0:T(8,128)(2,1)}, u32[]{:S(2)}, u32[]{:S(2)}) collective-permute-start(bf16[144,1024]{1,0:T(8,128)(2,1)} %collective-permute-done.10.refs_12_), channel_id=1, source_target_pairs={{8,0},{16,24},{9,1},{17,25},{10,2},{18,26},{11,3},{19,27},{12,4},{... | collective-permute-start | bytes 884744 | tf_op jit(solution)/shard_map/ppermute | solution.py:240
  57.9 0.0 copy-done.2
  57.9 0.1 copy.8
  58.0 0.0 collective-permute-done.1.refs_2_
  58.0 0.0 collective-permute-done.9.refs_8_
  58.0 0.7 collective-permute-done.11.refs_9_
  58.7 0.0 collective-permute-done.8.refs_7_
  58.7 0.0 collective-permute-done.6.refs_6_
  58.7 5.6 %gram_kernel.1 = bf16[8,592,128]{2,1,0:T(8,128)(2,1)} custom-call(s32[8,3]{1,0:T(8,128)S(1)} %get-tuple-element.22.source, s32[8,3]{1,0:T(8,128)S(1)} %get-tuple-element.21.column, bf16[512,1024]{1,0:T(8,128)(2,1)S(1)} %copy-done.1, bf16[256,1024]{1,0:T(8,128)(2,1)} %collective-permute-done.refs_1_, bf16[256,1024]{1,0:T(8,128)(2,1)} %collective-permute-done.1.refs_2_, ...), custom_call_target="tpu_custom_call" | custom-call | flops 805306368 | bytes 6291456 | tf_op jit(solution)/shard_map/gram_kernel/pallas_call | solution.py:116
  64.2 4.2 %all-to-all-start = ((bf16[8,592,128]{2,1,0:T(8,128)(2,1)}), bf16[8,592,128]{2,1,0:T(8,128)(2,1)S(1)}, u32[]{:S(2)}, u32[]{:S(2)}) async-start(bf16[8,592,128]{2,1,0:T(8,128)(2,1)} %gram_kernel.1), calls=%async_computation | async-start | bytes 2424832 | tf_op jit(solution)/shard_map/all_to_all | solution.py:272
  68.5 0.0 copy-done
  68.5 16.9 %all-to-all-done.parts = bf16[8,592,128]{2,1,0:T(8,128)(2,1)S(1)} async-done(((bf16[8,592,128]{2,1,0:T(8,128)(2,1)}), bf16[8,592,128]{2,1,0:T(8,128)(2,1)S(1)}, u32[]{:S(2)}, u32[]{:S(2)}) %all-to-all-start) | async-done | bytes 1212448 | tf_op jit(solution)/shard_map/all_to_all | solution.py:272
  85.4 0.6 first_kernel.1
  85.9 10.7 %all_to_all.49 = f32[16,1,128]{2,1,0:T(1,128)S(1)} all-to-all(f32[16,1,128]{2,1,0:T(1,128)S(1)} %bitcast.26), channel_id=1, replica_groups=mesh['z'=16,'xh'=2,'core'=2,'y'=4,'xl'=2] {'xh','y','xl'}, dimensions={0} | all-to-all | bytes 16384 | tf_op jit(solution)/shard_map/all_to_all | solution.py:229
  96.7 21.8 %all_to_all.50 = f32[32,1,128]{2,1,0:T(1,128)S(1)} all-to-all(f32[32,1,128]{2,1,0:T(1,128)S(1)} %bitcast.21), channel_id=1, replica_groups=mesh['z'=16,'xh'=2,'core'=2,'y'=4,'xl'=2] {'z','core'}, dimensions={0} | all-to-all | bytes 32768 | tf_op jit(solution)/shard_map/all_to_all | solution.py:231
  118.4 0.5 second_kernel.1
  118.9 9.1 %all_to_all.51 = f32[16,1,128]{2,1,0:T(1,128)S(1)} all-to-all(f32[16,1,128]{2,1,0:T(1,128)S(1)} %bitcast.25), channel_id=1, replica_groups=mesh['z'=16,'xh'=2,'core'=2,'y'=4,'xl'=2] {'xh','y','xl'}, dimensions={0} | all-to-all | bytes 16384 | tf_op jit(solution)/shard_map/all_to_all | solution.py:229
  128.0 16.8 %all_to_all.52 = f32[32,1,128]{2,1,0:T(1,128)S(1)} all-to-all(f32[32,1,128]{2,1,0:T(1,128)S(1)} %bitcast.22), channel_id=1, replica_groups=mesh['z'=16,'xh'=2,'core'=2,'y'=4,'xl'=2] {'z','core'}, dimensions={0} | all-to-all | bytes 32768 | tf_op jit(solution)/shard_map/all_to_all | solution.py:231
  144.8 0.9 last_kernel.1
  (4 shorter events, 0.1 us)
Async XLA Ops:
  0.0 68.5 %copy-start = (bf16[8,3,128,128]{3,2,1,0:T(8,128)(2,1)S(1)}, bf16[8,3,128,128]{3,2,1,0:T(8,128)(2,1)}, u32[]{:S(2)}) copy-start(bf16[8,3,128,128]{3,2,1,0:T(8,128)(2,1)} %param.5) | copy-start | bytes 2359300
  0.0 18.9 %copy-start.1 = (bf16[512,1024]{1,0:T(8,128)(2,1)S(1)}, bf16[512,1024]{1,0:T(8,128)(2,1)}, u32[]{:S(2)}) copy-start(bf16[512,1024]{1,0:T(8,128)(2,1)} %refs_0_.1) | copy-start | bytes 3145732
  1.2 10.8 %collective-permute-start.2 = (bf16[192,1024]{1,0:T(8,128)(2,1)S(1)}, bf16[192,1024]{1,0:T(8,128)(2,1)S(1)}, u32[]{:S(2)}, u32[]{:S(2)}) collective-permute-start(bf16[192,1024]{1,0:T(8,128)(2,1)S(1)} %slice.17), channel_id=1, source_target_pairs={{0,16},{16,0},{1,17},{17,1},{2,18},{18,2},{3,19},{19,3},{4,20},{20... | collective-permute-start | bytes 1179656 | tf_op jit(solution)/shard_map/ppermute | solution.py:235
  7.7 24.2 %collective-permute-start.3 = (bf16[176,1024]{1,0:T(8,128)(2,1)S(1)}, bf16[176,1024]{1,0:T(8,128)(2,1)S(1)}, u32[]{:S(2)}, u32[]{:S(2)}) collective-permute-start(bf16[176,1024]{1,0:T(8,128)(2,1)S(1)} %slice.18), channel_id=1, source_target_pairs={{0,16},{16,0},{1,17},{17,1},{2,18},{18,2},{3,19},{19,3},{4,20},{20... | collective-permute-start | bytes 1081352 | tf_op jit(solution)/shard_map/ppermute | solution.py:235
  12.0 32.0 %collective-permute-start.5 = (bf16[192,1024]{1,0:T(8,128)(2,1)S(1)}, bf16[192,1024]{1,0:T(8,128)(2,1)S(1)}, u32[]{:S(2)}, u32[]{:S(2)}) collective-permute-start(bf16[192,1024]{1,0:T(8,128)(2,1)S(1)} %collective-permute-done.2.refs_3_), channel_id=1, source_target_pairs={{0,32},{16,496},{32,64},{48,16},{64,96},{80,48},{96,128},{112,80},... | collective-permute-start | bytes 1179656 | tf_op jit(solution)/shard_map/ppermute | solution.py:249
  19.7 22.5 %collective-permute-start.4 = (bf16[144,1024]{1,0:T(8,128)(2,1)}, bf16[144,1024]{1,0:T(8,128)(2,1)}, u32[]{:S(2)}, u32[]{:S(2)}) collective-permute-start(bf16[144,1024]{1,0:T(8,128)(2,1)} %slice.19), channel_id=1, source_target_pairs={{0,16},{16,0},{1,17},{17,1},{2,18},{18,2},{3,19},{19,3},{4,20},{20... | collective-permute-start | bytes 884744 | tf_op jit(solution)/shard_map/ppermute | solution.py:235
  31.9 15.4 %collective-permute-start.7 = (bf16[176,1024]{1,0:T(8,128)(2,1)S(1)}, bf16[176,1024]{1,0:T(8,128)(2,1)S(1)}, u32[]{:S(2)}, u32[]{:S(2)}) collective-permute-start(bf16[176,1024]{1,0:T(8,128)(2,1)S(1)} %collective-permute-done.3.refs_4_), channel_id=1, source_target_pairs={{0,32},{16,496},{32,64},{48,16},{64,96},{80,48},{96,128},{112,80},... | collective-permute-start | bytes 1081352 | tf_op jit(solution)/shard_map/ppermute | solution.py:249
  34.9 23.0 %copy-start.2 = (s32[8,3]{0,1:T(4,128)S(1)}, s32[8,3]{0,1:T(4,128)}, u32[]{:S(2)}) copy-start(s32[8,3]{0,1:T(4,128)} %param.4) | copy-start | bytes 292
  34.9 15.1 %collective-permute-start = (bf16[256,1024]{1,0:T(8,128)(2,1)}, bf16[256,1024]{1,0:T(8,128)(2,1)}, u32[]{:S(2)}, u32[]{:S(2)}) collective-permute-start(bf16[256,1024]{1,0:T(8,128)(2,1)} %get-tuple-element.20), channel_id=1, source_target_pairs={{0,8},{8,0},{1,9},{9,1},{2,10},{10,2},{3,11},{11,3},{4,12},{12,4},... | collective-permute-start | bytes 1572872 | tf_op jit(solution)/shard_map/ppermute | solution.py:235
  40.2 17.8 %collective-permute-start.1 = (bf16[256,1024]{1,0:T(8,128)(2,1)}, bf16[256,1024]{1,0:T(8,128)(2,1)}, u32[]{:S(2)}, u32[]{:S(2)}) collective-permute-start(bf16[256,1024]{1,0:T(8,128)(2,1)} %get-tuple-element.19), channel_id=1, source_target_pairs={{0,8},{8,0},{1,9},{9,1},{2,10},{10,2},{3,11},{11,3},{4,12},{12,4},... | collective-permute-start | bytes 1572872 | tf_op jit(solution)/shard_map/ppermute | solution.py:235
  42.1 12.1 %collective-permute-start.10 = (bf16[144,1024]{1,0:T(8,128)(2,1)}, bf16[144,1024]{1,0:T(8,128)(2,1)}, u32[]{:S(2)}, u32[]{:S(2)}) collective-permute-start(bf16[144,1024]{1,0:T(8,128)(2,1)} %collective-permute-done.4.refs_5_), channel_id=1, source_target_pairs={{0,32},{16,496},{32,64},{48,16},{64,96},{80,48},{96,128},{112,80},... | collective-permute-start | bytes 884744 | tf_op jit(solution)/shard_map/ppermute | solution.py:249
  44.8 13.8 %collective-permute-start.6 = (bf16[192,1024]{1,0:T(8,128)(2,1)}, bf16[192,1024]{1,0:T(8,128)(2,1)}, u32[]{:S(2)}, u32[]{:S(2)}) collective-permute-start(bf16[192,1024]{1,0:T(8,128)(2,1)} %broadcast_select_fusion), channel_id=1, source_target_pairs={{0,8},{8,0},{1,9},{9,1},{2,10},{10,2},{3,11},{11,3},{4,12},{12,4},... | collective-permute-start | bytes 1179656 | tf_op jit(solution)/shard_map/ppermute | solution.py:235
  48.0 10.6 %collective-permute-start.8 = (bf16[176,1024]{1,0:T(8,128)(2,1)}, bf16[176,1024]{1,0:T(8,128)(2,1)}, u32[]{:S(2)}, u32[]{:S(2)}) collective-permute-start(bf16[176,1024]{1,0:T(8,128)(2,1)} %broadcast_select_fusion.1), channel_id=1, source_target_pairs={{0,8},{8,0},{1,9},{9,1},{2,10},{10,2},{3,11},{11,3},{4,12},{12,4},... | collective-permute-start | bytes 1081352 | tf_op jit(solution)/shard_map/ppermute | solution.py:235
  50.0 8.0 %collective-permute-start.9 = (bf16[144,1024]{1,0:T(8,128)(2,1)}, bf16[144,1024]{1,0:T(8,128)(2,1)}, u32[]{:S(2)}, u32[]{:S(2)}) collective-permute-start(bf16[144,1024]{1,0:T(8,128)(2,1)} %collective-permute-done.4.refs_5_), channel_id=1, source_target_pairs={{0,8},{24,16},{1,9},{25,17},{2,10},{26,18},{3,11},{27,19},{4,12},{... | collective-permute-start | bytes 884744 | tf_op jit(solution)/shard_map/ppermute | solution.py:240
  54.2 4.5 %collective-permute-start.11 = (bf16[144,1024]{1,0:T(8,128)(2,1)}, bf16[144,1024]{1,0:T(8,128)(2,1)}, u32[]{:S(2)}, u32[]{:S(2)}) collective-permute-start(bf16[144,1024]{1,0:T(8,128)(2,1)} %collective-permute-done.10.refs_12_), channel_id=1, source_target_pairs={{8,0},{16,24},{9,1},{17,25},{10,2},{18,26},{11,3},{19,27},{12,4},{... | collective-permute-start | bytes 884744 | tf_op jit(solution)/shard_map/ppermute | solution.py:240
  64.2 21.1 %all-to-all-start = ((bf16[8,592,128]{2,1,0:T(8,128)(2,1)}), bf16[8,592,128]{2,1,0:T(8,128)(2,1)S(1)}, u32[]{:S(2)}, u32[]{:S(2)}) async-start(bf16[8,592,128]{2,1,0:T(8,128)(2,1)} %gram_kernel.1), calls=%async_computation | async-start | bytes 2424832 | tf_op jit(solution)/shard_map/all_to_all | solution.py:272

commit v7 on v4

--- a/solution.py
+++ b/solution.py
@@ -13,7 +13,7 @@
 SIZES = (16, 2, 2, 4, 2)
 VAR_AXES = ("z", "xh", "core")
 SAMP_AXES = ("y", "xl")
-SIZES_OF_CHUNKS = (176, 176, 160)
+SIZES_OF_CHUNKS = (192, 192, 128)
 CHUNKS = len(SIZES_OF_CHUNKS)
 ROWB = 8
 K = 3
@@ -235,6 +235,15 @@
     return lax.ppermute(block, ("z", "xh"), route)
 
 
+def straight(block):
+    depth, wide = SIZES[0], SIZES[1]
+    route = []
+    for z in range(depth):
+        route.append((z * wide + 1, (z + 1) % depth * wide))
+        route.append((z * wide, (z - 1) % depth * wide + 1))
+    return lax.ppermute(block, ("z", "xh"), route)
+
+
 def body(observed, pattern, omega_init):
     z, xh, core = (lax.axis_index(a) for a in VAR_AXES)
     samp = lax.axis_index("y") * 2 + lax.axis_index("xl")
@@ -246,10 +255,12 @@
     source = jnp.where(offset == 0, 0, jnp.where(abs(offset) == 1, near, far)).astype(jnp.int32)
     column = (pattern % ROWB).astype(jnp.int32)
 
-    partner = swap(observed, "core")
     edges = [sum(SIZES_OF_CHUNKS[:i]) for i in range(CHUNKS + 1)]
-    across = [swap(observed[a:b], "xh") for a, b in zip(edges, edges[1:])]
-    beyond = [along_z(a) for a in across]
+    pieces = [observed[a:b] for a, b in zip(edges, edges[1:])]
+    across = [swap(a, "xh") for a in pieces]
+    beyond = [along_z(a) for a in across[:-1]] + [straight(pieces[-1])]
+    own, across[-1], beyond[-1] = lax.optimization_barrier((observed, across[-1], beyond[-1]))
+    partner = swap(own, "core")
     beside = [swap(jnp.where(core == xh, a, b), "core") for a, b in zip(across, beyond)]
     strips = [observed, partner, *across, *beside, *beyond]
     grams = on_strips(gram_kernel, (ROWB, GRAM_ROWS, BLK), [SMEM, SMEM], source, column, *strips)

time: 145 us -> 149 us (1.028)
  waiting for transfers between devices: 23.2 us -> 27.3 us
  starting transfers between devices: 50.8 us -> 48.4 us
    ppermute x0 -> x1, waiting for transfers between devices: none -> 4.97 us  [straight(): return lax.ppermute(block, ('z', 'xh'), route)]
    ppermute x7, starting transfers between devices: 36 us -> 32.3 us  [swap(): return lax.ppermute(block, axis, [(0, 1), (1, 0)])]
    ppermute x0 -> x1, starting transfers between devices: none -> 2.36 us  [straight(): return lax.ppermute(block, ('z', 'xh'), route)]
    ppermute x3 -> x2, waiting for transfers between devices: 1.95 us -> 0.01 us  [along_z(): return lax.ppermute(block, ('z', 'xh'), route)]
    unnamed x11 -> x19, local copies, waits for them, and re-layouts: 1.8 us -> 3.42 us
    ppermute x3 -> x2, starting transfers between devices: 10.6 us -> 9.56 us  [along_z(): return lax.ppermute(block, ('z', 'xh'), route)]
where the time goes in v7:
time: 149 us; the launch traced here: 148 us
  blocking collectives  58.2 us (39%)
  starting transfers between devices  48.4 us (32%)
  waiting for transfers between devices  27.3 us (18%)
  Pallas kernels  7.17 us (5%)
  local copies, waits for them, and re-layouts  4.75 us (3%)
  other arithmetic  2.35 us (2%)
    all_to_all x2, blocking collectives, everywhere(): return lax.all_to_all(rows, ('z', 'core'), 0, 0, tiled=True)  38.7 us
    ppermute x7, starting transfers between devices, swap(): return lax.ppermute(block, axis, [(0, 1), (1, 0)])  32.3 us
    all_to_all x2, blocking collectives, everywhere(): rows = lax.all_to_all(rows, ('xh', 'y', 'xl'), 0, 0, tiled=True)  19.6 us
    all_to_all x1, waiting for transfers between devices, body(): parts = lax.all_to_all(grams, SAMP_AXES, 0, 0, tiled=True)  17.2 us
    ppermute x2, starting transfers between devices, along_z(): return lax.ppermute(block, ('z', 'xh'), route)  9.56 us
    pallas_call x1, Pallas kernels, on_strips(): pl.pallas_call(kernel, out_shape=jax.ShapeDtypeStruct(shape, BF16), in_sp...  5.27 us
    ppermute x7, waiting for transfers between devices, swap(): return lax.ppermute(block, axis, [(0, 1), (1, 0)])  5.14 us
    ppermute x1, waiting for transfers between devices, straight(): return lax.ppermute(block, ('z', 'xh'), route)  4.97 us
  transfers between devices with their start and end apart: 11, of which 4 were waited for; matrix products, arithmetic and copies ran while one was open for 2% of the time, Pallas kernels for 0%

profile of v7, /device:TPU:1, one launch (start us, length us, event | category | flops | bytes accessed | tf_op | source)
XLA Modules:
  0.0 148.4 jit_solution(2700624304437627968)
XLA Ops:
  0.0 0.0 copy-start
  0.0 0.0 copy-start.1
  0.0 1.3 fusion.6
  1.3 5.5 %collective-permute-start.3 = (bf16[192,1024]{1,0:T(8,128)(2,1)S(1)}, bf16[192,1024]{1,0:T(8,128)(2,1)S(1)}, u32[]{:S(2)}, u32[]{:S(2)}) collective-permute-start(bf16[192,1024]{1,0:T(8,128)(2,1)S(1)} %get-tuple-element.26), channel_id=1, source_target_pairs={{0,16},{16,0},{1,17},{17,1},{2,18},{18,2},{3,19},{19,3},{4,20},{20... | collective-permute-start | bytes 1179656 | tf_op jit(solution)/shard_map/ppermute | solution.py:226
  6.8 1.9 %collective-permute-start.4 = (bf16[192,1024]{1,0:T(8,128)(2,1)S(1)}, bf16[192,1024]{1,0:T(8,128)(2,1)S(1)}, u32[]{:S(2)}, u32[]{:S(2)}) collective-permute-start(bf16[192,1024]{1,0:T(8,128)(2,1)S(1)} %get-tuple-element.25), channel_id=1, source_target_pairs={{0,16},{16,0},{1,17},{17,1},{2,18},{18,2},{3,19},{19,3},{4,20},{20... | collective-permute-start | bytes 1179656 | tf_op jit(solution)/shard_map/ppermute | solution.py:226
  8.7 3.4 %collective-permute-done.3.refs_2_ = bf16[192,1024]{1,0:T(8,128)(2,1)S(1)} collective-permute-done((bf16[192,1024]{1,0:T(8,128)(2,1)S(1)}, bf16[192,1024]{1,0:T(8,128)(2,1)S(1)}, u32[]{:S(2)}, u32[]{:S(2)}) %collective-permute-start.3) | collective-permute-done | bytes 393248 | tf_op jit(solution)/shard_map/ppermute | solution.py:226
  12.1 6.9 %collective-permute-start.5 = (bf16[192,1024]{1,0:T(8,128)(2,1)S(1)}, bf16[192,1024]{1,0:T(8,128)(2,1)S(1)}, u32[]{:S(2)}, u32[]{:S(2)}) collective-permute-start(bf16[192,1024]{1,0:T(8,128)(2,1)S(1)} %collective-permute-done.3.refs_2_), channel_id=1, source_target_pairs={{0,32},{16,496},{32,64},{48,16},{64,96},{80,48},{96,128},{112,80},... | collective-permute-start | bytes 1179656 | tf_op jit(solution)/shard_map/ppermute | solution.py:235
  19.1 0.0 copy-done.1
  19.1 12.2 %collective-permute-start = (bf16[128,1024]{1,0:T(8,128)(2,1)S(1)}, bf16[128,1024]{1,0:T(8,128)(2,1)S(1)}, u32[]{:S(2)}, u32[]{:S(2)}) collective-permute-start(bf16[128,1024]{1,0:T(8,128)(2,1)S(1)} %slice.9), channel_id=1, source_target_pairs={{0,16},{16,0},{1,17},{17,1},{2,18},{18,2},{3,19},{19,3},{4,20},{20... | collective-permute-start | bytes 786440 | tf_op jit(solution)/shard_map/ppermute | solution.py:226
  31.3 2.4 %collective-permute-start.1 = (bf16[128,1024]{1,0:T(8,128)(2,1)S(1)}, bf16[128,1024]{1,0:T(8,128)(2,1)S(1)}, u32[]{:S(2)}, u32[]{:S(2)}) collective-permute-start(bf16[128,1024]{1,0:T(8,128)(2,1)S(1)} %slice.9), channel_id=1, source_target_pairs={{16,32},{0,496},{48,64},{32,16},{80,96},{64,48},{112,128},{96,80},... | collective-permute-start | bytes 786440 | tf_op jit(solution)/shard_map/ppermute | solution.py:244
  33.7 0.0 collective-permute-done.4.refs_3_
  33.7 2.6 %collective-permute-start.7 = (bf16[192,1024]{1,0:T(8,128)(2,1)S(1)}, bf16[192,1024]{1,0:T(8,128)(2,1)S(1)}, u32[]{:S(2)}, u32[]{:S(2)}) collective-permute-start(bf16[192,1024]{1,0:T(8,128)(2,1)S(1)} %collective-permute-done.4.refs_3_), channel_id=1, source_target_pairs={{0,32},{16,496},{32,64},{48,16},{64,96},{80,48},{96,128},{112,80},... | collective-permute-start | bytes 1179656 | tf_op jit(solution)/shard_map/ppermute | solution.py:235
  36.4 0.0 collective-permute-done.refs_4_
  36.4 0.0 copy-start.2
  36.4 0.7 copy-done.2
  37.1 5.0 %collective-permute-done.1.refs_10_ = bf16[128,1024]{1,0:T(8,128)(2,1)S(1)} collective-permute-done((bf16[128,1024]{1,0:T(8,128)(2,1)S(1)}, bf16[128,1024]{1,0:T(8,128)(2,1)S(1)}, u32[]{:S(2)}, u32[]{:S(2)}) %collective-permute-start.1) | collective-permute-done | bytes 262176 | tf_op jit(solution)/shard_map/ppermute | solution.py:244
  42.1 0.0 copy-start.5
  42.1 0.7 copy-done.5
  42.8 6.3 %collective-permute-start.2 = (bf16[512,1024]{1,0:T(8,128)(2,1)S(1)}, bf16[512,1024]{1,0:T(8,128)(2,1)}, u32[]{:S(2)}, u32[]{:S(2)}) collective-permute-start(bf16[512,1024]{1,0:T(8,128)(2,1)S(1)} %copy-done.1), channel_id=1, source_target_pairs={{0,8},{8,0},{1,9},{9,1},{2,10},{10,2},{3,11},{11,3},{4,12},{12,4},... | collective-permute-start | bytes 3145736 | tf_op jit(solution)/shard_map/ppermute | solution.py:226
  49.1 0.0 copy-start.3
  49.1 0.0 copy-start.6
  49.1 0.0 collective-permute-done.5.refs_8_
  49.1 0.8 broadcast_select_fusion.1
  49.9 0.0 copy-start.8
  49.9 2.0 %collective-permute-start.6 = (bf16[192,1024]{1,0:T(8,128)(2,1)}, bf16[192,1024]{1,0:T(8,128)(2,1)}, u32[]{:S(2)}, u32[]{:S(2)}) collective-permute-start(bf16[192,1024]{1,0:T(8,128)(2,1)} %broadcast_select_fusion.1), channel_id=1, source_target_pairs={{0,8},{8,0},{1,9},{9,1},{2,10},{10,2},{3,11},{11,3},{4,12},{12,4},... | collective-permute-start | bytes 1179656 | tf_op jit(solution)/shard_map/ppermute | solution.py:226
  52.0 0.0 collective-permute-done.7.refs_9_
  52.0 0.8 broadcast_select_fusion
  52.8 2.4 %collective-permute-start.8 = (bf16[192,1024]{1,0:T(8,128)(2,1)}, bf16[192,1024]{1,0:T(8,128)(2,1)}, u32[]{:S(2)}, u32[]{:S(2)}) collective-permute-start(bf16[192,1024]{1,0:T(8,128)(2,1)} %broadcast_select_fusion), channel_id=1, source_target_pairs={{0,8},{8,0},{1,9},{9,1},{2,10},{10,2},{3,11},{11,3},{4,12},{12,4},... | collective-permute-start | bytes 1179656 | tf_op jit(solution)/shard_map/ppermute | solution.py:226
  55.2 0.0 copy-done.3
  55.2 0.0 copy-done.6
  55.2 0.7 broadcast_select_fusion.2
  55.9 1.9 %collective-permute-start.9 = (bf16[128,1024]{1,0:T(8,128)(2,1)}, bf16[128,1024]{1,0:T(8,128)(2,1)}, u32[]{:S(2)}, u32[]{:S(2)}) collective-permute-start(bf16[128,1024]{1,0:T(8,128)(2,1)} %broadcast_select_fusion.2), channel_id=1, source_target_pairs={{0,8},{8,0},{1,9},{9,1},{2,10},{10,2},{3,11},{11,3},{4,12},{12,4},... | collective-permute-start | bytes 786440 | tf_op jit(solution)/shard_map/ppermute | solution.py:226
  57.9 0.0 copy-done.8
  57.9 0.1 copy.8
  58.0 1.7 %collective-permute-done.9.refs_7_ = bf16[128,1024]{1,0:T(8,128)(2,1)} collective-permute-done((bf16[128,1024]{1,0:T(8,128)(2,1)}, bf16[128,1024]{1,0:T(8,128)(2,1)}, u32[]{:S(2)}, u32[]{:S(2)}) %collective-permute-start.9) | collective-permute-done | bytes 262176 | tf_op jit(solution)/shard_map/ppermute | solution.py:226
  59.7 0.0 collective-permute-done.6.refs_5_
  59.7 0.0 collective-permute-done.8.refs_6_
  59.7 0.0 collective-permute-done.2.refs_1_
  59.7 0.0 copy-start.4
  59.7 0.9 copy-done.4
  60.7 0.0 copy-start.7
  60.7 0.9 copy-done.7
  61.6 5.3 %gram_kernel.1 = bf16[8,592,128]{2,1,0:T(8,128)(2,1)} custom-call(s32[8,3]{1,0:T(8,128)S(1)} %get-tuple-element.28.source, s32[8,3]{1,0:T(8,128)S(1)} %get-tuple-element.27.column, bf16[512,1024]{1,0:T(8,128)(2,1)S(1)} %copy-done.1, bf16[512,1024]{1,0:T(8,128)(2,1)} %collective-permute-done.2.refs_1_, bf16[192,1024]{1,0:T(8,128)(2,1)S(1)} %collective-permute-done.3.refs_2_, ...), custom_call_target="tpu_custom_call" | custom-call | flops 805306368 | bytes 6291456 | tf_op jit(solution)/shard_map/gram_kernel/pallas_call | solution.py:107
  66.9 4.2 %all-to-all-start = ((bf16[8,592,128]{2,1,0:T(8,128)(2,1)}), bf16[8,592,128]{2,1,0:T(8,128)(2,1)S(1)}, u32[]{:S(2)}, u32[]{:S(2)}) async-start(bf16[8,592,128]{2,1,0:T(8,128)(2,1)} %gram_kernel.1), calls=%async_computation | async-start | bytes 2424832 | tf_op jit(solution)/shard_map/all_to_all | solution.py:267
  71.1 0.0 copy-done
  71.1 17.2 %all-to-all-done.parts = bf16[8,592,128]{2,1,0:T(8,128)(2,1)S(1)} async-done(((bf16[8,592,128]{2,1,0:T(8,128)(2,1)}), bf16[8,592,128]{2,1,0:T(8,128)(2,1)S(1)}, u32[]{:S(2)}, u32[]{:S(2)}) %all-to-all-start) | async-done | bytes 1212448 | tf_op jit(solution)/shard_map/all_to_all | solution.py:267
  88.3 0.6 first_kernel.1
  88.8 10.5 %all_to_all.49 = f32[16,1,128]{2,1,0:T(1,128)S(1)} all-to-all(f32[16,1,128]{2,1,0:T(1,128)S(1)} %bitcast.26), channel_id=1, replica_groups=mesh['z'=16,'xh'=2,'core'=2,'y'=4,'xl'=2] {'xh','y','xl'}, dimensions={0} | all-to-all | bytes 16384 | tf_op jit(solution)/shard_map/all_to_all | solution.py:220
  99.3 21.8 %all_to_all.50 = f32[32,1,128]{2,1,0:T(1,128)S(1)} all-to-all(f32[32,1,128]{2,1,0:T(1,128)S(1)} %bitcast.21), channel_id=1, replica_groups=mesh['z'=16,'xh'=2,'core'=2,'y'=4,'xl'=2] {'z','core'}, dimensions={0} | all-to-all | bytes 32768 | tf_op jit(solution)/shard_map/all_to_all | solution.py:222
  121.2 0.5 second_kernel.1
  121.6 9.1 %all_to_all.51 = f32[16,1,128]{2,1,0:T(1,128)S(1)} all-to-all(f32[16,1,128]{2,1,0:T(1,128)S(1)} %bitcast.25), channel_id=1, replica_groups=mesh['z'=16,'xh'=2,'core'=2,'y'=4,'xl'=2] {'xh','y','xl'}, dimensions={0} | all-to-all | bytes 16384 | tf_op jit(solution)/shard_map/all_to_all | solution.py:220
  130.7 16.8 %all_to_all.52 = f32[32,1,128]{2,1,0:T(1,128)S(1)} all-to-all(f32[32,1,128]{2,1,0:T(1,128)S(1)} %bitcast.22), channel_id=1, replica_groups=mesh['z'=16,'xh'=2,'core'=2,'y'=4,'xl'=2] {'z','core'}, dimensions={0} | all-to-all | bytes 32768 | tf_op jit(solution)/shard_map/all_to_all | solution.py:222
  147.6 0.9 last_kernel.1
  (5 shorter events, 0.1 us)
Async XLA Ops:
  0.0 71.1 %copy-start = (bf16[8,3,128,128]{3,2,1,0:T(8,128)(2,1)S(1)}, bf16[8,3,128,128]{3,2,1,0:T(8,128)(2,1)}, u32[]{:S(2)}) copy-start(bf16[8,3,128,128]{3,2,1,0:T(8,128)(2,1)} %param.5) | copy-start | bytes 2359300
  0.0 19.1 %copy-start.1 = (bf16[512,1024]{1,0:T(8,128)(2,1)S(1)}, bf16[512,1024]{1,0:T(8,128)(2,1)}, u32[]{:S(2)}) copy-start(bf16[512,1024]{1,0:T(8,128)(2,1)} %refs_0_.1) | copy-start | bytes 3145732
  1.3 10.8 %collective-permute-start.3 = (bf16[192,1024]{1,0:T(8,128)(2,1)S(1)}, bf16[192,1024]{1,0:T(8,128)(2,1)S(1)}, u32[]{:S(2)}, u32[]{:S(2)}) collective-permute-start(bf16[192,1024]{1,0:T(8,128)(2,1)S(1)} %get-tuple-element.26), channel_id=1, source_target_pairs={{0,16},{16,0},{1,17},{17,1},{2,18},{18,2},{3,19},{19,3},{4,20},{20... | collective-permute-start | bytes 1179656 | tf_op jit(solution)/shard_map/ppermute | solution.py:226
  6.8 26.9 %collective-permute-start.4 = (bf16[192,1024]{1,0:T(8,128)(2,1)S(1)}, bf16[192,1024]{1,0:T(8,128)(2,1)S(1)}, u32[]{:S(2)}, u32[]{:S(2)}) collective-permute-start(bf16[192,1024]{1,0:T(8,128)(2,1)S(1)} %get-tuple-element.25), channel_id=1, source_target_pairs={{0,16},{16,0},{1,17},{17,1},{2,18},{18,2},{3,19},{19,3},{4,20},{20... | collective-permute-start | bytes 1179656 | tf_op jit(solution)/shard_map/ppermute | solution.py:226
  12.1 37.0 %collective-permute-start.5 = (bf16[192,1024]{1,0:T(8,128)(2,1)S(1)}, bf16[192,1024]{1,0:T(8,128)(2,1)S(1)}, u32[]{:S(2)}, u32[]{:S(2)}) collective-permute-start(bf16[192,1024]{1,0:T(8,128)(2,1)S(1)} %collective-permute-done.3.refs_2_), channel_id=1, source_target_pairs={{0,32},{16,496},{32,64},{48,16},{64,96},{80,48},{96,128},{112,80},... | collective-permute-start | bytes 1179656 | tf_op jit(solution)/shard_map/ppermute | solution.py:235
  19.1 17.3 %collective-permute-start = (bf16[128,1024]{1,0:T(8,128)(2,1)S(1)}, bf16[128,1024]{1,0:T(8,128)(2,1)S(1)}, u32[]{:S(2)}, u32[]{:S(2)}) collective-permute-start(bf16[128,1024]{1,0:T(8,128)(2,1)S(1)} %slice.9), channel_id=1, source_target_pairs={{0,16},{16,0},{1,17},{17,1},{2,18},{18,2},{3,19},{19,3},{4,20},{20... | collective-permute-start | bytes 786440 | tf_op jit(solution)/shard_map/ppermute | solution.py:226
  31.3 10.7 %collective-permute-start.1 = (bf16[128,1024]{1,0:T(8,128)(2,1)S(1)}, bf16[128,1024]{1,0:T(8,128)(2,1)S(1)}, u32[]{:S(2)}, u32[]{:S(2)}) collective-permute-start(bf16[128,1024]{1,0:T(8,128)(2,1)S(1)} %slice.9), channel_id=1, source_target_pairs={{16,32},{0,496},{48,64},{32,16},{80,96},{64,48},{112,128},{96,80},... | collective-permute-start | bytes 786440 | tf_op jit(solution)/shard_map/ppermute | solution.py:244
  33.7 18.3 %collective-permute-start.7 = (bf16[192,1024]{1,0:T(8,128)(2,1)S(1)}, bf16[192,1024]{1,0:T(8,128)(2,1)S(1)}, u32[]{:S(2)}, u32[]{:S(2)}) collective-permute-start(bf16[192,1024]{1,0:T(8,128)(2,1)S(1)} %collective-permute-done.4.refs_3_), channel_id=1, source_target_pairs={{0,32},{16,496},{32,64},{48,16},{64,96},{80,48},{96,128},{112,80},... | collective-permute-start | bytes 1179656 | tf_op jit(solution)/shard_map/ppermute | solution.py:235
  36.4 0.7 copy-start.2
  42.1 0.7 copy-start.5
  42.8 16.9 %collective-permute-start.2 = (bf16[512,1024]{1,0:T(8,128)(2,1)S(1)}, bf16[512,1024]{1,0:T(8,128)(2,1)}, u32[]{:S(2)}, u32[]{:S(2)}) collective-permute-start(bf16[512,1024]{1,0:T(8,128)(2,1)S(1)} %copy-done.1), channel_id=1, source_target_pairs={{0,8},{8,0},{1,9},{9,1},{2,10},{10,2},{3,11},{11,3},{4,12},{12,4},... | collective-permute-start | bytes 3145736 | tf_op jit(solution)/shard_map/ppermute | solution.py:226
  49.1 6.1 %copy-start.3 = (bf16[128,1024]{1,0:T(8,128)(2,1)S(1)}, bf16[128,1024]{1,0:T(8,128)(2,1)}, u32[]{:S(2)}) copy-start(bf16[128,1024]{1,0:T(8,128)(2,1)} %copy-done.2) | copy-start | bytes 786436
  49.1 6.1 %copy-start.6 = (bf16[128,1024]{1,0:T(8,128)(2,1)S(1)}, bf16[128,1024]{1,0:T(8,128)(2,1)}, u32[]{:S(2)}) copy-start(bf16[128,1024]{1,0:T(8,128)(2,1)} %copy-done.5) | copy-start | bytes 786436
  49.9 7.9 %copy-start.8 = (s32[8,3]{0,1:T(4,128)S(1)}, s32[8,3]{0,1:T(4,128)}, u32[]{:S(2)}) copy-start(s32[8,3]{0,1:T(4,128)} %param.4) | copy-start | bytes 292
  49.9 9.8 %collective-permute-start.6 = (bf16[192,1024]{1,0:T(8,128)(2,1)}, bf16[192,1024]{1,0:T(8,128)(2,1)}, u32[]{:S(2)}, u32[]{:S(2)}) collective-permute-start(bf16[192,1024]{1,0:T(8,128)(2,1)} %broadcast_select_fusion.1), channel_id=1, source_target_pairs={{0,8},{8,0},{1,9},{9,1},{2,10},{10,2},{3,11},{11,3},{4,12},{12,4},... | collective-permute-start | bytes 1179656 | tf_op jit(solution)/shard_map/ppermute | solution.py:226
  52.8 6.9 %collective-permute-start.8 = (bf16[192,1024]{1,0:T(8,128)(2,1)}, bf16[192,1024]{1,0:T(8,128)(2,1)}, u32[]{:S(2)}, u32[]{:S(2)}) collective-permute-start(bf16[192,1024]{1,0:T(8,128)(2,1)} %broadcast_select_fusion), channel_id=1, source_target_pairs={{0,8},{8,0},{1,9},{9,1},{2,10},{10,2},{3,11},{11,3},{4,12},{12,4},... | collective-permute-start | bytes 1179656 | tf_op jit(solution)/shard_map/ppermute | solution.py:226
  55.9 3.8 %collective-permute-start.9 = (bf16[128,1024]{1,0:T(8,128)(2,1)}, bf16[128,1024]{1,0:T(8,128)(2,1)}, u32[]{:S(2)}, u32[]{:S(2)}) collective-permute-start(bf16[128,1024]{1,0:T(8,128)(2,1)} %broadcast_select_fusion.2), channel_id=1, source_target_pairs={{0,8},{8,0},{1,9},{9,1},{2,10},{10,2},{3,11},{11,3},{4,12},{12,4},... | collective-permute-start | bytes 786440 | tf_op jit(solution)/shard_map/ppermute | solution.py:226
  59.7 1.0 copy-start.4
  60.7 0.9 copy-start.7
  66.9 21.4 %all-to-all-start = ((bf16[8,592,128]{2,1,0:T(8,128)(2,1)}), bf16[8,592,128]{2,1,0:T(8,128)(2,1)S(1)}, u32[]{:S(2)}, u32[]{:S(2)}) async-start(bf16[8,592,128]{2,1,0:T(8,128)(2,1)} %gram_kernel.1), calls=%async_computation | async-start | bytes 2424832 | tf_op jit(solution)/shard_map/all_to_all | solution.py:267

commit v8 on v7

--- a/solution.py
+++ b/solution.py
@@ -13,7 +13,7 @@
 SIZES = (16, 2, 2, 4, 2)
 VAR_AXES = ("z", "xh", "core")
 SAMP_AXES = ("y", "xl")
-SIZES_OF_CHUNKS = (192, 192, 128)
+SIZES_OF_CHUNKS = (128, 192, 192)
 CHUNKS = len(SIZES_OF_CHUNKS)
 ROWB = 8
 K = 3
@@ -73,7 +73,7 @@
 def gram_kernel(source, column, *refs):
     *strips, out, held = refs
     inputs = [strips[:1], strips[1:2]]
-    inputs += [strips[2 + CHUNKS * i : 2 + CHUNKS * (i + 1)] for i in range(3)]
+    inputs += [strips[a:b] for a, b in ((2, 5), (5, 7), (7, 10))]
     choose(inputs, held, source, column)
     row, col = diagonal_mask()
     line = lax.broadcasted_iota(jnp.int32, (16, BLK), 0)
@@ -257,11 +257,14 @@
 
     edges = [sum(SIZES_OF_CHUNKS[:i]) for i in range(CHUNKS + 1)]
     pieces = [observed[a:b] for a, b in zip(edges, edges[1:])]
+    partner = swap(observed, "core")
     across = [swap(a, "xh") for a in pieces]
-    beyond = [along_z(a) for a in across[:-1]] + [straight(pieces[-1])]
-    own, across[-1], beyond[-1] = lax.optimization_barrier((observed, across[-1], beyond[-1]))
-    partner = swap(own, "core")
-    beside = [swap(jnp.where(core == xh, a, b), "core") for a, b in zip(across, beyond)]
+    beyond = [straight(pieces[0])] + [along_z(a) for a in across[1:]]
+    here, there = jnp.concatenate(across[:2]), jnp.concatenate(beyond[:2])
+    beside = [
+        swap(jnp.where(core == xh, here, there), "core"),
+        swap(jnp.where(core == xh, across[2], beyond[2]), "core"),
+    ]
     strips = [observed, partner, *across, *beside, *beyond]
     grams = on_strips(gram_kernel, (ROWB, GRAM_ROWS, BLK), [SMEM, SMEM], source, column, *strips)
     parts = lax.all_to_all(grams, SAMP_AXES, 0, 0, tiled=True)

time: 149 us -> 147 us (0.987)
  waiting for transfers between devices: 27.3 us -> 30.8 us
  starting transfers between devices: 48.4 us -> 45.6 us
  local copies, waits for them, and re-layouts: 4.75 us -> 2.12 us
    ppermute x7 -> x6, waiting for transfers between devices: 5.14 us -> 11.9 us  [swap(): return lax.ppermute(block, axis, [(0, 1), (1, 0)])]
    unnamed x19 -> x7, local copies, waits for them, and re-layouts: 3.42 us -> 0.1 us
    ppermute x1, waiting for transfers between devices: 4.97 us -> 1.79 us  [straight(): return lax.ppermute(block, ('z', 'xh'), route)]
    ppermute x7 -> x6, starting transfers between devices: 32.3 us -> 29.4 us  [swap(): return lax.ppermute(block, axis, [(0, 1), (1, 0)])]
  transfers between devices with their start and end apart: 11 -> 10, of which waited for: 4 -> 5; matrix products, arithmetic and copies ran while one was open for 2% -> 3% of each run, Pallas kernels for 0% -> 0%
where the time goes in v8:
time: 147 us; the launch traced here: 146 us
  blocking collectives  57.2 us (39%)
  starting transfers between devices  45.6 us (31%)
  waiting for transfers between devices  30.8 us (21%)
  Pallas kernels  7.33 us (5%)
  other arithmetic  2.95 us (2%)
  local copies, waits for them, and re-layouts  2.12 us (1%)
    all_to_all x2, blocking collectives, everywhere(): return lax.all_to_all(rows, ('z', 'core'), 0, 0, tiled=True)  37.4 us
    ppermute x6, starting transfers between devices, swap(): return lax.ppermute(block, axis, [(0, 1), (1, 0)])  29.4 us
    all_to_all x2, blocking collectives, everywhere(): rows = lax.all_to_all(rows, ('xh', 'y', 'xl'), 0, 0, tiled=True)  19.8 us
    all_to_all x1, waiting for transfers between devices, body(): parts = lax.all_to_all(grams, SAMP_AXES, 0, 0, tiled=True)  17.2 us
    ppermute x6, waiting for transfers between devices, swap(): return lax.ppermute(block, axis, [(0, 1), (1, 0)])  11.9 us
    ppermute x2, starting transfers between devices, along_z(): return lax.ppermute(block, ('z', 'xh'), route)  9.56 us
    pallas_call x1, Pallas kernels, on_strips(): pl.pallas_call(kernel, out_shape=jax.ShapeDtypeStruct(shape, BF16), in_sp...  5.43 us
    all_to_all x1, starting transfers between devices, body(): parts = lax.all_to_all(grams, SAMP_AXES, 0, 0, tiled=True)  4.22 us
  transfers between devices with their start and end apart: 10, of which 5 were waited for; matrix products, arithmetic and copies ran while one was open for 3% of the time, Pallas kernels for 0%

profile of v8, /device:TPU:1, one launch (start us, length us, event | category | flops | bytes accessed | tf_op | source)
XLA Modules:
  0.0 146.2 jit_solution(815729400037660881)
XLA Ops:
  0.0 0.0 copy-start
  0.0 0.0 copy-start.1
  0.0 1.3 fusion.6
  1.3 5.5 %collective-permute-start.2 = (bf16[192,1024]{1,0:T(8,128)(2,1)S(1)}, bf16[192,1024]{1,0:T(8,128)(2,1)S(1)}, u32[]{:S(2)}, u32[]{:S(2)}) collective-permute-start(bf16[192,1024]{1,0:T(8,128)(2,1)S(1)} %get-tuple-element.20), channel_id=1, source_target_pairs={{0,16},{16,0},{1,17},{17,1},{2,18},{18,2},{3,19},{19,3},{4,20},{20... | collective-permute-start | bytes 1179656 | tf_op jit(solution)/shard_map/ppermute | solution.py:226
  6.8 1.9 %collective-permute-start.3 = (bf16[192,1024]{1,0:T(8,128)(2,1)S(1)}, bf16[192,1024]{1,0:T(8,128)(2,1)S(1)}, u32[]{:S(2)}, u32[]{:S(2)}) collective-permute-start(bf16[192,1024]{1,0:T(8,128)(2,1)S(1)} %get-tuple-element.19), channel_id=1, source_target_pairs={{0,16},{16,0},{1,17},{17,1},{2,18},{18,2},{3,19},{19,3},{4,20},{20... | collective-permute-start | bytes 1179656 | tf_op jit(solution)/shard_map/ppermute | solution.py:226
  8.7 3.4 %collective-permute-done.2.refs_3_ = bf16[192,1024]{1,0:T(8,128)(2,1)S(1)} collective-permute-done((bf16[192,1024]{1,0:T(8,128)(2,1)S(1)}, bf16[192,1024]{1,0:T(8,128)(2,1)S(1)}, u32[]{:S(2)}, u32[]{:S(2)}) %collective-permute-start.2) | collective-permute-done | bytes 393248 | tf_op jit(solution)/shard_map/ppermute | solution.py:226
  12.1 6.9 %collective-permute-start.5 = (bf16[192,1024]{1,0:T(8,128)(2,1)S(1)}, bf16[192,1024]{1,0:T(8,128)(2,1)S(1)}, u32[]{:S(2)}, u32[]{:S(2)}) collective-permute-start(bf16[192,1024]{1,0:T(8,128)(2,1)S(1)} %collective-permute-done.2.refs_3_), channel_id=1, source_target_pairs={{0,32},{16,496},{32,64},{48,16},{64,96},{80,48},{96,128},{112,80},... | collective-permute-start | bytes 1179656 | tf_op jit(solution)/shard_map/ppermute | solution.py:235
  19.1 0.0 copy-done.1
  19.1 6.5 %collective-permute-start = (bf16[512,1024]{1,0:T(8,128)(2,1)S(1)}, bf16[512,1024]{1,0:T(8,128)(2,1)}, u32[]{:S(2)}, u32[]{:S(2)}) collective-permute-start(bf16[512,1024]{1,0:T(8,128)(2,1)S(1)} %copy-done.1), channel_id=1, source_target_pairs={{0,8},{8,0},{1,9},{9,1},{2,10},{10,2},{3,11},{11,3},{4,12},{12,4},... | collective-permute-start | bytes 3145736 | tf_op jit(solution)/shard_map/ppermute | solution.py:226
  25.6 0.7 slice.9
  26.3 10.6 %collective-permute-start.1 = (bf16[128,1024]{1,0:T(8,128)(2,1)}, bf16[128,1024]{1,0:T(8,128)(2,1)}, u32[]{:S(2)}, u32[]{:S(2)}) collective-permute-start(bf16[128,1024]{1,0:T(8,128)(2,1)} %slice.9), channel_id=1, source_target_pairs={{0,16},{16,0},{1,17},{17,1},{2,18},{18,2},{3,19},{19,3},{4,20},{20... | collective-permute-start | bytes 786440 | tf_op jit(solution)/shard_map/ppermute | solution.py:226
  36.9 2.4 %collective-permute-start.4 = (bf16[128,1024]{1,0:T(8,128)(2,1)}, bf16[128,1024]{1,0:T(8,128)(2,1)}, u32[]{:S(2)}, u32[]{:S(2)}) collective-permute-start(bf16[128,1024]{1,0:T(8,128)(2,1)} %slice.9), channel_id=1, source_target_pairs={{16,32},{0,496},{48,64},{32,16},{80,96},{64,48},{112,128},{96,80},... | collective-permute-start | bytes 786440 | tf_op jit(solution)/shard_map/ppermute | solution.py:244
  39.3 0.0 collective-permute-done.3.refs_4_
  39.3 2.6 %collective-permute-start.7 = (bf16[192,1024]{1,0:T(8,128)(2,1)S(1)}, bf16[192,1024]{1,0:T(8,128)(2,1)S(1)}, u32[]{:S(2)}, u32[]{:S(2)}) collective-permute-start(bf16[192,1024]{1,0:T(8,128)(2,1)S(1)} %collective-permute-done.3.refs_4_), channel_id=1, source_target_pairs={{0,32},{16,496},{32,64},{48,16},{64,96},{80,48},{96,128},{112,80},... | collective-permute-start | bytes 1179656 | tf_op jit(solution)/shard_map/ppermute | solution.py:235
  41.9 0.0 copy-start.2
  42.0 6.6 %collective-permute-done.1.refs_2_ = bf16[128,1024]{1,0:T(8,128)(2,1)} collective-permute-done((bf16[128,1024]{1,0:T(8,128)(2,1)}, bf16[128,1024]{1,0:T(8,128)(2,1)}, u32[]{:S(2)}, u32[]{:S(2)}) %collective-permute-start.1) | collective-permute-done | bytes 262176 | tf_op jit(solution)/shard_map/ppermute | solution.py:226
  48.5 1.8 %collective-permute-done.4.refs_7_ = bf16[128,1024]{1,0:T(8,128)(2,1)} collective-permute-done((bf16[128,1024]{1,0:T(8,128)(2,1)}, bf16[128,1024]{1,0:T(8,128)(2,1)}, u32[]{:S(2)}, u32[]{:S(2)}) %collective-permute-start.4) | collective-permute-done | bytes 262176 | tf_op jit(solution)/shard_map/ppermute | solution.py:244
  50.3 0.0 collective-permute-done.5.refs_8_
  50.3 2.1 %maximum_select_fusion = bf16[320,1024]{1,0:T(8,128)(2,1)} fusion(bf16[192,1024]{1,0:T(8,128)(2,1)S(1)} %collective-permute-done.2.refs_3_, bf16[128,1024]{1,0:T(8,128)(2,1)} %collective-permute-done.1.refs_2_, bf16[192,1024]{1,0:T(8,128)(2,1)S(1)} %collective-permute-done.5.refs_8_, bf16[128,1024]{1,0:T(8,128)(2,1)} %collective-permute-done.4.refs_7_, pred[]{:T(512)S(6)} %eq.47), kind=kLoop, calls=%fused_computation | loop fusion | flops 2949120 | bytes 1966081 | tf_op jit(solution)/shard_map/jit(_where)/select_n | solution.py:265
  52.5 3.0 %collective-permute-start.6 = (bf16[320,1024]{1,0:T(8,128)(2,1)}, bf16[320,1024]{1,0:T(8,128)(2,1)}, u32[]{:S(2)}, u32[]{:S(2)}) collective-permute-start(bf16[320,1024]{1,0:T(8,128)(2,1)} %maximum_select_fusion), channel_id=1, source_target_pairs={{0,8},{8,0},{1,9},{9,1},{2,10},{10,2},{3,11},{11,3},{4,12},{12,4},... | collective-permute-start | bytes 1966088 | tf_op jit(solution)/shard_map/ppermute | solution.py:226
  55.5 0.0 collective-permute-done.7.refs_9_
  55.5 0.8 broadcast_select_fusion
  56.3 1.9 %collective-permute-start.8 = (bf16[192,1024]{1,0:T(8,128)(2,1)}, bf16[192,1024]{1,0:T(8,128)(2,1)}, u32[]{:S(2)}, u32[]{:S(2)}) collective-permute-start(bf16[192,1024]{1,0:T(8,128)(2,1)} %broadcast_select_fusion), channel_id=1, source_target_pairs={{0,8},{8,0},{1,9},{9,1},{2,10},{10,2},{3,11},{11,3},{4,12},{12,4},... | collective-permute-start | bytes 1179656 | tf_op jit(solution)/shard_map/ppermute | solution.py:226
  58.2 0.0 copy-done.2
  58.2 0.1 copy.8
  58.3 0.0 collective-permute-done.refs_1_
  58.4 1.9 %collective-permute-done.8.refs_6_ = bf16[192,1024]{1,0:T(8,128)(2,1)} collective-permute-done((bf16[192,1024]{1,0:T(8,128)(2,1)}, bf16[192,1024]{1,0:T(8,128)(2,1)}, u32[]{:S(2)}, u32[]{:S(2)}) %collective-permute-start.8) | collective-permute-done | bytes 393248 | tf_op jit(solution)/shard_map/ppermute | solution.py:226
  60.2 0.0 collective-permute-done.6.refs_5_
  60.2 5.4 %gram_kernel.1 = bf16[8,592,128]{2,1,0:T(8,128)(2,1)} custom-call(s32[8,3]{1,0:T(8,128)S(1)} %get-tuple-element.22.source, s32[8,3]{1,0:T(8,128)S(1)} %get-tuple-element.21.column, bf16[512,1024]{1,0:T(8,128)(2,1)S(1)} %copy-done.1, bf16[512,1024]{1,0:T(8,128)(2,1)} %collective-permute-done.refs_1_, bf16[128,1024]{1,0:T(8,128)(2,1)} %collective-permute-done.1.refs_2_, ...), custom_call_target="tpu_custom_call" | custom-call | flops 805306368 | bytes 6291456 | tf_op jit(solution)/shard_map/gram_kernel/pallas_call | solution.py:107
  65.7 4.2 %all-to-all-start = ((bf16[8,592,128]{2,1,0:T(8,128)(2,1)}), bf16[8,592,128]{2,1,0:T(8,128)(2,1)S(1)}, u32[]{:S(2)}, u32[]{:S(2)}) async-start(bf16[8,592,128]{2,1,0:T(8,128)(2,1)} %gram_kernel.1), calls=%async_computation | async-start | bytes 2424832 | tf_op jit(solution)/shard_map/all_to_all | solution.py:270
  69.9 0.0 copy-done
  69.9 17.2 %all-to-all-done.parts = bf16[8,592,128]{2,1,0:T(8,128)(2,1)S(1)} async-done(((bf16[8,592,128]{2,1,0:T(8,128)(2,1)}), bf16[8,592,128]{2,1,0:T(8,128)(2,1)S(1)}, u32[]{:S(2)}, u32[]{:S(2)}) %all-to-all-start) | async-done | bytes 1212448 | tf_op jit(solution)/shard_map/all_to_all | solution.py:270
  87.1 0.6 first_kernel.1
  87.6 10.6 %all_to_all.49 = f32[16,1,128]{2,1,0:T(1,128)S(1)} all-to-all(f32[16,1,128]{2,1,0:T(1,128)S(1)} %bitcast.26), channel_id=1, replica_groups=mesh['z'=16,'xh'=2,'core'=2,'y'=4,'xl'=2] {'xh','y','xl'}, dimensions={0} | all-to-all | bytes 16384 | tf_op jit(solution)/shard_map/all_to_all | solution.py:220
  98.3 20.6 %all_to_all.50 = f32[32,1,128]{2,1,0:T(1,128)S(1)} all-to-all(f32[32,1,128]{2,1,0:T(1,128)S(1)} %bitcast.21), channel_id=1, replica_groups=mesh['z'=16,'xh'=2,'core'=2,'y'=4,'xl'=2] {'z','core'}, dimensions={0} | all-to-all | bytes 32768 | tf_op jit(solution)/shard_map/all_to_all | solution.py:222
  118.9 0.5 second_kernel.1
  119.3 9.1 %all_to_all.51 = f32[16,1,128]{2,1,0:T(1,128)S(1)} all-to-all(f32[16,1,128]{2,1,0:T(1,128)S(1)} %bitcast.25), channel_id=1, replica_groups=mesh['z'=16,'xh'=2,'core'=2,'y'=4,'xl'=2] {'xh','y','xl'}, dimensions={0} | all-to-all | bytes 16384 | tf_op jit(solution)/shard_map/all_to_all | solution.py:220
  128.5 16.8 %all_to_all.52 = f32[32,1,128]{2,1,0:T(1,128)S(1)} all-to-all(f32[32,1,128]{2,1,0:T(1,128)S(1)} %bitcast.22), channel_id=1, replica_groups=mesh['z'=16,'xh'=2,'core'=2,'y'=4,'xl'=2] {'z','core'}, dimensions={0} | all-to-all | bytes 32768 | tf_op jit(solution)/shard_map/all_to_all | solution.py:222
  145.3 0.9 last_kernel.1
  (4 shorter events, 0.1 us)
Async XLA Ops:
  0.0 69.9 %copy-start = (bf16[8,3,128,128]{3,2,1,0:T(8,128)(2,1)S(1)}, bf16[8,3,128,128]{3,2,1,0:T(8,128)(2,1)}, u32[]{:S(2)}) copy-start(bf16[8,3,128,128]{3,2,1,0:T(8,128)(2,1)} %param.5) | copy-start | bytes 2359300
  0.0 19.1 %copy-start.1 = (bf16[512,1024]{1,0:T(8,128)(2,1)S(1)}, bf16[512,1024]{1,0:T(8,128)(2,1)}, u32[]{:S(2)}) copy-start(bf16[512,1024]{1,0:T(8,128)(2,1)} %refs_0_.1) | copy-start | bytes 3145732
  1.3 10.8 %collective-permute-start.2 = (bf16[192,1024]{1,0:T(8,128)(2,1)S(1)}, bf16[192,1024]{1,0:T(8,128)(2,1)S(1)}, u32[]{:S(2)}, u32[]{:S(2)}) collective-permute-start(bf16[192,1024]{1,0:T(8,128)(2,1)S(1)} %get-tuple-element.20), channel_id=1, source_target_pairs={{0,16},{16,0},{1,17},{17,1},{2,18},{18,2},{3,19},{19,3},{4,20},{20... | collective-permute-start | bytes 1179656 | tf_op jit(solution)/shard_map/ppermute | solution.py:226
  6.8 32.5 %collective-permute-start.3 = (bf16[192,1024]{1,0:T(8,128)(2,1)S(1)}, bf16[192,1024]{1,0:T(8,128)(2,1)S(1)}, u32[]{:S(2)}, u32[]{:S(2)}) collective-permute-start(bf16[192,1024]{1,0:T(8,128)(2,1)S(1)} %get-tuple-element.19), channel_id=1, source_target_pairs={{0,16},{16,0},{1,17},{17,1},{2,18},{18,2},{3,19},{19,3},{4,20},{20... | collective-permute-start | bytes 1179656 | tf_op jit(solution)/shard_map/ppermute | solution.py:226
  12.1 38.2 %collective-permute-start.5 = (bf16[192,1024]{1,0:T(8,128)(2,1)S(1)}, bf16[192,1024]{1,0:T(8,128)(2,1)S(1)}, u32[]{:S(2)}, u32[]{:S(2)}) collective-permute-start(bf16[192,1024]{1,0:T(8,128)(2,1)S(1)} %collective-permute-done.2.refs_3_), channel_id=1, source_target_pairs={{0,32},{16,496},{32,64},{48,16},{64,96},{80,48},{96,128},{112,80},... | collective-permute-start | bytes 1179656 | tf_op jit(solution)/shard_map/ppermute | solution.py:235
  19.1 39.3 %collective-permute-start = (bf16[512,1024]{1,0:T(8,128)(2,1)S(1)}, bf16[512,1024]{1,0:T(8,128)(2,1)}, u32[]{:S(2)}, u32[]{:S(2)}) collective-permute-start(bf16[512,1024]{1,0:T(8,128)(2,1)S(1)} %copy-done.1), channel_id=1, source_target_pairs={{0,8},{8,0},{1,9},{9,1},{2,10},{10,2},{3,11},{11,3},{4,12},{12,4},... | collective-permute-start | bytes 3145736 | tf_op jit(solution)/shard_map/ppermute | solution.py:226
  26.3 22.3 %collective-permute-start.1 = (bf16[128,1024]{1,0:T(8,128)(2,1)}, bf16[128,1024]{1,0:T(8,128)(2,1)}, u32[]{:S(2)}, u32[]{:S(2)}) collective-permute-start(bf16[128,1024]{1,0:T(8,128)(2,1)} %slice.9), channel_id=1, source_target_pairs={{0,16},{16,0},{1,17},{17,1},{2,18},{18,2},{3,19},{19,3},{4,20},{20... | collective-permute-start | bytes 786440 | tf_op jit(solution)/shard_map/ppermute | solution.py:226
  36.9 13.4 %collective-permute-start.4 = (bf16[128,1024]{1,0:T(8,128)(2,1)}, bf16[128,1024]{1,0:T(8,128)(2,1)}, u32[]{:S(2)}, u32[]{:S(2)}) collective-permute-start(bf16[128,1024]{1,0:T(8,128)(2,1)} %slice.9), channel_id=1, source_target_pairs={{16,32},{0,496},{48,64},{32,16},{80,96},{64,48},{112,128},{96,80},... | collective-permute-start | bytes 786440 | tf_op jit(solution)/shard_map/ppermute | solution.py:244
  39.3 16.2 %collective-permute-start.7 = (bf16[192,1024]{1,0:T(8,128)(2,1)S(1)}, bf16[192,1024]{1,0:T(8,128)(2,1)S(1)}, u32[]{:S(2)}, u32[]{:S(2)}) collective-permute-start(bf16[192,1024]{1,0:T(8,128)(2,1)S(1)} %collective-permute-done.3.refs_4_), channel_id=1, source_target_pairs={{0,32},{16,496},{32,64},{48,16},{64,96},{80,48},{96,128},{112,80},... | collective-permute-start | bytes 1179656 | tf_op jit(solution)/shard_map/ppermute | solution.py:235
  41.9 16.3 %copy-start.2 = (s32[8,3]{0,1:T(4,128)S(1)}, s32[8,3]{0,1:T(4,128)}, u32[]{:S(2)}) copy-start(s32[8,3]{0,1:T(4,128)} %param.4) | copy-start | bytes 292
  52.5 7.8 %collective-permute-start.6 = (bf16[320,1024]{1,0:T(8,128)(2,1)}, bf16[320,1024]{1,0:T(8,128)(2,1)}, u32[]{:S(2)}, u32[]{:S(2)}) collective-permute-start(bf16[320,1024]{1,0:T(8,128)(2,1)} %maximum_select_fusion), channel_id=1, source_target_pairs={{0,8},{8,0},{1,9},{9,1},{2,10},{10,2},{3,11},{11,3},{4,12},{12,4},... | collective-permute-start | bytes 1966088 | tf_op jit(solution)/shard_map/ppermute | solution.py:226
  56.3 3.9 %collective-permute-start.8 = (bf16[192,1024]{1,0:T(8,128)(2,1)}, bf16[192,1024]{1,0:T(8,128)(2,1)}, u32[]{:S(2)}, u32[]{:S(2)}) collective-permute-start(bf16[192,1024]{1,0:T(8,128)(2,1)} %broadcast_select_fusion), channel_id=1, source_target_pairs={{0,8},{8,0},{1,9},{9,1},{2,10},{10,2},{3,11},{11,3},{4,12},{12,4},... | collective-permute-start | bytes 1179656 | tf_op jit(solution)/shard_map/ppermute | solution.py:226
  65.7 21.4 %all-to-all-start = ((bf16[8,592,128]{2,1,0:T(8,128)(2,1)}), bf16[8,592,128]{2,1,0:T(8,128)(2,1)S(1)}, u32[]{:S(2)}, u32[]{:S(2)}) async-start(bf16[8,592,128]{2,1,0:T(8,128)(2,1)} %gram_kernel.1), calls=%async_computation | async-start | bytes 2424832 | tf_op jit(solution)/shard_map/all_to_all | solution.py:270

commit v9 on v8

--- a/solution.py
+++ b/solution.py
@@ -260,6 +260,7 @@
     partner = swap(observed, "core")
     across = [swap(a, "xh") for a in pieces]
     beyond = [straight(pieces[0])] + [along_z(a) for a in across[1:]]
+    partner, across[0] = lax.optimization_barrier((partner, across[0]))
     here, there = jnp.concatenate(across[:2]), jnp.concatenate(beyond[:2])
     beside = [
         swap(jnp.where(core == xh, here, there), "core"),

time: 147 us -> 145 us (0.986)
  starting transfers between devices: 45.6 us -> 41.8 us
  waiting for transfers between devices: 30.8 us -> 33.2 us
    ppermute x2, starting transfers between devices: 9.56 us -> 4.56 us  [along_z(): return lax.ppermute(block, ('z', 'xh'), route)]
    ppermute x6, waiting for transfers between devices: 11.9 us -> 14.1 us  [swap(): return lax.ppermute(block, axis, [(0, 1), (1, 0)])]
where the time goes in v9:
time: 145 us
  blocking collectives  57.2 us (39%)
  starting transfers between devices  41.8 us (29%)
  waiting for transfers between devices  33.2 us (23%)
  Pallas kernels  7.33 us (5%)
  other arithmetic  2.95 us (2%)
  local copies, waits for them, and re-layouts  1.99 us (1%)
    all_to_all x2, blocking collectives, everywhere(): return lax.all_to_all(rows, ('z', 'core'), 0, 0, tiled=True)  37.4 us
    ppermute x6, starting transfers between devices, swap(): return lax.ppermute(block, axis, [(0, 1), (1, 0)])  30.6 us
    all_to_all x2, blocking collectives, everywhere(): rows = lax.all_to_all(rows, ('xh', 'y', 'xl'), 0, 0, tiled=True)  19.8 us
    all_to_all x1, waiting for transfers between devices, body(): parts = lax.all_to_all(grams, SAMP_AXES, 0, 0, tiled=True)  17.2 us
    ppermute x6, waiting for transfers between devices, swap(): return lax.ppermute(block, axis, [(0, 1), (1, 0)])  14.1 us
    pallas_call x1, Pallas kernels, on_strips(): pl.pallas_call(kernel, out_shape=jax.ShapeDtypeStruct(shape, BF16), in_sp...  5.43 us
    ppermute x2, starting transfers between devices, along_z(): return lax.ppermute(block, ('z', 'xh'), route)  4.56 us
    all_to_all x1, starting transfers between devices, body(): parts = lax.all_to_all(grams, SAMP_AXES, 0, 0, tiled=True)  4.22 us
  transfers between devices with their start and end apart: 10, of which 5 were waited for; matrix products, arithmetic and copies ran while one was open for 3% of the time, Pallas kernels for 0%

profile of v9, /device:TPU:1, one launch (start us, length us, event | category | flops | bytes accessed | tf_op | source)
XLA Modules:
  0.0 144.6 jit_solution(4002099283346914706)
XLA Ops:
  0.0 0.0 copy-start
  0.0 0.0 copy-start.1
  0.0 8.9 %collective-permute-start = (bf16[512,1024]{1,0:T(8,128)(2,1)}, bf16[512,1024]{1,0:T(8,128)(2,1)}, u32[]{:S(2)}, u32[]{:S(2)}) collective-permute-start(bf16[512,1024]{1,0:T(8,128)(2,1)} %refs_0_.1), channel_id=1, source_target_pairs={{0,8},{8,0},{1,9},{9,1},{2,10},{10,2},{3,11},{11,3},{4,12},{12,4},... | collective-permute-start | bytes 3145736 | tf_op jit(solution)/shard_map/ppermute | solution.py:226
  8.9 1.2 fusion.6
  10.1 1.9 %collective-permute-start.2 = (bf16[192,1024]{1,0:T(8,128)(2,1)S(1)}, bf16[192,1024]{1,0:T(8,128)(2,1)S(1)}, u32[]{:S(2)}, u32[]{:S(2)}) collective-permute-start(bf16[192,1024]{1,0:T(8,128)(2,1)S(1)} %get-tuple-element.24), channel_id=1, source_target_pairs={{0,16},{16,0},{1,17},{17,1},{2,18},{18,2},{3,19},{19,3},{4,20},{20... | collective-permute-start | bytes 1179656 | tf_op jit(solution)/shard_map/ppermute | solution.py:226
  12.0 4.9 %collective-permute-start.3 = (bf16[192,1024]{1,0:T(8,128)(2,1)S(1)}, bf16[192,1024]{1,0:T(8,128)(2,1)S(1)}, u32[]{:S(2)}, u32[]{:S(2)}) collective-permute-start(bf16[192,1024]{1,0:T(8,128)(2,1)S(1)} %get-tuple-element.23), channel_id=1, source_target_pairs={{0,16},{16,0},{1,17},{17,1},{2,18},{18,2},{3,19},{19,3},{4,20},{20... | collective-permute-start | bytes 1179656 | tf_op jit(solution)/shard_map/ppermute | solution.py:226
  16.9 7.3 %collective-permute-done.2.refs_3_ = bf16[192,1024]{1,0:T(8,128)(2,1)S(1)} collective-permute-done((bf16[192,1024]{1,0:T(8,128)(2,1)S(1)}, bf16[192,1024]{1,0:T(8,128)(2,1)S(1)}, u32[]{:S(2)}, u32[]{:S(2)}) %collective-permute-start.2) | collective-permute-done | bytes 393248 | tf_op jit(solution)/shard_map/ppermute | solution.py:226
  24.2 1.9 %collective-permute-start.5 = (bf16[192,1024]{1,0:T(8,128)(2,1)S(1)}, bf16[192,1024]{1,0:T(8,128)(2,1)S(1)}, u32[]{:S(2)}, u32[]{:S(2)}) collective-permute-start(bf16[192,1024]{1,0:T(8,128)(2,1)S(1)} %collective-permute-done.2.refs_3_), channel_id=1, source_target_pairs={{0,32},{16,496},{32,64},{48,16},{64,96},{80,48},{96,128},{112,80},... | collective-permute-start | bytes 1179656 | tf_op jit(solution)/shard_map/ppermute | solution.py:235
  26.1 0.0 copy-done.1
  26.2 0.7 slice.9
  26.9 8.5 %collective-permute-start.1 = (bf16[128,1024]{1,0:T(8,128)(2,1)}, bf16[128,1024]{1,0:T(8,128)(2,1)}, u32[]{:S(2)}, u32[]{:S(2)}) collective-permute-start(bf16[128,1024]{1,0:T(8,128)(2,1)} %slice.9), channel_id=1, source_target_pairs={{0,16},{16,0},{1,17},{17,1},{2,18},{18,2},{3,19},{19,3},{4,20},{20... | collective-permute-start | bytes 786440 | tf_op jit(solution)/shard_map/ppermute | solution.py:226
  35.3 2.4 %collective-permute-start.4 = (bf16[128,1024]{1,0:T(8,128)(2,1)}, bf16[128,1024]{1,0:T(8,128)(2,1)}, u32[]{:S(2)}, u32[]{:S(2)}) collective-permute-start(bf16[128,1024]{1,0:T(8,128)(2,1)} %slice.9), channel_id=1, source_target_pairs={{16,32},{0,496},{48,64},{32,16},{80,96},{64,48},{112,128},{96,80},... | collective-permute-start | bytes 786440 | tf_op jit(solution)/shard_map/ppermute | solution.py:244
  37.7 0.0 collective-permute-done.3.refs_4_
  37.7 2.6 %collective-permute-start.7 = (bf16[192,1024]{1,0:T(8,128)(2,1)S(1)}, bf16[192,1024]{1,0:T(8,128)(2,1)S(1)}, u32[]{:S(2)}, u32[]{:S(2)}) collective-permute-start(bf16[192,1024]{1,0:T(8,128)(2,1)S(1)} %collective-permute-done.3.refs_4_), channel_id=1, source_target_pairs={{0,32},{16,496},{32,64},{48,16},{64,96},{80,48},{96,128},{112,80},... | collective-permute-start | bytes 1179656 | tf_op jit(solution)/shard_map/ppermute | solution.py:235
  40.4 0.0 copy-start.2
  40.4 4.8 %collective-permute-done.1.refs_2_ = bf16[128,1024]{1,0:T(8,128)(2,1)} collective-permute-done((bf16[128,1024]{1,0:T(8,128)(2,1)}, bf16[128,1024]{1,0:T(8,128)(2,1)}, u32[]{:S(2)}, u32[]{:S(2)}) %collective-permute-start.1) | collective-permute-done | bytes 262176 | tf_op jit(solution)/shard_map/ppermute | solution.py:226
  45.2 0.0 collective-permute-done.refs_1_
  45.2 2.0 %collective-permute-done.4.refs_7_ = bf16[128,1024]{1,0:T(8,128)(2,1)} collective-permute-done((bf16[128,1024]{1,0:T(8,128)(2,1)}, bf16[128,1024]{1,0:T(8,128)(2,1)}, u32[]{:S(2)}, u32[]{:S(2)}) %collective-permute-start.4) | collective-permute-done | bytes 262176 | tf_op jit(solution)/shard_map/ppermute | solution.py:244
  47.2 0.0 collective-permute-done.5.refs_8_
  47.2 2.1 %maximum_select_fusion = bf16[320,1024]{1,0:T(8,128)(2,1)} fusion(bf16[192,1024]{1,0:T(8,128)(2,1)S(1)} %collective-permute-done.2.refs_3_, bf16[128,1024]{1,0:T(8,128)(2,1)} %collective-permute-done.1.refs_2_, bf16[192,1024]{1,0:T(8,128)(2,1)S(1)} %collective-permute-done.5.refs_8_, bf16[128,1024]{1,0:T(8,128)(2,1)} %collective-permute-done.4.refs_7_, pred[]{:T(512)S(6)} %eq.47), kind=kLoop, calls=%fused_computation | loop fusion | flops 2949120 | bytes 1966081 | tf_op jit(solution)/shard_map/jit(_where)/select_n | solution.py:266
  49.3 4.6 %collective-permute-start.6 = (bf16[320,1024]{1,0:T(8,128)(2,1)}, bf16[320,1024]{1,0:T(8,128)(2,1)}, u32[]{:S(2)}, u32[]{:S(2)}) collective-permute-start(bf16[320,1024]{1,0:T(8,128)(2,1)} %maximum_select_fusion), channel_id=1, source_target_pairs={{0,8},{8,0},{1,9},{9,1},{2,10},{10,2},{3,11},{11,3},{4,12},{12,4},... | collective-permute-start | bytes 1966088 | tf_op jit(solution)/shard_map/ppermute | solution.py:226
  53.9 0.0 collective-permute-done.7.refs_9_
  53.9 0.8 broadcast_select_fusion
  54.7 1.9 %collective-permute-start.8 = (bf16[192,1024]{1,0:T(8,128)(2,1)}, bf16[192,1024]{1,0:T(8,128)(2,1)}, u32[]{:S(2)}, u32[]{:S(2)}) collective-permute-start(bf16[192,1024]{1,0:T(8,128)(2,1)} %broadcast_select_fusion), channel_id=1, source_target_pairs={{0,8},{8,0},{1,9},{9,1},{2,10},{10,2},{3,11},{11,3},{4,12},{12,4},... | collective-permute-start | bytes 1179656 | tf_op jit(solution)/shard_map/ppermute | solution.py:226
  56.7 0.0 copy-done.2
  56.7 0.1 copy.8
  56.8 1.9 %collective-permute-done.8.refs_6_ = bf16[192,1024]{1,0:T(8,128)(2,1)} collective-permute-done((bf16[192,1024]{1,0:T(8,128)(2,1)}, bf16[192,1024]{1,0:T(8,128)(2,1)}, u32[]{:S(2)}, u32[]{:S(2)}) %collective-permute-start.8) | collective-permute-done | bytes 393248 | tf_op jit(solution)/shard_map/ppermute | solution.py:226
  58.7 0.0 collective-permute-done.6.refs_5_
  58.7 5.4 %gram_kernel.1 = bf16[8,592,128]{2,1,0:T(8,128)(2,1)} custom-call(s32[8,3]{1,0:T(8,128)S(1)} %get-tuple-element.26.source, s32[8,3]{1,0:T(8,128)S(1)} %get-tuple-element.25.column, bf16[512,1024]{1,0:T(8,128)(2,1)S(1)} %copy-done.1, bf16[512,1024]{1,0:T(8,128)(2,1)} %collective-permute-done.refs_1_, bf16[128,1024]{1,0:T(8,128)(2,1)} %collective-permute-done.1.refs_2_, ...), custom_call_target="tpu_custom_call" | custom-call | flops 805306368 | bytes 6291456 | tf_op jit(solution)/shard_map/gram_kernel/pallas_call | solution.py:107
  64.1 4.2 %all-to-all-start = ((bf16[8,592,128]{2,1,0:T(8,128)(2,1)}), bf16[8,592,128]{2,1,0:T(8,128)(2,1)S(1)}, u32[]{:S(2)}, u32[]{:S(2)}) async-start(bf16[8,592,128]{2,1,0:T(8,128)(2,1)} %gram_kernel.1), calls=%async_computation | async-start | bytes 2424832 | tf_op jit(solution)/shard_map/all_to_all | solution.py:271
  68.3 0.0 copy-done
  68.4 17.2 %all-to-all-done.parts = bf16[8,592,128]{2,1,0:T(8,128)(2,1)S(1)} async-done(((bf16[8,592,128]{2,1,0:T(8,128)(2,1)}), bf16[8,592,128]{2,1,0:T(8,128)(2,1)S(1)}, u32[]{:S(2)}, u32[]{:S(2)}) %all-to-all-start) | async-done | bytes 1212448 | tf_op jit(solution)/shard_map/all_to_all | solution.py:271
  85.5 0.6 first_kernel.1
  86.1 10.6 %all_to_all.49 = f32[16,1,128]{2,1,0:T(1,128)S(1)} all-to-all(f32[16,1,128]{2,1,0:T(1,128)S(1)} %bitcast.26), channel_id=1, replica_groups=mesh['z'=16,'xh'=2,'core'=2,'y'=4,'xl'=2] {'xh','y','xl'}, dimensions={0} | all-to-all | bytes 16384 | tf_op jit(solution)/shard_map/all_to_all | solution.py:220
  96.7 20.6 %all_to_all.50 = f32[32,1,128]{2,1,0:T(1,128)S(1)} all-to-all(f32[32,1,128]{2,1,0:T(1,128)S(1)} %bitcast.21), channel_id=1, replica_groups=mesh['z'=16,'xh'=2,'core'=2,'y'=4,'xl'=2] {'z','core'}, dimensions={0} | all-to-all | bytes 32768 | tf_op jit(solution)/shard_map/all_to_all | solution.py:222
  117.3 0.5 second_kernel.1
  117.8 9.1 %all_to_all.51 = f32[16,1,128]{2,1,0:T(1,128)S(1)} all-to-all(f32[16,1,128]{2,1,0:T(1,128)S(1)} %bitcast.25), channel_id=1, replica_groups=mesh['z'=16,'xh'=2,'core'=2,'y'=4,'xl'=2] {'xh','y','xl'}, dimensions={0} | all-to-all | bytes 16384 | tf_op jit(solution)/shard_map/all_to_all | solution.py:220
  126.9 16.8 %all_to_all.52 = f32[32,1,128]{2,1,0:T(1,128)S(1)} all-to-all(f32[32,1,128]{2,1,0:T(1,128)S(1)} %bitcast.22), channel_id=1, replica_groups=mesh['z'=16,'xh'=2,'core'=2,'y'=4,'xl'=2] {'z','core'}, dimensions={0} | all-to-all | bytes 32768 | tf_op jit(solution)/shard_map/all_to_all | solution.py:222
  143.7 0.9 last_kernel.1
  (4 shorter events, 0.1 us)
Async XLA Ops:
  0.0 68.3 %copy-start = (bf16[8,3,128,128]{3,2,1,0:T(8,128)(2,1)S(1)}, bf16[8,3,128,128]{3,2,1,0:T(8,128)(2,1)}, u32[]{:S(2)}) copy-start(bf16[8,3,128,128]{3,2,1,0:T(8,128)(2,1)} %param.5) | copy-start | bytes 2359300
  0.0 26.1 %copy-start.1 = (bf16[512,1024]{1,0:T(8,128)(2,1)S(1)}, bf16[512,1024]{1,0:T(8,128)(2,1)}, u32[]{:S(2)}) copy-start(bf16[512,1024]{1,0:T(8,128)(2,1)} %refs_0_.1) | copy-start | bytes 3145732
  0.0 45.2 %collective-permute-start = (bf16[512,1024]{1,0:T(8,128)(2,1)}, bf16[512,1024]{1,0:T(8,128)(2,1)}, u32[]{:S(2)}, u32[]{:S(2)}) collective-permute-start(bf16[512,1024]{1,0:T(8,128)(2,1)} %refs_0_.1), channel_id=1, source_target_pairs={{0,8},{8,0},{1,9},{9,1},{2,10},{10,2},{3,11},{11,3},{4,12},{12,4},... | collective-permute-start | bytes 3145736 | tf_op jit(solution)/shard_map/ppermute | solution.py:226
  10.1 14.1 %collective-permute-start.2 = (bf16[192,1024]{1,0:T(8,128)(2,1)S(1)}, bf16[192,1024]{1,0:T(8,128)(2,1)S(1)}, u32[]{:S(2)}, u32[]{:S(2)}) collective-permute-start(bf16[192,1024]{1,0:T(8,128)(2,1)S(1)} %get-tuple-element.24), channel_id=1, source_target_pairs={{0,16},{16,0},{1,17},{17,1},{2,18},{18,2},{3,19},{19,3},{4,20},{20... | collective-permute-start | bytes 1179656 | tf_op jit(solution)/shard_map/ppermute | solution.py:226
  12.0 25.7 %collective-permute-start.3 = (bf16[192,1024]{1,0:T(8,128)(2,1)S(1)}, bf16[192,1024]{1,0:T(8,128)(2,1)S(1)}, u32[]{:S(2)}, u32[]{:S(2)}) collective-permute-start(bf16[192,1024]{1,0:T(8,128)(2,1)S(1)} %get-tuple-element.23), channel_id=1, source_target_pairs={{0,16},{16,0},{1,17},{17,1},{2,18},{18,2},{3,19},{19,3},{4,20},{20... | collective-permute-start | bytes 1179656 | tf_op jit(solution)/shard_map/ppermute | solution.py:226
  24.2 23.0 %collective-permute-start.5 = (bf16[192,1024]{1,0:T(8,128)(2,1)S(1)}, bf16[192,1024]{1,0:T(8,128)(2,1)S(1)}, u32[]{:S(2)}, u32[]{:S(2)}) collective-permute-start(bf16[192,1024]{1,0:T(8,128)(2,1)S(1)} %collective-permute-done.2.refs_3_), channel_id=1, source_target_pairs={{0,32},{16,496},{32,64},{48,16},{64,96},{80,48},{96,128},{112,80},... | collective-permute-start | bytes 1179656 | tf_op jit(solution)/shard_map/ppermute | solution.py:235
  26.9 18.4 %collective-permute-start.1 = (bf16[128,1024]{1,0:T(8,128)(2,1)}, bf16[128,1024]{1,0:T(8,128)(2,1)}, u32[]{:S(2)}, u32[]{:S(2)}) collective-permute-start(bf16[128,1024]{1,0:T(8,128)(2,1)} %slice.9), channel_id=1, source_target_pairs={{0,16},{16,0},{1,17},{17,1},{2,18},{18,2},{3,19},{19,3},{4,20},{20... | collective-permute-start | bytes 786440 | tf_op jit(solution)/shard_map/ppermute | solution.py:226
  35.3 11.9 %collective-permute-start.4 = (bf16[128,1024]{1,0:T(8,128)(2,1)}, bf16[128,1024]{1,0:T(8,128)(2,1)}, u32[]{:S(2)}, u32[]{:S(2)}) collective-permute-start(bf16[128,1024]{1,0:T(8,128)(2,1)} %slice.9), channel_id=1, source_target_pairs={{16,32},{0,496},{48,64},{32,16},{80,96},{64,48},{112,128},{96,80},... | collective-permute-start | bytes 786440 | tf_op jit(solution)/shard_map/ppermute | solution.py:244
  37.7 16.2 %collective-permute-start.7 = (bf16[192,1024]{1,0:T(8,128)(2,1)S(1)}, bf16[192,1024]{1,0:T(8,128)(2,1)S(1)}, u32[]{:S(2)}, u32[]{:S(2)}) collective-permute-start(bf16[192,1024]{1,0:T(8,128)(2,1)S(1)} %collective-permute-done.3.refs_4_), channel_id=1, source_target_pairs={{0,32},{16,496},{32,64},{48,16},{64,96},{80,48},{96,128},{112,80},... | collective-permute-start | bytes 1179656 | tf_op jit(solution)/shard_map/ppermute | solution.py:235
  40.4 16.3 %copy-start.2 = (s32[8,3]{0,1:T(4,128)S(1)}, s32[8,3]{0,1:T(4,128)}, u32[]{:S(2)}) copy-start(s32[8,3]{0,1:T(4,128)} %param.4) | copy-start | bytes 292
  49.3 9.3 %collective-permute-start.6 = (bf16[320,1024]{1,0:T(8,128)(2,1)}, bf16[320,1024]{1,0:T(8,128)(2,1)}, u32[]{:S(2)}, u32[]{:S(2)}) collective-permute-start(bf16[320,1024]{1,0:T(8,128)(2,1)} %maximum_select_fusion), channel_id=1, source_target_pairs={{0,8},{8,0},{1,9},{9,1},{2,10},{10,2},{3,11},{11,3},{4,12},{12,4},... | collective-permute-start | bytes 1966088 | tf_op jit(solution)/shard_map/ppermute | solution.py:226
  54.7 3.9 %collective-permute-start.8 = (bf16[192,1024]{1,0:T(8,128)(2,1)}, bf16[192,1024]{1,0:T(8,128)(2,1)}, u32[]{:S(2)}, u32[]{:S(2)}) collective-permute-start(bf16[192,1024]{1,0:T(8,128)(2,1)} %broadcast_select_fusion), channel_id=1, source_target_pairs={{0,8},{8,0},{1,9},{9,1},{2,10},{10,2},{3,11},{11,3},{4,12},{12,4},... | collective-permute-start | bytes 1179656 | tf_op jit(solution)/shard_map/ppermute | solution.py:226
  64.1 21.4 %all-to-all-start = ((bf16[8,592,128]{2,1,0:T(8,128)(2,1)}), bf16[8,592,128]{2,1,0:T(8,128)(2,1)S(1)}, u32[]{:S(2)}, u32[]{:S(2)}) async-start(bf16[8,592,128]{2,1,0:T(8,128)(2,1)} %gram_kernel.1), calls=%async_computation | async-start | bytes 2424832 | tf_op jit(solution)/shard_map/all_to_all | solution.py:271

commit v10 on v9

--- a/solution.py
+++ b/solution.py
@@ -13,7 +13,7 @@
 SIZES = (16, 2, 2, 4, 2)
 VAR_AXES = ("z", "xh", "core")
 SAMP_AXES = ("y", "xl")
-SIZES_OF_CHUNKS = (128, 192, 192)
+SIZES_OF_CHUNKS = (128, 208, 176)
 CHUNKS = len(SIZES_OF_CHUNKS)
 ROWB = 8
 K = 3
@@ -55,7 +55,7 @@
 
         return carry
 
-    lax.fori_loop(0, ROWB * (K - 1), one, 0)
+    lax.fori_loop(0, ROWB * (K - 1), one, 0, unroll=True)
 
 
 def dot(left, right, left_dim, right_dim):

time: 145 us -> 146 us (level)
  transfers between devices with their start and end apart: 10 -> 10, of which waited for: 5 -> 5; matrix products, arithmetic and copies ran while one was open for 3% -> 4% of each run, Pallas kernels for 0% -> 0%
where the time goes in v10:
time: 146 us; the launch traced here: 145 us
  blocking collectives  57.2 us (39%)
  starting transfers between devices  41.8 us (29%)
  waiting for transfers between devices  32.8 us (22%)
  Pallas kernels  7.12 us (5%)
  other arithmetic  2.95 us (2%)
  local copies, waits for them, and re-layouts  2.89 us (2%)
    all_to_all x2, blocking collectives, everywhere(): return lax.all_to_all(rows, ('z', 'core'), 0, 0, tiled=True)  37.4 us
    ppermute x6, starting transfers between devices, swap(): return lax.ppermute(block, axis, [(0, 1), (1, 0)])  30.6 us
    all_to_all x2, blocking collectives, everywhere(): rows = lax.all_to_all(rows, ('xh', 'y', 'xl'), 0, 0, tiled=True)  19.8 us
    all_to_all x1, waiting for transfers between devices, body(): parts = lax.all_to_all(grams, SAMP_AXES, 0, 0, tiled=True)  17.2 us
    ppermute x6, waiting for transfers between devices, swap(): return lax.ppermute(block, axis, [(0, 1), (1, 0)])  13.7 us
    pallas_call x1, Pallas kernels, on_strips(): pl.pallas_call(kernel, out_shape=jax.ShapeDtypeStruct(shape, BF16), in_sp...  5.22 us
    ppermute x2, starting transfers between devices, along_z(): return lax.ppermute(block, ('z', 'xh'), route)  4.56 us
    all_to_all x1, starting transfers between devices, body(): parts = lax.all_to_all(grams, SAMP_AXES, 0, 0, tiled=True)  4.22 us
  transfers between devices with their start and end apart: 10, of which 5 were waited for; matrix products, arithmetic and copies ran while one was open for 4% of the time, Pallas kernels for 0%

profile of v10, /device:TPU:1, one launch (start us, length us, event | category | flops | bytes accessed | tf_op | source)
XLA Modules:
  0.0 144.9 jit_solution(18304033169806229106)
XLA Ops:
  0.0 0.0 copy-start
  0.0 0.0 copy-start.1
  0.0 8.9 %collective-permute-start = (bf16[512,1024]{1,0:T(8,128)(2,1)}, bf16[512,1024]{1,0:T(8,128)(2,1)}, u32[]{:S(2)}, u32[]{:S(2)}) collective-permute-start(bf16[512,1024]{1,0:T(8,128)(2,1)} %refs_0_.1), channel_id=1, source_target_pairs={{0,8},{8,0},{1,9},{9,1},{2,10},{10,2},{3,11},{11,3},{4,12},{12,4},... | collective-permute-start | bytes 3145736 | tf_op jit(solution)/shard_map/ppermute | solution.py:226
  8.9 1.0 slice.10
  10.0 1.9 %collective-permute-start.2 = (bf16[208,1024]{1,0:T(8,128)(2,1)S(1)}, bf16[208,1024]{1,0:T(8,128)(2,1)S(1)}, u32[]{:S(2)}, u32[]{:S(2)}) collective-permute-start(bf16[208,1024]{1,0:T(8,128)(2,1)S(1)} %slice.10), channel_id=1, source_target_pairs={{0,16},{16,0},{1,17},{17,1},{2,18},{18,2},{3,19},{19,3},{4,20},{20... | collective-permute-start | bytes 1277960 | tf_op jit(solution)/shard_map/ppermute | solution.py:226
  11.9 1.0 slice.11
  12.9 4.9 %collective-permute-start.3 = (bf16[176,1024]{1,0:T(8,128)(2,1)S(1)}, bf16[176,1024]{1,0:T(8,128)(2,1)S(1)}, u32[]{:S(2)}, u32[]{:S(2)}) collective-permute-start(bf16[176,1024]{1,0:T(8,128)(2,1)S(1)} %slice.11), channel_id=1, source_target_pairs={{0,16},{16,0},{1,17},{17,1},{2,18},{18,2},{3,19},{19,3},{4,20},{20... | collective-permute-start | bytes 1081352 | tf_op jit(solution)/shard_map/ppermute | solution.py:226
  17.8 7.0 %collective-permute-done.2.refs_3_ = bf16[208,1024]{1,0:T(8,128)(2,1)S(1)} collective-permute-done((bf16[208,1024]{1,0:T(8,128)(2,1)S(1)}, bf16[208,1024]{1,0:T(8,128)(2,1)S(1)}, u32[]{:S(2)}, u32[]{:S(2)}) %collective-permute-start.2) | collective-permute-done | bytes 426016 | tf_op jit(solution)/shard_map/ppermute | solution.py:226
  24.8 1.9 %collective-permute-start.5 = (bf16[208,1024]{1,0:T(8,128)(2,1)S(1)}, bf16[208,1024]{1,0:T(8,128)(2,1)S(1)}, u32[]{:S(2)}, u32[]{:S(2)}) collective-permute-start(bf16[208,1024]{1,0:T(8,128)(2,1)S(1)} %collective-permute-done.2.refs_3_), channel_id=1, source_target_pairs={{0,32},{16,496},{32,64},{48,16},{64,96},{80,48},{96,128},{112,80},... | collective-permute-start | bytes 1277960 | tf_op jit(solution)/shard_map/ppermute | solution.py:235
  26.7 0.0 copy-done.1
  26.7 0.7 slice.9
  27.5 8.5 %collective-permute-start.1 = (bf16[128,1024]{1,0:T(8,128)(2,1)}, bf16[128,1024]{1,0:T(8,128)(2,1)}, u32[]{:S(2)}, u32[]{:S(2)}) collective-permute-start(bf16[128,1024]{1,0:T(8,128)(2,1)} %slice.9), channel_id=1, source_target_pairs={{0,16},{16,0},{1,17},{17,1},{2,18},{18,2},{3,19},{19,3},{4,20},{20... | collective-permute-start | bytes 786440 | tf_op jit(solution)/shard_map/ppermute | solution.py:226
  35.9 2.4 %collective-permute-start.4 = (bf16[128,1024]{1,0:T(8,128)(2,1)}, bf16[128,1024]{1,0:T(8,128)(2,1)}, u32[]{:S(2)}, u32[]{:S(2)}) collective-permute-start(bf16[128,1024]{1,0:T(8,128)(2,1)} %slice.9), channel_id=1, source_target_pairs={{16,32},{0,496},{48,64},{32,16},{80,96},{64,48},{112,128},{96,80},... | collective-permute-start | bytes 786440 | tf_op jit(solution)/shard_map/ppermute | solution.py:244
  38.3 0.0 collective-permute-done.3.refs_4_
  38.3 2.6 %collective-permute-start.7 = (bf16[176,1024]{1,0:T(8,128)(2,1)S(1)}, bf16[176,1024]{1,0:T(8,128)(2,1)S(1)}, u32[]{:S(2)}, u32[]{:S(2)}) collective-permute-start(bf16[176,1024]{1,0:T(8,128)(2,1)S(1)} %collective-permute-done.3.refs_4_), channel_id=1, source_target_pairs={{0,32},{16,496},{32,64},{48,16},{64,96},{80,48},{96,128},{112,80},... | collective-permute-start | bytes 1081352 | tf_op jit(solution)/shard_map/ppermute | solution.py:235
  41.0 0.0 copy-start.2
  41.0 4.8 %collective-permute-done.1.refs_2_ = bf16[128,1024]{1,0:T(8,128)(2,1)} collective-permute-done((bf16[128,1024]{1,0:T(8,128)(2,1)}, bf16[128,1024]{1,0:T(8,128)(2,1)}, u32[]{:S(2)}, u32[]{:S(2)}) %collective-permute-start.1) | collective-permute-done | bytes 262176 | tf_op jit(solution)/shard_map/ppermute | solution.py:226
  45.8 0.0 collective-permute-done.refs_1_
  45.8 2.0 %collective-permute-done.4.refs_7_ = bf16[128,1024]{1,0:T(8,128)(2,1)} collective-permute-done((bf16[128,1024]{1,0:T(8,128)(2,1)}, bf16[128,1024]{1,0:T(8,128)(2,1)}, u32[]{:S(2)}, u32[]{:S(2)}) %collective-permute-start.4) | collective-permute-done | bytes 262176 | tf_op jit(solution)/shard_map/ppermute | solution.py:244
  47.8 0.0 collective-permute-done.5.refs_8_
  47.8 2.1 %maximum_select_fusion = bf16[336,1024]{1,0:T(8,128)(2,1)} fusion(bf16[208,1024]{1,0:T(8,128)(2,1)S(1)} %collective-permute-done.2.refs_3_, bf16[128,1024]{1,0:T(8,128)(2,1)} %collective-permute-done.1.refs_2_, bf16[208,1024]{1,0:T(8,128)(2,1)S(1)} %collective-permute-done.5.refs_8_, bf16[128,1024]{1,0:T(8,128)(2,1)} %collective-permute-done.4.refs_7_, pred[]{:T(512)S(6)} %eq.47), kind=kLoop, calls=%fused_computation | loop fusion | flops 3096576 | bytes 2064385 | tf_op jit(solution)/shard_map/jit(_where)/select_n | solution.py:266
  49.9 4.6 %collective-permute-start.6 = (bf16[336,1024]{1,0:T(8,128)(2,1)}, bf16[336,1024]{1,0:T(8,128)(2,1)}, u32[]{:S(2)}, u32[]{:S(2)}) collective-permute-start(bf16[336,1024]{1,0:T(8,128)(2,1)} %maximum_select_fusion), channel_id=1, source_target_pairs={{0,8},{8,0},{1,9},{9,1},{2,10},{10,2},{3,11},{11,3},{4,12},{12,4},... | collective-permute-start | bytes 2064392 | tf_op jit(solution)/shard_map/ppermute | solution.py:226
  54.5 0.0 collective-permute-done.7.refs_9_
  54.5 0.8 broadcast_select_fusion
  55.3 1.9 %collective-permute-start.8 = (bf16[176,1024]{1,0:T(8,128)(2,1)}, bf16[176,1024]{1,0:T(8,128)(2,1)}, u32[]{:S(2)}, u32[]{:S(2)}) collective-permute-start(bf16[176,1024]{1,0:T(8,128)(2,1)} %broadcast_select_fusion), channel_id=1, source_target_pairs={{0,8},{8,0},{1,9},{9,1},{2,10},{10,2},{3,11},{11,3},{4,12},{12,4},... | collective-permute-start | bytes 1081352 | tf_op jit(solution)/shard_map/ppermute | solution.py:226
  57.3 0.0 copy-done.2
  57.3 0.1 copy.8
  57.4 1.8 %collective-permute-done.8.refs_6_ = bf16[176,1024]{1,0:T(8,128)(2,1)} collective-permute-done((bf16[176,1024]{1,0:T(8,128)(2,1)}, bf16[176,1024]{1,0:T(8,128)(2,1)}, u32[]{:S(2)}, u32[]{:S(2)}) %collective-permute-start.8) | collective-permute-done | bytes 360480 | tf_op jit(solution)/shard_map/ppermute | solution.py:226
  59.2 0.0 collective-permute-done.6.refs_5_
  59.2 5.2 %gram_kernel.1 = bf16[8,592,128]{2,1,0:T(8,128)(2,1)} custom-call(s32[8,3]{1,0:T(8,128)S(1)} %get-tuple-element.24.source, s32[8,3]{1,0:T(8,128)S(1)} %get-tuple-element.23.column, bf16[512,1024]{1,0:T(8,128)(2,1)S(1)} %copy-done.1, bf16[512,1024]{1,0:T(8,128)(2,1)} %collective-permute-done.refs_1_, bf16[128,1024]{1,0:T(8,128)(2,1)} %collective-permute-done.1.refs_2_, ...), custom_call_target="tpu_custom_call" | custom-call | flops 805306368 | bytes 6291456 | tf_op jit(solution)/shard_map/gram_kernel/pallas_call | solution.py:107
  64.4 4.2 %all-to-all-start = ((bf16[8,592,128]{2,1,0:T(8,128)(2,1)}), bf16[8,592,128]{2,1,0:T(8,128)(2,1)S(1)}, u32[]{:S(2)}, u32[]{:S(2)}) async-start(bf16[8,592,128]{2,1,0:T(8,128)(2,1)} %gram_kernel.1), calls=%async_computation | async-start | bytes 2424832 | tf_op jit(solution)/shard_map/all_to_all | solution.py:271
  68.7 0.0 copy-done
  68.7 17.2 %all-to-all-done.parts = bf16[8,592,128]{2,1,0:T(8,128)(2,1)S(1)} async-done(((bf16[8,592,128]{2,1,0:T(8,128)(2,1)}), bf16[8,592,128]{2,1,0:T(8,128)(2,1)S(1)}, u32[]{:S(2)}, u32[]{:S(2)}) %all-to-all-start) | async-done | bytes 1212448 | tf_op jit(solution)/shard_map/all_to_all | solution.py:271
  85.8 0.6 first_kernel.1
  86.4 10.7 %all_to_all.49 = f32[16,1,128]{2,1,0:T(1,128)S(1)} all-to-all(f32[16,1,128]{2,1,0:T(1,128)S(1)} %bitcast.26), channel_id=1, replica_groups=mesh['z'=16,'xh'=2,'core'=2,'y'=4,'xl'=2] {'xh','y','xl'}, dimensions={0} | all-to-all | bytes 16384 | tf_op jit(solution)/shard_map/all_to_all | solution.py:220
  97.1 20.6 %all_to_all.50 = f32[32,1,128]{2,1,0:T(1,128)S(1)} all-to-all(f32[32,1,128]{2,1,0:T(1,128)S(1)} %bitcast.21), channel_id=1, replica_groups=mesh['z'=16,'xh'=2,'core'=2,'y'=4,'xl'=2] {'z','core'}, dimensions={0} | all-to-all | bytes 32768 | tf_op jit(solution)/shard_map/all_to_all | solution.py:222
  117.7 0.5 second_kernel.1
  118.1 9.1 %all_to_all.51 = f32[16,1,128]{2,1,0:T(1,128)S(1)} all-to-all(f32[16,1,128]{2,1,0:T(1,128)S(1)} %bitcast.25), channel_id=1, replica_groups=mesh['z'=16,'xh'=2,'core'=2,'y'=4,'xl'=2] {'xh','y','xl'}, dimensions={0} | all-to-all | bytes 16384 | tf_op jit(solution)/shard_map/all_to_all | solution.py:220
  127.2 16.8 %all_to_all.52 = f32[32,1,128]{2,1,0:T(1,128)S(1)} all-to-all(f32[32,1,128]{2,1,0:T(1,128)S(1)} %bitcast.22), channel_id=1, replica_groups=mesh['z'=16,'xh'=2,'core'=2,'y'=4,'xl'=2] {'z','core'}, dimensions={0} | all-to-all | bytes 32768 | tf_op jit(solution)/shard_map/all_to_all | solution.py:222
  144.1 0.9 last_kernel.1
  (4 shorter events, 0.1 us)
Async XLA Ops:
  0.0 68.7 %copy-start = (bf16[8,3,128,128]{3,2,1,0:T(8,128)(2,1)S(1)}, bf16[8,3,128,128]{3,2,1,0:T(8,128)(2,1)}, u32[]{:S(2)}) copy-start(bf16[8,3,128,128]{3,2,1,0:T(8,128)(2,1)} %param.5) | copy-start | bytes 2359300
  0.0 26.7 %copy-start.1 = (bf16[512,1024]{1,0:T(8,128)(2,1)S(1)}, bf16[512,1024]{1,0:T(8,128)(2,1)}, u32[]{:S(2)}) copy-start(bf16[512,1024]{1,0:T(8,128)(2,1)} %refs_0_.1) | copy-start | bytes 3145732
  0.0 45.8 %collective-permute-start = (bf16[512,1024]{1,0:T(8,128)(2,1)}, bf16[512,1024]{1,0:T(8,128)(2,1)}, u32[]{:S(2)}, u32[]{:S(2)}) collective-permute-start(bf16[512,1024]{1,0:T(8,128)(2,1)} %refs_0_.1), channel_id=1, source_target_pairs={{0,8},{8,0},{1,9},{9,1},{2,10},{10,2},{3,11},{11,3},{4,12},{12,4},... | collective-permute-start | bytes 3145736 | tf_op jit(solution)/shard_map/ppermute | solution.py:226
  10.0 14.8 %collective-permute-start.2 = (bf16[208,1024]{1,0:T(8,128)(2,1)S(1)}, bf16[208,1024]{1,0:T(8,128)(2,1)S(1)}, u32[]{:S(2)}, u32[]{:S(2)}) collective-permute-start(bf16[208,1024]{1,0:T(8,128)(2,1)S(1)} %slice.10), channel_id=1, source_target_pairs={{0,16},{16,0},{1,17},{17,1},{2,18},{18,2},{3,19},{19,3},{4,20},{20... | collective-permute-start | bytes 1277960 | tf_op jit(solution)/shard_map/ppermute | solution.py:226
  12.9 25.4 %collective-permute-start.3 = (bf16[176,1024]{1,0:T(8,128)(2,1)S(1)}, bf16[176,1024]{1,0:T(8,128)(2,1)S(1)}, u32[]{:S(2)}, u32[]{:S(2)}) collective-permute-start(bf16[176,1024]{1,0:T(8,128)(2,1)S(1)} %slice.11), channel_id=1, source_target_pairs={{0,16},{16,0},{1,17},{17,1},{2,18},{18,2},{3,19},{19,3},{4,20},{20... | collective-permute-start | bytes 1081352 | tf_op jit(solution)/shard_map/ppermute | solution.py:226
  24.8 23.0 %collective-permute-start.5 = (bf16[208,1024]{1,0:T(8,128)(2,1)S(1)}, bf16[208,1024]{1,0:T(8,128)(2,1)S(1)}, u32[]{:S(2)}, u32[]{:S(2)}) collective-permute-start(bf16[208,1024]{1,0:T(8,128)(2,1)S(1)} %collective-permute-done.2.refs_3_), channel_id=1, source_target_pairs={{0,32},{16,496},{32,64},{48,16},{64,96},{80,48},{96,128},{112,80},... | collective-permute-start | bytes 1277960 | tf_op jit(solution)/shard_map/ppermute | solution.py:235
  27.5 18.4 %collective-permute-start.1 = (bf16[128,1024]{1,0:T(8,128)(2,1)}, bf16[128,1024]{1,0:T(8,128)(2,1)}, u32[]{:S(2)}, u32[]{:S(2)}) collective-permute-start(bf16[128,1024]{1,0:T(8,128)(2,1)} %slice.9), channel_id=1, source_target_pairs={{0,16},{16,0},{1,17},{17,1},{2,18},{18,2},{3,19},{19,3},{4,20},{20... | collective-permute-start | bytes 786440 | tf_op jit(solution)/shard_map/ppermute | solution.py:226
  35.9 11.9 %collective-permute-start.4 = (bf16[128,1024]{1,0:T(8,128)(2,1)}, bf16[128,1024]{1,0:T(8,128)(2,1)}, u32[]{:S(2)}, u32[]{:S(2)}) collective-permute-start(bf16[128,1024]{1,0:T(8,128)(2,1)} %slice.9), channel_id=1, source_target_pairs={{16,32},{0,496},{48,64},{32,16},{80,96},{64,48},{112,128},{96,80},... | collective-permute-start | bytes 786440 | tf_op jit(solution)/shard_map/ppermute | solution.py:244
  38.3 16.2 %collective-permute-start.7 = (bf16[176,1024]{1,0:T(8,128)(2,1)S(1)}, bf16[176,1024]{1,0:T(8,128)(2,1)S(1)}, u32[]{:S(2)}, u32[]{:S(2)}) collective-permute-start(bf16[176,1024]{1,0:T(8,128)(2,1)S(1)} %collective-permute-done.3.refs_4_), channel_id=1, source_target_pairs={{0,32},{16,496},{32,64},{48,16},{64,96},{80,48},{96,128},{112,80},... | collective-permute-start | bytes 1081352 | tf_op jit(solution)/shard_map/ppermute | solution.py:235
  41.0 16.3 %copy-start.2 = (s32[8,3]{0,1:T(4,128)S(1)}, s32[8,3]{0,1:T(4,128)}, u32[]{:S(2)}) copy-start(s32[8,3]{0,1:T(4,128)} %param.4) | copy-start | bytes 292
  49.9 9.3 %collective-permute-start.6 = (bf16[336,1024]{1,0:T(8,128)(2,1)}, bf16[336,1024]{1,0:T(8,128)(2,1)}, u32[]{:S(2)}, u32[]{:S(2)}) collective-permute-start(bf16[336,1024]{1,0:T(8,128)(2,1)} %maximum_select_fusion), channel_id=1, source_target_pairs={{0,8},{8,0},{1,9},{9,1},{2,10},{10,2},{3,11},{11,3},{4,12},{12,4},... | collective-permute-start | bytes 2064392 | tf_op jit(solution)/shard_map/ppermute | solution.py:226
  55.3 3.9 %collective-permute-start.8 = (bf16[176,1024]{1,0:T(8,128)(2,1)}, bf16[176,1024]{1,0:T(8,128)(2,1)}, u32[]{:S(2)}, u32[]{:S(2)}) collective-permute-start(bf16[176,1024]{1,0:T(8,128)(2,1)} %broadcast_select_fusion), channel_id=1, source_target_pairs={{0,8},{8,0},{1,9},{9,1},{2,10},{10,2},{3,11},{11,3},{4,12},{12,4},... | collective-permute-start | bytes 1081352 | tf_op jit(solution)/shard_map/ppermute | solution.py:226
  64.4 21.4 %all-to-all-start = ((bf16[8,592,128]{2,1,0:T(8,128)(2,1)}), bf16[8,592,128]{2,1,0:T(8,128)(2,1)S(1)}, u32[]{:S(2)}, u32[]{:S(2)}) async-start(bf16[8,592,128]{2,1,0:T(8,128)(2,1)} %gram_kernel.1), calls=%async_computation | async-start | bytes 2424832 | tf_op jit(solution)/shard_map/all_to_all | solution.py:271

commit v11 on v10

--- a/solution.py
+++ b/solution.py
@@ -13,7 +13,7 @@
 SIZES = (16, 2, 2, 4, 2)
 VAR_AXES = ("z", "xh", "core")
 SAMP_AXES = ("y", "xl")
-SIZES_OF_CHUNKS = (128, 208, 176)
+SIZES_OF_CHUNKS = (128, 192, 192)
 CHUNKS = len(SIZES_OF_CHUNKS)
 ROWB = 8
 K = 3

time: 146 us -> 145 us (level)
  transfers between devices with their start and end apart: 10 -> 10, of which waited for: 5 -> 5; matrix products, arithmetic and copies ran while one was open for 4% -> 3% of each run, Pallas kernels for 0% -> 0%
where the time goes in v11:
time: 145 us; the launch traced here: 144 us
  blocking collectives  57.2 us (39%)
  starting transfers between devices  41.8 us (29%)
  waiting for transfers between devices  33.2 us (23%)
  Pallas kernels  7.11 us (5%)
  other arithmetic  2.95 us (2%)
  local copies, waits for them, and re-layouts  1.99 us (1%)
    all_to_all x2, blocking collectives, everywhere(): return lax.all_to_all(rows, ('z', 'core'), 0, 0, tiled=True)  37.4 us
    ppermute x6, starting transfers between devices, swap(): return lax.ppermute(block, axis, [(0, 1), (1, 0)])  30.6 us
    all_to_all x2, blocking collectives, everywhere(): rows = lax.all_to_all(rows, ('xh', 'y', 'xl'), 0, 0, tiled=True)  19.7 us
    all_to_all x1, waiting for transfers between devices, body(): parts = lax.all_to_all(grams, SAMP_AXES, 0, 0, tiled=True)  17.2 us
    ppermute x6, waiting for transfers between devices, swap(): return lax.ppermute(block, axis, [(0, 1), (1, 0)])  14.1 us
    pallas_call x1, Pallas kernels, on_strips(): pl.pallas_call(kernel, out_shape=jax.ShapeDtypeStruct(shape, BF16), in_sp...  5.21 us
    ppermute x2, starting transfers between devices, along_z(): return lax.ppermute(block, ('z', 'xh'), route)  4.56 us
    all_to_all x1, starting transfers between devices, body(): parts = lax.all_to_all(grams, SAMP_AXES, 0, 0, tiled=True)  4.22 us
  transfers between devices with their start and end apart: 10, of which 5 were waited for; matrix products, arithmetic and copies ran while one was open for 3% of the time, Pallas kernels for 0%

profile of v11, /device:TPU:1, one launch (start us, length us, event | category | flops | bytes accessed | tf_op | source)
XLA Modules:
  0.0 144.4 jit_solution(13435262930393490303)
XLA Ops:
  0.0 0.0 copy-start
  0.0 0.0 copy-start.1
  0.0 8.9 %collective-permute-start = (bf16[512,1024]{1,0:T(8,128)(2,1)}, bf16[512,1024]{1,0:T(8,128)(2,1)}, u32[]{:S(2)}, u32[]{:S(2)}) collective-permute-start(bf16[512,1024]{1,0:T(8,128)(2,1)} %refs_0_.1), channel_id=1, source_target_pairs={{0,8},{8,0},{1,9},{9,1},{2,10},{10,2},{3,11},{11,3},{4,12},{12,4},... | collective-permute-start | bytes 3145736 | tf_op jit(solution)/shard_map/ppermute | solution.py:226
  8.9 1.2 fusion.6
  10.1 1.9 %collective-permute-start.2 = (bf16[192,1024]{1,0:T(8,128)(2,1)S(1)}, bf16[192,1024]{1,0:T(8,128)(2,1)S(1)}, u32[]{:S(2)}, u32[]{:S(2)}) collective-permute-start(bf16[192,1024]{1,0:T(8,128)(2,1)S(1)} %get-tuple-element.24), channel_id=1, source_target_pairs={{0,16},{16,0},{1,17},{17,1},{2,18},{18,2},{3,19},{19,3},{4,20},{20... | collective-permute-start | bytes 1179656 | tf_op jit(solution)/shard_map/ppermute | solution.py:226
  12.0 4.9 %collective-permute-start.3 = (bf16[192,1024]{1,0:T(8,128)(2,1)S(1)}, bf16[192,1024]{1,0:T(8,128)(2,1)S(1)}, u32[]{:S(2)}, u32[]{:S(2)}) collective-permute-start(bf16[192,1024]{1,0:T(8,128)(2,1)S(1)} %get-tuple-element.23), channel_id=1, source_target_pairs={{0,16},{16,0},{1,17},{17,1},{2,18},{18,2},{3,19},{19,3},{4,20},{20... | collective-permute-start | bytes 1179656 | tf_op jit(solution)/shard_map/ppermute | solution.py:226
  16.9 7.3 %collective-permute-done.2.refs_3_ = bf16[192,1024]{1,0:T(8,128)(2,1)S(1)} collective-permute-done((bf16[192,1024]{1,0:T(8,128)(2,1)S(1)}, bf16[192,1024]{1,0:T(8,128)(2,1)S(1)}, u32[]{:S(2)}, u32[]{:S(2)}) %collective-permute-start.2) | collective-permute-done | bytes 393248 | tf_op jit(solution)/shard_map/ppermute | solution.py:226
  24.2 1.9 %collective-permute-start.5 = (bf16[192,1024]{1,0:T(8,128)(2,1)S(1)}, bf16[192,1024]{1,0:T(8,128)(2,1)S(1)}, u32[]{:S(2)}, u32[]{:S(2)}) collective-permute-start(bf16[192,1024]{1,0:T(8,128)(2,1)S(1)} %collective-permute-done.2.refs_3_), channel_id=1, source_target_pairs={{0,32},{16,496},{32,64},{48,16},{64,96},{80,48},{96,128},{112,80},... | collective-permute-start | bytes 1179656 | tf_op jit(solution)/shard_map/ppermute | solution.py:235
  26.1 0.0 copy-done.1
  26.2 0.7 slice.9
  26.9 8.5 %collective-permute-start.1 = (bf16[128,1024]{1,0:T(8,128)(2,1)}, bf16[128,1024]{1,0:T(8,128)(2,1)}, u32[]{:S(2)}, u32[]{:S(2)}) collective-permute-start(bf16[128,1024]{1,0:T(8,128)(2,1)} %slice.9), channel_id=1, source_target_pairs={{0,16},{16,0},{1,17},{17,1},{2,18},{18,2},{3,19},{19,3},{4,20},{20... | collective-permute-start | bytes 786440 | tf_op jit(solution)/shard_map/ppermute | solution.py:226
  35.3 2.4 %collective-permute-start.4 = (bf16[128,1024]{1,0:T(8,128)(2,1)}, bf16[128,1024]{1,0:T(8,128)(2,1)}, u32[]{:S(2)}, u32[]{:S(2)}) collective-permute-start(bf16[128,1024]{1,0:T(8,128)(2,1)} %slice.9), channel_id=1, source_target_pairs={{16,32},{0,496},{48,64},{32,16},{80,96},{64,48},{112,128},{96,80},... | collective-permute-start | bytes 786440 | tf_op jit(solution)/shard_map/ppermute | solution.py:244
  37.7 0.0 collective-permute-done.3.refs_4_
  37.7 2.6 %collective-permute-start.7 = (bf16[192,1024]{1,0:T(8,128)(2,1)S(1)}, bf16[192,1024]{1,0:T(8,128)(2,1)S(1)}, u32[]{:S(2)}, u32[]{:S(2)}) collective-permute-start(bf16[192,1024]{1,0:T(8,128)(2,1)S(1)} %collective-permute-done.3.refs_4_), channel_id=1, source_target_pairs={{0,32},{16,496},{32,64},{48,16},{64,96},{80,48},{96,128},{112,80},... | collective-permute-start | bytes 1179656 | tf_op jit(solution)/shard_map/ppermute | solution.py:235
  40.4 0.0 copy-start.2
  40.4 4.8 %collective-permute-done.1.refs_2_ = bf16[128,1024]{1,0:T(8,128)(2,1)} collective-permute-done((bf16[128,1024]{1,0:T(8,128)(2,1)}, bf16[128,1024]{1,0:T(8,128)(2,1)}, u32[]{:S(2)}, u32[]{:S(2)}) %collective-permute-start.1) | collective-permute-done | bytes 262176 | tf_op jit(solution)/shard_map/ppermute | solution.py:226
  45.2 0.0 collective-permute-done.refs_1_
  45.2 2.0 %collective-permute-done.4.refs_7_ = bf16[128,1024]{1,0:T(8,128)(2,1)} collective-permute-done((bf16[128,1024]{1,0:T(8,128)(2,1)}, bf16[128,1024]{1,0:T(8,128)(2,1)}, u32[]{:S(2)}, u32[]{:S(2)}) %collective-permute-start.4) | collective-permute-done | bytes 262176 | tf_op jit(solution)/shard_map/ppermute | solution.py:244
  47.2 0.0 collective-permute-done.5.refs_8_
  47.2 2.1 %maximum_select_fusion = bf16[320,1024]{1,0:T(8,128)(2,1)} fusion(bf16[192,1024]{1,0:T(8,128)(2,1)S(1)} %collective-permute-done.2.refs_3_, bf16[128,1024]{1,0:T(8,128)(2,1)} %collective-permute-done.1.refs_2_, bf16[192,1024]{1,0:T(8,128)(2,1)S(1)} %collective-permute-done.5.refs_8_, bf16[128,1024]{1,0:T(8,128)(2,1)} %collective-permute-done.4.refs_7_, pred[]{:T(512)S(6)} %eq.47), kind=kLoop, calls=%fused_computation | loop fusion | flops 2949120 | bytes 1966081 | tf_op jit(solution)/shard_map/jit(_where)/select_n | solution.py:266
  49.3 4.6 %collective-permute-start.6 = (bf16[320,1024]{1,0:T(8,128)(2,1)}, bf16[320,1024]{1,0:T(8,128)(2,1)}, u32[]{:S(2)}, u32[]{:S(2)}) collective-permute-start(bf16[320,1024]{1,0:T(8,128)(2,1)} %maximum_select_fusion), channel_id=1, source_target_pairs={{0,8},{8,0},{1,9},{9,1},{2,10},{10,2},{3,11},{11,3},{4,12},{12,4},... | collective-permute-start | bytes 1966088 | tf_op jit(solution)/shard_map/ppermute | solution.py:226
  53.9 0.0 collective-permute-done.7.refs_9_
  53.9 0.8 broadcast_select_fusion
  54.7 1.9 %collective-permute-start.8 = (bf16[192,1024]{1,0:T(8,128)(2,1)}, bf16[192,1024]{1,0:T(8,128)(2,1)}, u32[]{:S(2)}, u32[]{:S(2)}) collective-permute-start(bf16[192,1024]{1,0:T(8,128)(2,1)} %broadcast_select_fusion), channel_id=1, source_target_pairs={{0,8},{8,0},{1,9},{9,1},{2,10},{10,2},{3,11},{11,3},{4,12},{12,4},... | collective-permute-start | bytes 1179656 | tf_op jit(solution)/shard_map/ppermute | solution.py:226
  56.7 0.0 copy-done.2
  56.7 0.1 copy.8
  56.8 1.9 %collective-permute-done.8.refs_6_ = bf16[192,1024]{1,0:T(8,128)(2,1)} collective-permute-done((bf16[192,1024]{1,0:T(8,128)(2,1)}, bf16[192,1024]{1,0:T(8,128)(2,1)}, u32[]{:S(2)}, u32[]{:S(2)}) %collective-permute-start.8) | collective-permute-done | bytes 393248 | tf_op jit(solution)/shard_map/ppermute | solution.py:226
  58.7 0.0 collective-permute-done.6.refs_5_
  58.7 5.2 %gram_kernel.1 = bf16[8,592,128]{2,1,0:T(8,128)(2,1)} custom-call(s32[8,3]{1,0:T(8,128)S(1)} %get-tuple-element.26.source, s32[8,3]{1,0:T(8,128)S(1)} %get-tuple-element.25.column, bf16[512,1024]{1,0:T(8,128)(2,1)S(1)} %copy-done.1, bf16[512,1024]{1,0:T(8,128)(2,1)} %collective-permute-done.refs_1_, bf16[128,1024]{1,0:T(8,128)(2,1)} %collective-permute-done.1.refs_2_, ...), custom_call_target="tpu_custom_call" | custom-call | flops 805306368 | bytes 6291456 | tf_op jit(solution)/shard_map/gram_kernel/pallas_call | solution.py:107
  63.9 4.2 %all-to-all-start = ((bf16[8,592,128]{2,1,0:T(8,128)(2,1)}), bf16[8,592,128]{2,1,0:T(8,128)(2,1)S(1)}, u32[]{:S(2)}, u32[]{:S(2)}) async-start(bf16[8,592,128]{2,1,0:T(8,128)(2,1)} %gram_kernel.1), calls=%async_computation | async-start | bytes 2424832 | tf_op jit(solution)/shard_map/all_to_all | solution.py:271
  68.1 0.0 copy-done
  68.1 17.2 %all-to-all-done.parts = bf16[8,592,128]{2,1,0:T(8,128)(2,1)S(1)} async-done(((bf16[8,592,128]{2,1,0:T(8,128)(2,1)}), bf16[8,592,128]{2,1,0:T(8,128)(2,1)S(1)}, u32[]{:S(2)}, u32[]{:S(2)}) %all-to-all-start) | async-done | bytes 1212448 | tf_op jit(solution)/shard_map/all_to_all | solution.py:271
  85.3 0.6 first_kernel.1
  85.9 10.6 %all_to_all.49 = f32[16,1,128]{2,1,0:T(1,128)S(1)} all-to-all(f32[16,1,128]{2,1,0:T(1,128)S(1)} %bitcast.26), channel_id=1, replica_groups=mesh['z'=16,'xh'=2,'core'=2,'y'=4,'xl'=2] {'xh','y','xl'}, dimensions={0} | all-to-all | bytes 16384 | tf_op jit(solution)/shard_map/all_to_all | solution.py:220
  96.5 20.6 %all_to_all.50 = f32[32,1,128]{2,1,0:T(1,128)S(1)} all-to-all(f32[32,1,128]{2,1,0:T(1,128)S(1)} %bitcast.21), channel_id=1, replica_groups=mesh['z'=16,'xh'=2,'core'=2,'y'=4,'xl'=2] {'z','core'}, dimensions={0} | all-to-all | bytes 32768 | tf_op jit(solution)/shard_map/all_to_all | solution.py:222
  117.1 0.5 second_kernel.1
  117.6 9.1 %all_to_all.51 = f32[16,1,128]{2,1,0:T(1,128)S(1)} all-to-all(f32[16,1,128]{2,1,0:T(1,128)S(1)} %bitcast.25), channel_id=1, replica_groups=mesh['z'=16,'xh'=2,'core'=2,'y'=4,'xl'=2] {'xh','y','xl'}, dimensions={0} | all-to-all | bytes 16384 | tf_op jit(solution)/shard_map/all_to_all | solution.py:220
  126.7 16.8 %all_to_all.52 = f32[32,1,128]{2,1,0:T(1,128)S(1)} all-to-all(f32[32,1,128]{2,1,0:T(1,128)S(1)} %bitcast.22), channel_id=1, replica_groups=mesh['z'=16,'xh'=2,'core'=2,'y'=4,'xl'=2] {'z','core'}, dimensions={0} | all-to-all | bytes 32768 | tf_op jit(solution)/shard_map/all_to_all | solution.py:222
  143.5 0.9 last_kernel.1
  (4 shorter events, 0.1 us)
Async XLA Ops:
  0.0 68.1 %copy-start = (bf16[8,3,128,128]{3,2,1,0:T(8,128)(2,1)S(1)}, bf16[8,3,128,128]{3,2,1,0:T(8,128)(2,1)}, u32[]{:S(2)}) copy-start(bf16[8,3,128,128]{3,2,1,0:T(8,128)(2,1)} %param.5) | copy-start | bytes 2359300
  0.0 26.1 %copy-start.1 = (bf16[512,1024]{1,0:T(8,128)(2,1)S(1)}, bf16[512,1024]{1,0:T(8,128)(2,1)}, u32[]{:S(2)}) copy-start(bf16[512,1024]{1,0:T(8,128)(2,1)} %refs_0_.1) | copy-start | bytes 3145732
  0.0 45.2 %collective-permute-start = (bf16[512,1024]{1,0:T(8,128)(2,1)}, bf16[512,1024]{1,0:T(8,128)(2,1)}, u32[]{:S(2)}, u32[]{:S(2)}) collective-permute-start(bf16[512,1024]{1,0:T(8,128)(2,1)} %refs_0_.1), channel_id=1, source_target_pairs={{0,8},{8,0},{1,9},{9,1},{2,10},{10,2},{3,11},{11,3},{4,12},{12,4},... | collective-permute-start | bytes 3145736 | tf_op jit(solution)/shard_map/ppermute | solution.py:226
  10.1 14.1 %collective-permute-start.2 = (bf16[192,1024]{1,0:T(8,128)(2,1)S(1)}, bf16[192,1024]{1,0:T(8,128)(2,1)S(1)}, u32[]{:S(2)}, u32[]{:S(2)}) collective-permute-start(bf16[192,1024]{1,0:T(8,128)(2,1)S(1)} %get-tuple-element.24), channel_id=1, source_target_pairs={{0,16},{16,0},{1,17},{17,1},{2,18},{18,2},{3,19},{19,3},{4,20},{20... | collective-permute-start | bytes 1179656 | tf_op jit(solution)/shard_map/ppermute | solution.py:226
  12.0 25.7 %collective-permute-start.3 = (bf16[192,1024]{1,0:T(8,128)(2,1)S(1)}, bf16[192,1024]{1,0:T(8,128)(2,1)S(1)}, u32[]{:S(2)}, u32[]{:S(2)}) collective-permute-start(bf16[192,1024]{1,0:T(8,128)(2,1)S(1)} %get-tuple-element.23), channel_id=1, source_target_pairs={{0,16},{16,0},{1,17},{17,1},{2,18},{18,2},{3,19},{19,3},{4,20},{20... | collective-permute-start | bytes 1179656 | tf_op jit(solution)/shard_map/ppermute | solution.py:226
  24.2 23.0 %collective-permute-start.5 = (bf16[192,1024]{1,0:T(8,128)(2,1)S(1)}, bf16[192,1024]{1,0:T(8,128)(2,1)S(1)}, u32[]{:S(2)}, u32[]{:S(2)}) collective-permute-start(bf16[192,1024]{1,0:T(8,128)(2,1)S(1)} %collective-permute-done.2.refs_3_), channel_id=1, source_target_pairs={{0,32},{16,496},{32,64},{48,16},{64,96},{80,48},{96,128},{112,80},... | collective-permute-start | bytes 1179656 | tf_op jit(solution)/shard_map/ppermute | solution.py:235
  26.9 18.4 %collective-permute-start.1 = (bf16[128,1024]{1,0:T(8,128)(2,1)}, bf16[128,1024]{1,0:T(8,128)(2,1)}, u32[]{:S(2)}, u32[]{:S(2)}) collective-permute-start(bf16[128,1024]{1,0:T(8,128)(2,1)} %slice.9), channel_id=1, source_target_pairs={{0,16},{16,0},{1,17},{17,1},{2,18},{18,2},{3,19},{19,3},{4,20},{20... | collective-permute-start | bytes 786440 | tf_op jit(solution)/shard_map/ppermute | solution.py:226
  35.3 11.9 %collective-permute-start.4 = (bf16[128,1024]{1,0:T(8,128)(2,1)}, bf16[128,1024]{1,0:T(8,128)(2,1)}, u32[]{:S(2)}, u32[]{:S(2)}) collective-permute-start(bf16[128,1024]{1,0:T(8,128)(2,1)} %slice.9), channel_id=1, source_target_pairs={{16,32},{0,496},{48,64},{32,16},{80,96},{64,48},{112,128},{96,80},... | collective-permute-start | bytes 786440 | tf_op jit(solution)/shard_map/ppermute | solution.py:244
  37.7 16.2 %collective-permute-start.7 = (bf16[192,1024]{1,0:T(8,128)(2,1)S(1)}, bf16[192,1024]{1,0:T(8,128)(2,1)S(1)}, u32[]{:S(2)}, u32[]{:S(2)}) collective-permute-start(bf16[192,1024]{1,0:T(8,128)(2,1)S(1)} %collective-permute-done.3.refs_4_), channel_id=1, source_target_pairs={{0,32},{16,496},{32,64},{48,16},{64,96},{80,48},{96,128},{112,80},... | collective-permute-start | bytes 1179656 | tf_op jit(solution)/shard_map/ppermute | solution.py:235
  40.4 16.3 %copy-start.2 = (s32[8,3]{0,1:T(4,128)S(1)}, s32[8,3]{0,1:T(4,128)}, u32[]{:S(2)}) copy-start(s32[8,3]{0,1:T(4,128)} %param.4) | copy-start | bytes 292
  49.3 9.3 %collective-permute-start.6 = (bf16[320,1024]{1,0:T(8,128)(2,1)}, bf16[320,1024]{1,0:T(8,128)(2,1)}, u32[]{:S(2)}, u32[]{:S(2)}) collective-permute-start(bf16[320,1024]{1,0:T(8,128)(2,1)} %maximum_select_fusion), channel_id=1, source_target_pairs={{0,8},{8,0},{1,9},{9,1},{2,10},{10,2},{3,11},{11,3},{4,12},{12,4},... | collective-permute-start | bytes 1966088 | tf_op jit(solution)/shard_map/ppermute | solution.py:226
  54.7 3.9 %collective-permute-start.8 = (bf16[192,1024]{1,0:T(8,128)(2,1)}, bf16[192,1024]{1,0:T(8,128)(2,1)}, u32[]{:S(2)}, u32[]{:S(2)}) collective-permute-start(bf16[192,1024]{1,0:T(8,128)(2,1)} %broadcast_select_fusion), channel_id=1, source_target_pairs={{0,8},{8,0},{1,9},{9,1},{2,10},{10,2},{3,11},{11,3},{4,12},{12,4},... | collective-permute-start | bytes 1179656 | tf_op jit(solution)/shard_map/ppermute | solution.py:226
  63.9 21.4 %all-to-all-start = ((bf16[8,592,128]{2,1,0:T(8,128)(2,1)}), bf16[8,592,128]{2,1,0:T(8,128)(2,1)S(1)}, u32[]{:S(2)}, u32[]{:S(2)}) async-start(bf16[8,592,128]{2,1,0:T(8,128)(2,1)} %gram_kernel.1), calls=%async_computation | async-start | bytes 2424832 | tf_op jit(solution)/shard_map/all_to_all | solution.py:271
